TPU v7x, 32 devices: a whole 2x2x4 slice. The times are simulated.
32 devices in a mesh: xs: 16 (over z, y, core), ys: 2 (over x).
Axes of the slice: x: 2, y: 2, z: 4, core: 2. Of those that a mesh axis runs over, the one named last changes fastest.
Arguments:
- fields: float32 [6, 16, 512, 256], P(None, None, 'xs', 'ys'), may hold values from -6 to 6
- permittivity: float32 [16, 512, 256], P(None, 'xs', 'ys'), may hold values from 1 to 12
- adj_values: float32 [128, 128], P(('xs', 'ys')), may hold values from -6 to 6
- adj_owner: int32 [128, 1], P(('xs', 'ys')), may hold values from 0 to 1; in each aligned block of 4 rows (0 to 3, 4 to 7, ...) at most 4 rows name the same one
- adj_row: int32 [128], P(('xs', 'ys')), may hold values from 0 to 31
- angle_wave: int32 [128], replicated, may hold values from 0 to 4999
Outputs:
- new_fields: float32 [6, 16, 512, 256], P(None, None, 'xs', 'ys')
- far_field: float32 [128, 2, 4, 256], P('xs', None, None, 'ys')
Inputs may be any that keep to these rules, and one draw needn't show every extreme that they name: `adj_owner`: among the 4 rows of one device no ys index is named more than 4 times.
All inputs are finite; a program needn't handle non-finite values.
Results may differ from a plain program's by a relative error of at most 0.000071.
Values sent between devices are 32-bit elements; how exact they have to be, the bound alone decides.
No kernel may reach another device: no remote copies, remote signals or barrier semaphores. Data moves between devices by JAX's collectives and lax.ppermute only.
A program may use at most 64 MiB of HBM per device.

v0:
```python
import math

import jax
import jax.numpy as jnp
from jax import lax
from jax.sharding import PartitionSpec as P

STEPS = 3
CAP = 4
GRID_X = 5000
X0 = 2000
ZS = 8


time_step = 0.5


def from_behind(block, axis, distance):
    devices = range(lax.axis_size(axis))
    route = [(i - distance, i) for i in devices if i - distance in devices]
    return lax.ppermute(block, axis, route)


def along_next(inner, edge, axis):
    return jnp.concatenate([lax.slice_in_dim(inner, 1, inner.shape[axis], axis=axis), edge], axis)


def along_prev(inner, edge, axis):
    return jnp.concatenate(
        [edge, lax.slice_in_dim(inner, 0, inner.shape[axis] - 1, axis=axis)], axis
    )


def across_x(plane, offset):
    return from_behind(plane, "xs", offset)


def across_y(plane, offset):
    return from_behind(plane, "ys", offset)


def from_next_x(plane):
    return across_x(plane, -1)


def from_next_y(plane):
    return across_y(plane, -1)


def from_prev_x(plane):
    return across_x(plane, 1)


def from_prev_y(plane):
    return across_y(plane, 1)


def advance(fields, coeffs, source, next_x, next_y, prev_x, prev_y):
    elec = [fields[0], fields[1], fields[2]]
    magn = [fields[3], fields[4], fields[5]]
    zero_layer = jnp.zeros((1,) + elec[0].shape[1:], jnp.float32)
    edge_x = next_x(jnp.stack([elec[1][:, 0, :], elec[2][:, 0, :]]))
    edge_y = next_y(jnp.stack([elec[0][:, :, 0], elec[2][:, :, 0]]))
    ey_xnext = along_next(elec[1], edge_x[0][:, None, :], 1)
    ez_xnext = along_next(elec[2], edge_x[1][:, None, :], 1)
    ex_ynext = along_next(elec[0], edge_y[0][:, :, None], 2)
    ez_ynext = along_next(elec[2], edge_y[1][:, :, None], 2)
    ex_znext = along_next(elec[0], zero_layer, 0)
    ey_znext = along_next(elec[1], zero_layer, 0)
    hx_new = magn[0] - time_step * (ez_ynext - elec[2] - (ey_znext - elec[1]))
    hy_new = magn[1] - time_step * (ex_znext - elec[0] - (ez_xnext - elec[2]))
    hz_new = magn[2] - time_step * (ey_xnext - elec[1] - (ex_ynext - elec[0]))
    back_x = prev_x(jnp.stack([hy_new[:, -1, :], hz_new[:, -1, :]]))
    back_y = prev_y(jnp.stack([hx_new[:, :, -1], hz_new[:, :, -1]]))
    hy_xprev = along_prev(hy_new, back_x[0][:, None, :], 1)
    hz_xprev = along_prev(hz_new, back_x[1][:, None, :], 1)
    hx_yprev = along_prev(hx_new, back_y[0][:, :, None], 2)
    hz_yprev = along_prev(hz_new, back_y[1][:, :, None], 2)
    hx_zprev = along_prev(hx_new, zero_layer, 0)
    hy_zprev = along_prev(hy_new, zero_layer, 0)
    ex_new = elec[0] + coeffs * (hz_new - hz_yprev - (hy_new - hy_zprev))
    ey_new = elec[1] + coeffs * (hx_new - hx_zprev - (hz_new - hz_xprev))
    ez_new = elec[2] + coeffs * (hy_new - hy_xprev - (hx_new - hx_yprev) - source)
    return jnp.stack([ex_new, ey_new, ez_new, hx_new, hy_new, hz_new])


def spectrum(tile, angles, first_x):
    positions = X0 + first_x + jnp.arange(tile.shape[1], dtype=jnp.int32)
    phase = angles[:, None] * positions[None, :] % GRID_X
    angle = phase.astype(jnp.float32) * (2.0 * math.pi / GRID_X)
    cosine = jnp.cos(angle)
    sine = -jnp.sin(angle)
    real_part = jnp.einsum("ax,cxy->acy", cosine, tile, precision=lax.Precision.HIGHEST)
    imag_part = jnp.einsum("ax,cxy->acy", sine, tile, precision=lax.Precision.HIGHEST)
    return jnp.stack([real_part, imag_part], axis=1)


def on_device(fields, permittivity, adj_values, adj_owner, adj_row, angle_wave):
    cells_x = fields.shape[2]
    cells_y = fields.shape[3]
    layers = fields.shape[1]
    groups = lax.axis_size("ys")
    total_x = cells_x * lax.axis_size("xs")
    per_block = angle_wave.shape[0] // lax.axis_size("xs")
    owners = adj_owner[:, 0]
    hits = (owners[:, None] == jnp.arange(groups, dtype=jnp.int32)[None, :]).astype(jnp.int32)
    before = jnp.cumsum(hits, axis=0) - hits
    slot_index = owners * CAP + jnp.sum(before * hits, axis=1)
    placing = (jnp.arange(groups * CAP, dtype=jnp.int32)[:, None] == slot_index[None, :]).astype(
        jnp.float32
    )
    outgoing = jnp.dot(placing, adj_values, precision=lax.Precision.HIGHEST).reshape(
        groups, CAP, cells_y
    )
    out_rows = jnp.dot(
        placing, adj_row.astype(jnp.float32), precision=lax.Precision.HIGHEST
    ).reshape(groups, CAP)
    incoming, in_rows = (
        lax.all_to_all(outgoing, "ys", split_axis=0, concat_axis=0, tiled=True),
        lax.all_to_all(out_rows, "ys", split_axis=0, concat_axis=0, tiled=True),
    )
    landing = (
        jnp.arange(cells_x, dtype=jnp.float32)[:, None] == in_rows.reshape(-1)[None, :]
    ).astype(jnp.float32)
    current = jnp.dot(
        landing, incoming.reshape(groups * CAP, cells_y), precision=lax.Precision.HIGHEST
    )
    coeffs = time_step / permittivity
    layer_mask = (jnp.arange(layers, dtype=jnp.int32) == ZS).astype(jnp.float32)[:, None, None]
    source = layer_mask * current[None]
    for iteration in range(STEPS):
        fields = advance(fields, coeffs, source, from_next_x, from_next_y, from_prev_x, from_prev_y)
    tile = jnp.stack([-fields[4][ZS], fields[3][ZS], fields[1][ZS], -fields[0][ZS]])
    my_angles = lax.dynamic_slice_in_dim(angle_wave, lax.axis_index("xs") * per_block, per_block)
    summed = spectrum(lax.all_gather(tile, "xs", axis=1, tiled=True), my_angles, jnp.int32(0))
    far_field = summed / math.sqrt(total_x)
    return (fields, far_field)


def solution(mesh):
    placed = (
        P(None, None, "xs", "ys"),
        P(None, "xs", "ys"),
        P(("xs", "ys"), None),
        P(("xs", "ys"), None),
        P(("xs", "ys")),
        P(),
    )
    return jax.shard_map(
        on_device,
        mesh=mesh,
        in_specs=placed,
        out_specs=(P(None, None, "xs", "ys"), P("xs", None, None, "ys")),
        check_vma=False,
    )
```

profile of v0, /device:TPU:0, one launch (start us, length us, event | category | flops | bytes accessed | tf_op | source)
XLA Modules:
  0.0 138.8 jit_solution(6876716979290097198)
XLA Ops:
  7.2 1.3 fusion.91
  8.7 1.3 collective-permute-start.1
  10.4 1.3 collective-permute-start
  12.7 4.2 %all-to-all-start = ((f32[2,1,4]{2,1,0:T(1,128)}), f32[2,1,4]{2,1,0:T(1,128)S(1)}, u32[]{:S(2)}, u32[]{:S(2)}) async-start(f32[2,1,4]{2,1,0:T(1,128)} %bitcast.26), calls=%async_computation | async-start | bytes 2048 | tf_op jit(solution)/shard_map/all_to_all | solution.py:120
  16.9 0.8 slice_bitcast_fusion.2
  17.7 0.7 fusion.79
  18.4 2.2 %all-to-all-done = f32[2,1,4]{2,1,0:T(1,128)S(1)} async-done(((f32[2,1,4]{2,1,0:T(1,128)}), f32[2,1,4]{2,1,0:T(1,128)S(1)}, u32[]{:S(2)}, u32[]{:S(2)}) %all-to-all-start) | async-done | bytes 64 | tf_op jit(solution)/shard_map/all_to_all | solution.py:120
  20.7 3.2 %all-to-all-start.1 = ((f32[2,4,128]{2,1,0:T(4,128)}), f32[2,4,128]{2,1,0:T(4,128)S(1)}, u32[]{:S(2)}, u32[]{:S(2)}) async-start(f32[2,4,128]{2,1,0:T(4,128)} %bitcast.27), calls=%async_computation.1 | async-start | bytes 8192 | tf_op jit(solution)/shard_map/all_to_all | solution.py:119
  24.1 0.7 slice.386
  26.4 1.3 all-to-all-done.1
  27.8 0.9 copy.245
  28.9 1.5 %fusion.12 = (f32[16,32,128]{2,0,1:T(8,128)S(1)}, f32[16,32,128]{2,0,1:T(8,128)S(1)}) fusion(f32[16,32,1]{2,0,1:T(8,128)} %copy.245, f32[16,32,127]{2,0,1:T(8,128)S(1)} %slice.394, f32[15,32,128]{2,0,1:T(8,128)S(1)} %bitcast.191, f32[16,32,128]{2,1,0:T(8,128)S(1)} %get-tuple-element.29, f32[1,16,32,128]{3,2,1,0:T(8,128)S(1)} %get-tuple-element.28, ...), kind=kLoop, calls=%fused_computation.33 | loop fusion | flops 458752 | bytes 1818624 | tf_op jit(solution)/shard_map/mul | solution.py:70
  31.4 2.6 %collective-permute-start.2 = (f32[2,16,32]{2,1,0:T(8,128)S(1)}, f32[2,16,32]{2,1,0:T(8,128)S(1)}, u32[]{:S(2)}, u32[]{:S(2)}) collective-permute-start(f32[2,16,32]{2,1,0:T(8,128)S(1)} %pad_maximum_fusion.3), channel_id=1, source_target_pairs={{0,1},{2,3},{4,5},{6,7},{8,9},{10,11},{12,13},{14,15},{16,17},{18,... | collective-permute-start | bytes 12296 | tf_op jit(solution)/shard_map/ppermute | solution.py:21
  34.7 0.7 slice.403
  35.4 1.3 collective-permute-start.3
  36.8 0.9 copy.250
  37.7 0.9 copy.256
  38.6 1.8 %fusion.1 = (f32[16,32,128]{2,1,0:T(8,128)S(1)}, f32[16,32,128]{2,1,0:T(8,128)S(1)}, f32[16,32,128]{2,1,0:T(8,128)S(1)}) fusion(f32[16,32,128]{2,1,0:T(8,128)S(1)} %get-tuple-element.23, f32[16,31,128]{2,1,0:T(8,128)S(1)} %bitcast.188, f32[16,1,128]{2,1,0:T(1,128)S(1)} %bitcast.200, f32[16,32,128]{2,1,0:T(8,128)S(1)} %get-tuple-element.24, ...), kind=kLoop, calls=%fused_computation.7 | loop fusion | flops 1441792 | bytes 4177984 | tf_op jit(solution)/shard_map/add | solution.py:83
  40.7 1.3 collective-permute-start.5
  42.3 0.7 slice.428
  43.1 0.7 slice.422
  43.8 0.7 slice.427
  44.5 1.3 collective-permute-start.4
  46.3 0.9 copy.259
  47.2 0.9 copy.260
  48.1 2.9 %collective-permute-done.4 = f32[2,16,128]{2,1,0:T(8,128)S(1)} collective-permute-done((f32[2,16,128]{2,1,0:T(8,128)S(1)}, f32[2,16,128]{2,1,0:T(8,128)S(1)}, u32[]{:S(2)}, u32[]{:S(2)}) %collective-permute-start.4) | collective-permute-done | bytes 16416 | tf_op jit(solution)/shard_map/ppermute | solution.py:21
  51.0 1.8 %fusion.34 = (f32[16,32,128]{2,1,0:T(8,128)S(1)}, f32[16,32,128]{2,1,0:T(8,128)S(1)}, f32[16,32,128]{2,1,0:T(8,128)S(1)}) fusion(f32[16,32,128]{2,1,0:T(8,128)S(1)} %get-tuple-element.23, f32[16,32,128]{2,1,0:T(8,128)S(1)} %get-tuple-element.20, f32[16,1,128]{2,1,0:T(1,128)S(1)} %bitcast.194, f32[16,31,128]{2,1,0:T(8,128)} %slice.428, ...), kind=kLoop, calls=%fused_computation.65 | loop fusion | flops 1245184 | bytes 3899392 | tf_op jit(solution)/shard_map/sub | solution.py:71
  53.4 4.3 %collective-permute-start.6 = (f32[2,16,32]{2,1,0:T(8,128)S(1)}, f32[2,16,32]{2,1,0:T(8,128)S(1)}, u32[]{:S(2)}, u32[]{:S(2)}) collective-permute-start(f32[2,16,32]{2,1,0:T(8,128)S(1)} %pad_maximum_fusion.7), channel_id=1, source_target_pairs={{0,1},{2,3},{4,5},{6,7},{8,9},{10,11},{12,13},{14,15},{16,17},{18,... | collective-permute-start | bytes 12296 | tf_op jit(solution)/shard_map/ppermute | solution.py:21
  57.7 0.7 slice.431
  58.4 4.1 %collective-permute-start.7 = (f32[2,16,128]{2,1,0:T(8,128)S(1)}, f32[2,16,128]{2,1,0:T(8,128)S(1)}, u32[]{:S(2)}, u32[]{:S(2)}) collective-permute-start(f32[2,16,128]{2,1,0:T(8,128)S(1)} %pad_maximum_fusion.8), channel_id=1, source_target_pairs={{0,2},{2,4},{4,6},{6,8},{8,10},{10,12},{12,14},{14,16},{16,18},{18... | collective-permute-start | bytes 49160 | tf_op jit(solution)/shard_map/ppermute | solution.py:21
  63.3 1.4 %fusion.37 = (f32[16,32,128]{2,1,0:T(8,128)S(1)}, f32[16,32,128]{2,1,0:T(8,128)S(1)}, f32[16,32,128]{2,1,0:T(8,128)S(1)}) fusion(f32[16,32,128]{2,1,0:T(8,128)S(1)} %get-tuple-element.21, f32[16,32,128]{2,1,0:T(8,128)S(1)} %get-tuple-element.38, f32[16,31,128]{2,1,0:T(8,128)S(1)} %bitcast.180, f32[16,1,128]{2,1,0:T(1,128)S(1)} %bitcast.198, ...), kind=kLoop, calls=%fused_computation.69 | loop fusion | flops 1441792 | bytes 4177984 | tf_op jit(solution)/shard_map/add | solution.py:82
  65.1 1.3 collective-permute-start.9
  66.7 0.7 slice.456
  67.5 0.7 slice.450
  68.2 0.7 slice.455
  68.9 1.3 collective-permute-start.8
  70.8 0.9 copy.269
  71.6 0.9 copy.270
  72.5 1.8 %fusion.44 = (f32[16,32,128]{2,1,0:T(8,128)S(1)}, f32[16,32,128]{2,1,0:T(8,128)S(1)}, f32[16,32,128]{2,1,0:T(8,128)S(1)}) fusion(f32[16,32,128]{2,1,0:T(8,128)S(1)} %get-tuple-element.39, f32[16,32,128]{2,1,0:T(8,128)S(1)} %get-tuple-element.32, f32[16,32,1]{2,1,0:T(8,128)} %copy.270, f32[16,32,127]{2,1,0:T(8,128)S(1)} %slice.448, ...), kind=kLoop, calls=%fused_computation.81 | loop fusion | flops 1245184 | bytes 3899392 | tf_op jit(solution)/shard_map/sub | solution.py:70
  74.9 4.0 %collective-permute-start.10 = (f32[2,16,32]{2,1,0:T(8,128)S(1)}, f32[2,16,32]{2,1,0:T(8,128)S(1)}, u32[]{:S(2)}, u32[]{:S(2)}) collective-permute-start(f32[2,16,32]{2,1,0:T(8,128)S(1)} %pad_maximum_fusion.11), channel_id=1, source_target_pairs={{0,1},{2,3},{4,5},{6,7},{8,9},{10,11},{12,13},{14,15},{16,17},{18,... | collective-permute-start | bytes 12296 | tf_op jit(solution)/shard_map/ppermute | solution.py:21
  78.9 5.0 %collective-permute-start.11 = (f32[2,16,128]{2,1,0:T(8,128)S(1)}, f32[2,16,128]{2,1,0:T(8,128)S(1)}, u32[]{:S(2)}, u32[]{:S(2)}) collective-permute-start(f32[2,16,128]{2,1,0:T(8,128)S(1)} %pad_maximum_fusion.12), channel_id=1, source_target_pairs={{0,2},{2,4},{4,6},{6,8},{8,10},{10,12},{12,14},{14,16},{16,18},{18... | collective-permute-start | bytes 49160 | tf_op jit(solution)/shard_map/ppermute | solution.py:21
  84.9 1.1 copy-done.6
  87.0 0.9 fusion.7
  87.9 0.7 bitcast_dynamic-update-slice_fusion.2
  88.6 0.7 bitcast_dynamic-update-slice_fusion.1
  89.3 0.7 bitcast_dynamic-update-slice_fusion
  90.1 38.6 %all-gather.2.cloned.1.call-done = f32[4,512,128]{2,1,0:T(8,128)} async-done(((f32[4,32,128]{2,1,0:T(8,128)}), f32[4,512,128]{2,1,0:T(8,128)}) %all-gather.2.cloned.1.call-update) | async-done | bytes 1048592 | tf_op jit(solution)/shard_map/all_gather | solution.py:135
  128.7 2.0 %convolution_bitcast_fusion.1 = f32[8,1,4,128]{3,0,2,1:T(8,128)S(1)} fusion(f32[4,512,128]{2,1,0:T(8,128)} %all-gather.2.cloned.1.call-done, s32[512]{0:T(512)S(1)} %iota_add_fusion, s32[8]{0:T(128)S(1)} %dynamic_slice.3), kind=kOutput, calls=%fused_computation.1 | convolution fusion | flops 25202688 | bytes 1067040 | tf_op jit(solution)/shard_map/ax,cxy->acy/dot_general | solution.py:93
  (124 shorter events, 12.8 us)
Async XLA Ops:
  7.2 10.5 %copy-start = (f32[4,128]{1,0:T(4,128)S(1)}, f32[4,128]{1,0:T(4,128)}, u32[]{:S(2)}) copy-start(f32[4,128]{1,0:T(4,128)} %param.8) | copy-start | bytes 6148
  7.2 9.7 %copy-start.1 = (f32[6,16,32,128]{3,2,1,0:T(8,128)S(1)}, f32[6,16,32,128]{3,2,1,0:T(8,128)}, u32[]{:S(2)}) copy-start(f32[6,16,32,128]{3,2,1,0:T(8,128)} %param.6) | copy-start | bytes 4718596
  7.2 4.5 %copy-start.7 = (s32[4,1]{0,1:T(1,128)S(1)}, s32[4,1]{0,1:T(1,128)}, u32[]{:S(2)}) copy-start(s32[4,1]{0,1:T(1,128)} %param.9) | copy-start | bytes 52
  7.2 4.7 %copy-start.8 = (s32[4]{0:T(128)S(1)}, s32[4]{0:T(128)}, u32[]{:S(2)}) copy-start(s32[4]{0:T(128)} %param.10) | copy-start | bytes 52
  8.7 19.1 %collective-permute-start.1 = (f32[2,16,32]{2,1,0:T(8,128)S(1)}, f32[2,16,32]{2,1,0:T(8,128)S(1)}, u32[]{:S(2)}, u32[]{:S(2)}) collective-permute-start(f32[2,16,32]{2,1,0:T(8,128)S(1)} %pad_maximum_fusion.2), channel_id=1, source_target_pairs={{1,0},{3,2},{5,4},{7,6},{9,8},{11,10},{13,12},{15,14},{17,16},{19,... | collective-permute-start | bytes 12296 | tf_op jit(solution)/shard_map/ppermute | solution.py:21
  10.4 18.5 %collective-permute-start = (f32[2,16,128]{2,1,0:T(8,128)S(1)}, f32[2,16,128]{2,1,0:T(8,128)S(1)}, u32[]{:S(2)}, u32[]{:S(2)}) collective-permute-start(f32[2,16,128]{2,1,0:T(8,128)S(1)} %pad_maximum_fusion.1), channel_id=1, source_target_pairs={{2,0},{4,2},{6,4},{8,6},{10,8},{12,10},{14,12},{16,14},{18,16},{20... | collective-permute-start | bytes 49160 | tf_op jit(solution)/shard_map/ppermute | solution.py:21
  12.7 8.0 %all-to-all-start = ((f32[2,1,4]{2,1,0:T(1,128)}), f32[2,1,4]{2,1,0:T(1,128)S(1)}, u32[]{:S(2)}, u32[]{:S(2)}) async-start(f32[2,1,4]{2,1,0:T(1,128)} %bitcast.26), calls=%async_computation | async-start | bytes 2048 | tf_op jit(solution)/shard_map/all_to_all | solution.py:120
  20.7 7.0 %all-to-all-start.1 = ((f32[2,4,128]{2,1,0:T(4,128)}), f32[2,4,128]{2,1,0:T(4,128)S(1)}, u32[]{:S(2)}, u32[]{:S(2)}) async-start(f32[2,4,128]{2,1,0:T(4,128)} %bitcast.27), calls=%async_computation.1 | async-start | bytes 8192 | tf_op jit(solution)/shard_map/all_to_all | solution.py:119
  23.9 104.8 %all-gather.2.cloned.1.call-start = ((), (), s32[]{:S(2)}) async-start(), calls=%async_computation.2 | async-start | bytes 1114112 | tf_op jit(solution)/shard_map/all_gather | solution.py:135
  23.9 1.0 copy-start.5
  28.9 1.5 %copy-start.4 = (f32[15,32,128]{2,1,0:T(8,128)S(1)}, f32[15,32,128]{2,1,0:T(8,128)}, u32[]{:S(2)}) copy-start(f32[15,32,128]{2,1,0:T(8,128)} %get-tuple-element.26) | copy-start | bytes 737284
  30.8 7.7 %copy-start.2 = (f32[16,32,128]{2,1,0:T(8,128)S(1)}, f32[16,32,128]{2,1,0:T(8,128)}, u32[]{:S(2)}) copy-start(f32[16,32,128]{2,1,0:T(8,128)} %param.7) | copy-start | bytes 786436
  31.4 5.4 %collective-permute-start.2 = (f32[2,16,32]{2,1,0:T(8,128)S(1)}, f32[2,16,32]{2,1,0:T(8,128)S(1)}, u32[]{:S(2)}, u32[]{:S(2)}) collective-permute-start(f32[2,16,32]{2,1,0:T(8,128)S(1)} %pad_maximum_fusion.3), channel_id=1, source_target_pairs={{0,1},{2,3},{4,5},{6,7},{8,9},{10,11},{12,13},{14,15},{16,17},{18,... | collective-permute-start | bytes 12296 | tf_op jit(solution)/shard_map/ppermute | solution.py:21
  35.4 3.1 %collective-permute-start.3 = (f32[2,16,128]{2,1,0:T(8,128)S(1)}, f32[2,16,128]{2,1,0:T(8,128)S(1)}, u32[]{:S(2)}, u32[]{:S(2)}) collective-permute-start(f32[2,16,128]{2,1,0:T(8,128)S(1)} %pad_maximum_fusion.4), channel_id=1, source_target_pairs={{0,2},{2,4},{4,6},{6,8},{8,10},{10,12},{12,14},{14,16},{16,18},{18... | collective-permute-start | bytes 49160 | tf_op jit(solution)/shard_map/ppermute | solution.py:21
  40.7 5.6 %collective-permute-start.5 = (f32[2,16,32]{2,1,0:T(8,128)S(1)}, f32[2,16,32]{2,1,0:T(8,128)S(1)}, u32[]{:S(2)}, u32[]{:S(2)}) collective-permute-start(f32[2,16,32]{2,1,0:T(8,128)S(1)} %pad_maximum_fusion.6), channel_id=1, source_target_pairs={{1,0},{3,2},{5,4},{7,6},{9,8},{11,10},{13,12},{15,14},{17,16},{19,... | collective-permute-start | bytes 12296 | tf_op jit(solution)/shard_map/ppermute | solution.py:21
  44.5 6.5 %collective-permute-start.4 = (f32[2,16,128]{2,1,0:T(8,128)S(1)}, f32[2,16,128]{2,1,0:T(8,128)S(1)}, u32[]{:S(2)}, u32[]{:S(2)}) collective-permute-start(f32[2,16,128]{2,1,0:T(8,128)S(1)} %pad_maximum_fusion.5), channel_id=1, source_target_pairs={{2,0},{4,2},{6,4},{8,6},{10,8},{12,10},{14,12},{16,14},{18,16},{20... | collective-permute-start | bytes 49160 | tf_op jit(solution)/shard_map/ppermute | solution.py:21
  53.4 9.1 %collective-permute-start.6 = (f32[2,16,32]{2,1,0:T(8,128)S(1)}, f32[2,16,32]{2,1,0:T(8,128)S(1)}, u32[]{:S(2)}, u32[]{:S(2)}) collective-permute-start(f32[2,16,32]{2,1,0:T(8,128)S(1)} %pad_maximum_fusion.7), channel_id=1, source_target_pairs={{0,1},{2,3},{4,5},{6,7},{8,9},{10,11},{12,13},{14,15},{16,17},{18,... | collective-permute-start | bytes 12296 | tf_op jit(solution)/shard_map/ppermute | solution.py:21
  58.4 4.9 %collective-permute-start.7 = (f32[2,16,128]{2,1,0:T(8,128)S(1)}, f32[2,16,128]{2,1,0:T(8,128)S(1)}, u32[]{:S(2)}, u32[]{:S(2)}) collective-permute-start(f32[2,16,128]{2,1,0:T(8,128)S(1)} %pad_maximum_fusion.8), channel_id=1, source_target_pairs={{0,2},{2,4},{4,6},{6,8},{8,10},{10,12},{12,14},{14,16},{16,18},{18... | collective-permute-start | bytes 49160 | tf_op jit(solution)/shard_map/ppermute | solution.py:21
  65.1 5.6 %collective-permute-start.9 = (f32[2,16,32]{2,1,0:T(8,128)S(1)}, f32[2,16,32]{2,1,0:T(8,128)S(1)}, u32[]{:S(2)}, u32[]{:S(2)}) collective-permute-start(f32[2,16,32]{2,1,0:T(8,128)S(1)} %pad_maximum_fusion.10), channel_id=1, source_target_pairs={{1,0},{3,2},{5,4},{7,6},{9,8},{11,10},{13,12},{15,14},{17,16},{19,... | collective-permute-start | bytes 12296 | tf_op jit(solution)/shard_map/ppermute | solution.py:21
  68.9 3.6 %collective-permute-start.8 = (f32[2,16,128]{2,1,0:T(8,128)S(1)}, f32[2,16,128]{2,1,0:T(8,128)S(1)}, u32[]{:S(2)}, u32[]{:S(2)}) collective-permute-start(f32[2,16,128]{2,1,0:T(8,128)S(1)} %pad_maximum_fusion.9), channel_id=1, source_target_pairs={{2,0},{4,2},{6,4},{8,6},{10,8},{12,10},{14,12},{16,14},{18,16},{20... | collective-permute-start | bytes 49160 | tf_op jit(solution)/shard_map/ppermute | solution.py:21
  74.9 9.0 %collective-permute-start.10 = (f32[2,16,32]{2,1,0:T(8,128)S(1)}, f32[2,16,32]{2,1,0:T(8,128)S(1)}, u32[]{:S(2)}, u32[]{:S(2)}) collective-permute-start(f32[2,16,32]{2,1,0:T(8,128)S(1)} %pad_maximum_fusion.11), channel_id=1, source_target_pairs={{0,1},{2,3},{4,5},{6,7},{8,9},{10,11},{12,13},{14,15},{16,17},{18,... | collective-permute-start | bytes 12296 | tf_op jit(solution)/shard_map/ppermute | solution.py:21
  78.9 5.8 %collective-permute-start.11 = (f32[2,16,128]{2,1,0:T(8,128)S(1)}, f32[2,16,128]{2,1,0:T(8,128)S(1)}, u32[]{:S(2)}, u32[]{:S(2)}) collective-permute-start(f32[2,16,128]{2,1,0:T(8,128)S(1)} %pad_maximum_fusion.12), channel_id=1, source_target_pairs={{0,2},{2,4},{4,6},{6,8},{8,10},{10,12},{12,14},{14,16},{16,18},{18... | collective-permute-start | bytes 49160 | tf_op jit(solution)/shard_map/ppermute | solution.py:21
  84.3 2.4 %copy-start.9 = (s32[128]{0:T(128)S(1)}, s32[128]{0:T(128)}, u32[]{:S(2)}) copy-start(s32[128]{0:T(128)} %param.11) | copy-start | bytes 1540
  84.9 1.1 copy-start.6
  128.7 2.0 %copy-start.3 = (f32[4,512,128]{2,1,0:T(8,128)S(1)}, f32[4,512,128]{2,1,0:T(8,128)}, u32[]{:S(2)}) copy-start(f32[4,512,128]{2,1,0:T(8,128)} %all-gather.2.cloned.1.call-done) | copy-start | bytes 3145732
Sparse Core Ops, SparseCore 0:
  86.8 41.8 all-gather.1
where the time goes:
time: 139 us
  waiting for transfers between devices  47 us (34%)
  starting transfers between devices  36.4 us (26%)
  local copies, waits for them, and re-layouts  25.4 us (18%)
  between operations  14.8 us (11%)
  other arithmetic  11.6 us (8%)
  matrix products  3.64 us (3%)
    all_gather x1, waiting for transfers between devices, on_device(): lax.all_gather(tile, 'xs', axis=1, tiled=True)  38.6 us
    ppermute x12, starting transfers between devices, from_behind(): return lax.ppermute(block, axis, route)  28.9 us
    slice x17, local copies, waits for them, and re-layouts, along_next(): lax.slice_in_dim(inner, 1, inner.shape[axis], axis=axis)  6.67 us
    ppermute x12, waiting for transfers between devices, from_behind(): return lax.ppermute(block, axis, route)  4.93 us
    all_to_all x1, starting transfers between devices, on_device(): lax.all_to_all(out_rows, 'ys', split_axis=0, concat_axis=0, tiled=True)  4.2 us
    unnamed x25, local copies, waits for them, and re-layouts  3.55 us
    all_to_all x1, starting transfers between devices, on_device(): lax.all_to_all(outgoing, 'ys', split_axis=0, concat_axis=0, tiled=True)  3.22 us
  transfers between devices with their start and end apart: 15, of which 8 were waited for; matrix products, arithmetic and copies ran while one was open for 16% of the time, Pallas kernels for 0%

commit v1 on v0

v1 whole, which is shorter than its diff:
```python
import functools
import math

import jax
import jax.numpy as jnp
from jax import lax
from jax.experimental import pallas as pl
from jax.experimental.pallas import tpu as pltpu
from jax.sharding import PartitionSpec as P

STEPS = 3
CAP = 4
GRID_X = 5000
X0 = 2000
ZS = 8

time_step = 0.5

TILE = 8
REACH = 4
SLOT = 8
PARTS = 7
PAIRS = (PARTS + 1) // 2

VMEM = pl.BlockSpec(memory_space=pltpu.VMEM)
SMEM = pl.BlockSpec(memory_space=pltpu.SMEM)
PARAMS = pltpu.CompilerParams(vmem_limit_bytes=24 * 1024 * 1024)


def lanes_of(shape):
    return lax.broadcasted_iota(jnp.int32, shape, len(shape) - 1)


def rows_of(shape):
    return lax.broadcasted_iota(jnp.int32, shape, len(shape) - 2)


def swaps(size):
    found = []
    for first in (0, 1):
        pairs = [(i, i + 1) for i in range(first, size - 1, 2)]
        if pairs:
            found.append(pairs + [(j, i) for i, j in pairs])
    return found


def halo_tile(even, odd, px, c, z, layers):
    at = pl.ds((c * (layers // 2) + z // 2) * TILE, TILE)
    from_even, from_odd = even[at, :], odd[at, :]
    same = px == z % 2
    from_even = jnp.where(same, from_even, pltpu.roll(from_even, REACH, 0))
    from_odd = jnp.where(same, pltpu.roll(from_odd, REACH, 0), from_odd)
    odd_half = (rows_of(from_even.shape) >= REACH) == (px == 0)
    return jnp.where(odd_half, from_odd, from_even)


def pack_x(f_lo, f_hi, p_lo, p_hi, *rest, n_adj):
    if n_adj:
        values, rows, owners, to_even, to_odd, blocks = rest
    else:
        to_even, to_odd = rest
    px = lax.axis_index("xs") % 2
    layers = f_lo.shape[1]
    for c in range(PARTS):
        for pair in range(layers // 2):
            if c < 6:
                lo = [f_lo[c, 2 * pair + k] for k in (0, 1)]
                hi = [f_hi[c, 2 * pair + k] for k in (0, 1)]
            else:
                lo = [time_step / p_lo[2 * pair + k] for k in (0, 1)]
                hi = [time_step / p_hi[2 * pair + k] for k in (0, 1)]
            upper = rows_of(lo[0].shape) >= REACH
            first = jnp.where(upper, pltpu.roll(lo[1], REACH, 0), lo[0])
            last = jnp.where(upper, hi[1], pltpu.roll(hi[0], REACH, 0))
            at = pl.ds((c * (layers // 2) + pair) * TILE, TILE)
            to_even[at, :] = jnp.where(px == 0, last, first)
            to_odd[at, :] = jnp.where(px == 0, first, last)
    if n_adj:
        blocks[...] = jnp.zeros(blocks.shape, jnp.float32)
        blocks[0:n_adj, :] = values[...]
        for b in range(n_adj):
            one = (1, blocks.shape[1])
            blocks[n_adj + b : n_adj + b + 1, :] = jnp.full(one, rows[b], jnp.int32).astype(
                jnp.float32
            )
            blocks[2 * n_adj + b : 2 * n_adj + b + 1, :] = jnp.full(
                one, owners[b, 0], jnp.int32
            ).astype(jnp.float32)
        end = PARTS * (layers // 2) * TILE
        to_even[end:, :] = blocks[...]
        to_odd[end:, :] = blocks[...]


def pack_y(fields, permittivity, even, *rest, n_rows, swap):
    if n_rows:
        blocks, to_y, to_diag = rest
    else:
        to_y, to_diag = rest
    px = lax.axis_index("xs") % 2
    to_next = lax.axis_index("ys") % 2 == swap
    layers, cells_x = fields.shape[1], fields.shape[2]
    tiles = cells_x // TILE
    ring = cells_x + TILE
    offset = jnp.where(to_next, 3, 0)
    width = fields.shape[3]
    quad = ((lanes_of((TILE, width)) + offset) % width) // 4
    half = layers // 2 * TILE
    for q in range(PAIRS):
        for r in range(tiles + 1):
            total = jnp.zeros((TILE, width), jnp.float32)
            for b in range(2):
                c = 2 * q + b
                if c >= PARTS:
                    continue
                for z in range(layers):
                    if r < tiles:
                        rows = slice(r * TILE, (r + 1) * TILE)
                        if c < 6:
                            block = fields[c, z, rows, :]
                        else:
                            block = time_step / permittivity[z, rows, :]
                    else:
                        at = pl.ds(c * half + z // 2 * TILE, TILE)
                        block = even[at, :]
                        block = jnp.where(px == z % 2, block, pltpu.roll(block, REACH, 0))
                    shift = SLOT * z + 4 * b
                    if shift:
                        block = pltpu.roll(block, shift, 1)
                    total = jnp.where(quad == 2 * z + b, block, total)
            to_y[q * ring + r * TILE : q * ring + (r + 1) * TILE, :] = pltpu.roll(total, offset, 1)
    upper = rows_of((TILE, width)) >= REACH
    for k in range(PAIRS // 2):
        starts = [(2 * k + j) * ring for j in (0, 1)]
        lo = [to_y[s : s + TILE, :] for s in starts]
        hi = [to_y[s + cells_x - TILE : s + cells_x, :] for s in starts]
        first = jnp.where(upper, pltpu.roll(lo[1], REACH, 0), lo[0])
        last = jnp.where(upper, hi[1], pltpu.roll(hi[0], REACH, 0))
        to_diag[k * TILE : (k + 1) * TILE, :] = jnp.where(px == 0, first, last)
    if n_rows:
        end = PAIRS * ring
        to_y[end : end + n_rows, :] = blocks[...]
        to_y[end + n_rows : end + 2 * n_rows, :] = even[PARTS * half :, :]
        to_diag[PAIRS // 2 * TILE :, :] = blocks[...]


def gather_sources(sets, px, me, source, n_adj):
    ring, width = source.shape[1:]
    row_at = rows_of((ring, width)).astype(jnp.float32)
    mine = jnp.zeros((ring, width), jnp.float32)
    other = jnp.zeros((ring, width), jnp.float32)
    own_index = jnp.where(me == 0, 0.0, 1.0)
    cells_x = ring - TILE
    for ref, start, is_next in sets:
        for b in range(n_adj):
            value = ref[start + b : start + b + 1, :]
            row = ref[start + n_adj + b : start + n_adj + b + 1, :]
            owner = ref[start + 2 * n_adj + b : start + 2 * n_adj + b + 1, :]
            if is_next is not None:
                after = jnp.where(row < REACH, row + cells_x, -1.0)
                before = jnp.where(row >= cells_x - REACH, row + TILE, -1.0)
                row = jnp.where(is_next, after, before)
            is_mine = owner == own_index
            mine = mine + jnp.where(row_at == jnp.where(is_mine, row, -1.0), value, 0.0)
            other = other + jnp.where(row_at == jnp.where(is_mine, -1.0, row), value, 0.0)
    lane = lanes_of((ring, width))
    slot = (lane >= SLOT * ZS) & (lane < SLOT * (ZS + 1))
    place = lane - SLOT * ZS
    shift = SLOT * ZS + 3
    before = jnp.where(me == 0, 0.0, pltpu.roll(other, shift, 1))
    source[0] = mine
    source[1] = jnp.where(slot, jnp.where(place < 3, before, pltpu.roll(mine, shift, 1)), 0.0)
    shift = SLOT * ZS + 5
    after = jnp.where(me == 0, pltpu.roll(other, shift, 1), 0.0)
    source[2] = jnp.where(slot, jnp.where(place < 5, pltpu.roll(mine, shift, 1), after), 0.0)


def evolve(*refs, n_adj, n_rows, n_swaps):
    fields, permittivity, even, odd = refs[:4]
    y_halos = [refs[4 + 2 * k : 6 + 2 * k] for k in range(n_swaps)]
    rest = refs[4 + 2 * n_swaps :]
    if n_adj:
        blocks, rest = rest[0], rest[1:]
    else:
        given, rest = rest[0], rest[1:]
    out, tile, grid, coeffs, strip, strip_coeffs, source, edge_e, edge_h = rest
    px = lax.axis_index("xs") % 2
    me = lax.axis_index("ys")
    layers, cells_x, width = fields.shape[1:]
    tiles = cells_x // TILE
    ring = cells_x + TILE
    full = (ring, width)
    lane, row = lanes_of(full), rows_of(full)

    for z in range(layers):
        for c in range(6):
            grid[c, z, 0:cells_x, :] = fields[c, z]
            grid[c, z, cells_x:ring, :] = halo_tile(even, odd, px, c, z, layers)
        coeffs[z, 0:cells_x, :] = time_step / permittivity[z]
        coeffs[z, cells_x:ring, :] = halo_tile(even, odd, px, 6, z, layers)

    if n_adj:
        end = PARTS * (layers // 2) * TILE
        y_end, d_end = PAIRS * ring, PAIRS // 2 * TILE
        y_ref, d_ref = y_halos[0]
        sets = [
            (blocks, 0, None),
            (even, end, px == 0),
            (odd, end, px == 1),
            (y_ref, y_end, None),
            (y_ref, y_end + n_rows, px == 0),
            (d_ref, d_end, px == 1),
        ]
        gather_sources(sets, px, me, source, n_adj)
    else:
        source[...] = given[...]

    place = lane % SLOT
    odd_half = (row[0:TILE] >= REACH) == (px == 0)
    for q in range(PAIRS):
        arrived = []
        for y_ref, d_ref in y_halos:
            corner = d_ref[q // 2 * TILE : (q // 2 + 1) * TILE, :]
            corner = jnp.where(px == q % 2, pltpu.roll(corner, REACH, 0), corner)
            last = y_ref[q * ring + cells_x : (q + 1) * ring, :]
            arrived.append(
                jnp.concatenate(
                    [y_ref[q * ring : q * ring + cells_x, :], jnp.where(odd_half, corner, last)], 0
                )
            )
        before = jnp.zeros(full, jnp.float32)
        after = jnp.zeros(full, jnp.float32)
        for k, block in enumerate(arrived):
            is_next = me % 2 == k
            after = jnp.where(is_next, block, after)
            before = jnp.where(is_next, before, block)
        for b in range(2):
            c = 2 * q + b
            if c >= PARTS:
                continue
            halo = (
                pltpu.roll(before, width - 4, 1) if b else before,
                pltpu.roll(after, 1 if b else 5, 1),
            )
            for side in (0, 1):
                total = jnp.zeros(full, jnp.float32)
                for z in range(layers):
                    block = grid[c, z] if c < 6 else coeffs[z]
                    shift = (SLOT * z + (5 if side else 3)) % width
                    total = jnp.where(lane // SLOT == z, pltpu.roll(block, shift, 1), total)
                total = jnp.where((place >= 5) if side else (place < 3), halo[side], total)
                if c < 6:
                    strip[side, c] = total
                else:
                    strip_coeffs[side] = total

    no_prev_x = (row >= ring - REACH) & (lax.axis_index("xs") == 0)
    step_main = jnp.where(no_prev_x, 0.0, time_step)
    step_strip = (
        jnp.where((place < 3) & (me == 0), 0.0, step_main),
        step_main,
    )

    def next_x(v):
        return pltpu.roll(v, ring - 1, 0)

    def prev_x(v):
        return pltpu.roll(v, 1, 0)

    for step in range(STEPS):
        for side in (0, 1):
            ex, ey, ez, hx, hy, hz = [strip[side, c] for c in range(6)]
            dt, co = step_strip[side], strip_coeffs[side]
            if side:
                edge_e[step, 0], edge_e[step, 1] = ex, ez

            def next_y(v):
                return pltpu.roll(v, width - 1, 1)

            def prev_y(v):
                return pltpu.roll(v, 1, 1)

            def next_z(v):
                return jnp.where(lane < width - SLOT, pltpu.roll(v, width - SLOT, 1), 0.0)

            def prev_z(v):
                return jnp.where(lane >= SLOT, pltpu.roll(v, SLOT, 1), 0.0)

            hx = hx - dt * (next_y(ez) - ez - (next_z(ey) - ey))
            hy = hy - dt * (next_z(ex) - ex - (next_x(ez) - ez))
            hz = hz - dt * (next_x(ey) - ey - (next_y(ex) - ex))
            if not side:
                edge_h[step, 0], edge_h[step, 1] = hx, hz
            if step + 1 == STEPS:
                continue
            ex = ex + co * (hz - prev_y(hz) - (hy - prev_z(hy)))
            ey = ey + co * (hx - prev_z(hx) - (hz - prev_x(hz)))
            ez = ez + co * (hy - prev_x(hy) - (hx - prev_y(hx)) - source[1 + side])
            for c, v in enumerate((ex, ey, ez, hx, hy, hz)):
                strip[side, c] = v

    for step in range(STEPS):
        final = step + 1 == STEPS
        below = (None, None)
        for z in range(layers):
            ex, ey, ez, hx, hy, hz = [grid[c, z] for c in range(6)]
            co = coeffs[z]
            if z + 1 < layers:
                ex_z, ey_z = grid[0, z + 1] - ex, grid[1, z + 1] - ey
            else:
                ex_z, ey_z = 0.0 - ex, 0.0 - ey

            def next_y(v, edge):
                shift = (width - 1 - (SLOT * z + 5)) % width
                return jnp.where(
                    lane == width - 1, pltpu.roll(edge, shift, 1), pltpu.roll(v, width - 1, 1)
                )

            def prev_y(v, edge):
                shift = (width - (SLOT * z + 2)) % width
                return jnp.where(lane == 0, pltpu.roll(edge, shift, 1), pltpu.roll(v, 1, 1))

            hx = hx - step_main * (next_y(ez, edge_e[step, 1]) - ez - ey_z)
            hy = hy - step_main * (ex_z - (next_x(ez) - ez))
            hz = hz - step_main * (next_x(ey) - ey - (next_y(ex, edge_e[step, 0]) - ex))
            hx_z = hx - below[0] if z else hx
            hy_z = hy - below[1] if z else hy
            hx_y = hx - prev_y(hx, edge_h[step, 0])
            ex = ex + co * (hz - prev_y(hz, edge_h[step, 1]) - hy_z)
            ey = ey + co * (hx_z - (hz - prev_x(hz)))
            ez_change = hy - prev_x(hy) - hx_y
            if z == ZS:
                ez_change = ez_change - source[0]
            ez = ez + co * ez_change
            below = (hx, hy)
            for c, v in enumerate((ex, ey, ez, hx, hy, hz)):
                if final:
                    out[c, z] = v[0:cells_x]
                else:
                    grid[c, z] = v
            if final and z == ZS:
                for k, v in enumerate((-hy, hx, ey, -ex)):
                    tile[:, k * width : (k + 1) * width] = v[0:cells_x]


def multiply(weights, own, other, keep, send):
    tiles = jnp.concatenate([own[...], other[...]], 0)
    total = jnp.dot(
        weights[...],
        tiles,
        precision=lax.Precision.HIGHEST,
        preferred_element_type=jnp.float32,
    )
    half = keep.shape[0]
    keep[...] = total[0:half]
    send[...] = total[half:]


def add_split(first, second, keep, send):
    half = keep.shape[0]
    keep[...] = first[0:half, :] + second[0:half, :]
    send[...] = first[half:, :] + second[half:, :]


def shape_of(*dims):
    return jax.ShapeDtypeStruct(dims, jnp.float32)


def far_field_weights(angle_wave, xs_size, cells_x):
    me = lax.axis_index("xs")
    bits = xs_size.bit_length() - 1
    per_block = angle_wave.shape[0] // xs_size
    view = angle_wave.reshape((2,) * bits + (per_block,))
    for k in range(bits):
        bit = (me >> (bits - 1 - k)) & 1
        view = jnp.where(bit == 1, jnp.flip(view, k), view)
    view = view[(slice(None),) * (bits - 1) + (0,)]
    order = tuple(range(bits - 2, -1, -1)) + (bits - 1,)
    angles = view.transpose(order).reshape(-1)
    within = jnp.arange(cells_x, dtype=jnp.int32)
    positions = X0 + jnp.concatenate([me * cells_x + within, (me ^ 1) * cells_x + within])
    phase = angles[:, None] * positions[None, :] % GRID_X
    angle = phase.astype(jnp.float32) * (2.0 * math.pi / GRID_X)
    scale = 1.0 / math.sqrt(cells_x * xs_size)
    both = jnp.stack([jnp.cos(angle) * scale, -jnp.sin(angle) * scale], axis=1)
    return both.reshape(-1, 2 * cells_x)


def far_field_exchange(tile, angle_wave, xs_size):
    cells_x, columns = tile.shape
    bits = xs_size.bit_length() - 1
    weights = far_field_weights(angle_wave, xs_size, cells_x)

    def across(block, mask):
        return lax.ppermute(block, "xs", [(i, i ^ mask) for i in range(xs_size)])

    other = across(tile, 1)
    half = weights.shape[0] // 2
    keep, send = pl.pallas_call(
        multiply,
        out_shape=(shape_of(half, columns),) * 2,
        in_specs=[VMEM] * 3,
        out_specs=(VMEM, VMEM),
        compiler_params=PARAMS,
        name="partial_spectrum",
    )(weights, tile, other)
    for k in range(1, bits):
        arrived = across(send, 1 << k)
        if k + 1 == bits:
            return keep + arrived
        half = half // 2
        keep, send = pl.pallas_call(
            add_split,
            out_shape=(shape_of(half, columns),) * 2,
            in_specs=[VMEM] * 2,
            out_specs=(VMEM, VMEM),
            compiler_params=PARAMS,
            name="add_arrived",
        )(keep, arrived)


def gathered_sources(adj_values, adj_owner, adj_row, cells_x, cells_y):
    groups = lax.axis_size("ys")
    owners = adj_owner[:, 0]
    hits = (owners[:, None] == jnp.arange(groups, dtype=jnp.int32)[None, :]).astype(jnp.int32)
    before = jnp.cumsum(hits, axis=0) - hits
    slot_index = owners * CAP + jnp.sum(before * hits, axis=1)
    placing = (jnp.arange(groups * CAP, dtype=jnp.int32)[:, None] == slot_index[None, :]).astype(
        jnp.float32
    )
    rows = jnp.broadcast_to(adj_row.astype(jnp.float32)[:, None], (adj_row.shape[0], 1))
    outgoing = jnp.dot(
        placing, jnp.concatenate([adj_values, rows], 1), precision=lax.Precision.HIGHEST
    ).reshape(groups, CAP, cells_y + 1)
    incoming = lax.all_to_all(outgoing, "ys", split_axis=0, concat_axis=0, tiled=True)
    incoming = incoming.reshape(groups * CAP, cells_y + 1)
    landing = (
        jnp.arange(cells_x, dtype=jnp.float32)[:, None] == incoming[:, cells_y][None, :]
    ).astype(jnp.float32)
    current = jnp.dot(landing, incoming[:, :cells_y], precision=lax.Precision.HIGHEST)

    def shifted(block, axis, distance):
        size = lax.axis_size(axis)
        route = [(i, i + distance) for i in range(size) if 0 <= i + distance < size]
        return lax.ppermute(block, axis, route)

    after = shifted(current[:REACH], "xs", -1)
    before = shifted(current[-REACH:], "xs", 1)
    ringed = jnp.concatenate([current, after, before], 0)
    right = shifted(ringed[:, :3], "ys", -1)
    left = shifted(ringed[:, -3:], "ys", 1)
    start, end = SLOT * ZS, cells_y - SLOT * (ZS + 1)
    first = jnp.pad(jnp.concatenate([left, ringed[:, :5]], 1), ((0, 0), (start, end)))
    second = jnp.pad(jnp.concatenate([ringed[:, -5:], right], 1), ((0, 0), (start, end)))
    return jnp.stack([ringed, first, second])


def on_device(fields, permittivity, adj_values, adj_owner, adj_row, angle_wave):
    layers, cells_x, cells_y = fields.shape[1:]
    xs_size, ys_size = lax.axis_size("xs"), lax.axis_size("ys")
    raw = ys_size == 2
    n_adj = adj_values.shape[0] if raw else 0
    n_rows = -(-3 * n_adj // TILE) * TILE
    ring = cells_x + TILE
    x_rows = PARTS * (layers // 2) * TILE + n_rows
    y_rows = PAIRS * ring + 2 * n_rows
    d_rows = PAIRS // 2 * TILE + n_rows

    lo = pl.BlockSpec((6, layers, TILE, cells_y), lambda i: (0, 0, 0, 0))
    hi = pl.BlockSpec((6, layers, TILE, cells_y), lambda i: (0, 0, cells_x // TILE - 1, 0))
    p_lo = pl.BlockSpec((layers, TILE, cells_y), lambda i: (0, 0, 0))
    p_hi = pl.BlockSpec((layers, TILE, cells_y), lambda i: (0, cells_x // TILE - 1, 0))
    extra = (adj_values, adj_row, adj_owner) if raw else ()
    packed = pl.pallas_call(
        functools.partial(pack_x, n_adj=n_adj),
        grid=(1,),
        out_shape=(shape_of(x_rows, cells_y),) * 2 + ((shape_of(n_rows, cells_y),) if raw else ()),
        in_specs=[lo, hi, p_lo, p_hi] + ([VMEM, SMEM, SMEM] if raw else []),
        out_specs=(VMEM,) * (3 if raw else 2),
        compiler_params=PARAMS,
        name="pack_x_edges",
    )(fields, fields, permittivity, permittivity, *extra)
    blocks = packed[2:]
    x_even, x_odd = swaps(xs_size)
    from_even = lax.ppermute(packed[0], "xs", x_even)
    from_odd = lax.ppermute(packed[1], "xs", x_odd)

    y_halos = []
    y_swaps = swaps(ys_size)
    for k, route in enumerate(y_swaps):
        to_y, to_diag = pl.pallas_call(
            functools.partial(pack_y, n_rows=n_rows, swap=k),
            out_shape=(shape_of(y_rows, cells_y), shape_of(d_rows, cells_y)),
            in_specs=[VMEM] * (3 + len(blocks)),
            out_specs=(VMEM, VMEM),
            compiler_params=PARAMS,
            name="pack_y_edges",
        )(fields, permittivity, from_even, *blocks)
        diagonal = [(a * ys_size + c, b * ys_size + d) for a, b in x_odd for c, d in route]
        y_halos += [
            lax.ppermute(to_y, "ys", route),
            lax.ppermute(to_diag, ("xs", "ys"), diagonal),
        ]

    if raw:
        sources = blocks
    else:
        sources = (gathered_sources(adj_values, adj_owner, adj_row, cells_x, cells_y),)

    new_fields, tile = pl.pallas_call(
        functools.partial(evolve, n_adj=n_adj, n_rows=n_rows, n_swaps=len(y_swaps)),
        out_shape=(shape_of(*fields.shape), shape_of(cells_x, 4 * cells_y)),
        in_specs=[VMEM] * (4 + len(y_halos) + 1),
        out_specs=(VMEM, VMEM),
        scratch_shapes=[
            pltpu.VMEM((6, layers, ring, cells_y), jnp.float32),
            pltpu.VMEM((layers, ring, cells_y), jnp.float32),
            pltpu.VMEM((2, 6, ring, cells_y), jnp.float32),
            pltpu.VMEM((2, ring, cells_y), jnp.float32),
            pltpu.VMEM((3, ring, cells_y), jnp.float32),
            pltpu.VMEM((STEPS, 2, ring, cells_y), jnp.float32),
            pltpu.VMEM((STEPS, 2, ring, cells_y), jnp.float32),
        ],
        compiler_params=PARAMS,
        name="time_steps",
    )(fields, permittivity, from_even, from_odd, *y_halos, *sources)
    far = far_field_exchange(tile, angle_wave, xs_size)
    per_block = angle_wave.shape[0] // xs_size
    return (new_fields, far.reshape(per_block, 2, 4, cells_y))


def solution(mesh):
    placed = (
        P(None, None, "xs", "ys"),
        P(None, "xs", "ys"),
        P(("xs", "ys"), None),
        P(("xs", "ys"), None),
        P(("xs", "ys")),
        P(),
    )
    return jax.shard_map(
        on_device,
        mesh=mesh,
        in_specs=placed,
        out_specs=(P(None, None, "xs", "ys"), P("xs", None, None, "ys")),
        check_vma=False,
    )
```

time: 139 us -> 45.6 us (0.33)
  waiting for transfers between devices: 47 us -> 10.7 us
  local copies, waits for them, and re-layouts: 25.4 us -> 5.34 us
  starting transfers between devices: 36.4 us -> 18 us
  between operations: 14.8 us -> 0.78 us
  other arithmetic: 11.6 us -> 0.34 us
  Pallas kernels: 0 us -> 10.2 us
  matrix products: 3.64 us -> 0 us
    all_gather x1 -> x0, waiting for transfers between devices: 38.6 us -> none  [on_device(): lax.all_gather(tile, 'xs', axis=1, tiled=True)]
    slice x53 -> x0, local copies, waits for them, and re-layouts: 12.6 us -> none  [the longest x17 6.67 us: along_next(): lax.slice_in_dim(inner, 1, inner.shape[axis], axis=axis)]
    ppermute x12 -> x8, starting transfers between devices: 28.9 us -> 18 us  [the longest x4 13.3 us: across(): return lax.ppermute(block, 'xs', [(i, i ^ mask) for i in range(xs_size)])]
    pallas_call x0 -> x6, Pallas kernels: none -> 10.2 us  [the longest x1 7.43 us: on_device(): pl.pallas_call(functools.partial(evolve, n_adj=n_adj, n_rows=n_rows, n_sw...]
    another operation x21 -> x1, local copies, waits for them, and re-layouts: 7.77 us -> 0.05 us  [far_field_weights(): both = jnp.stack([jnp.cos(angle) * scale, -jnp.sin(angle) * scale], axis=1)]
    all_to_all x2 -> x0, starting transfers between devices: 7.43 us -> none  [the longest x1 4.2 us: on_device(): lax.all_to_all(out_rows, 'ys', split_axis=0, concat_axis=0, tiled=True)]
    ppermute x12 -> x8, waiting for transfers between devices: 4.93 us -> 10.7 us  [the longest x4 8.98 us: across(): return lax.ppermute(block, 'xs', [(i, i ^ mask) for i in range(xs_size)])]
    sub x3 -> x0, other arithmetic: 4.01 us -> none  [the longest x2 2.26 us: advance(): hy_new = magn[1] - time_step * (ex_znext - elec[0] - (ez_xnext - elec[2]))]
  transfers between devices with their start and end apart: 15 -> 8, of which waited for: 8 -> 6; matrix products, arithmetic and copies ran while one was open for 16% -> 1% of each run, Pallas kernels for 0% -> 4%
where the time goes in v1:
time: 45.6 us; the launch traced here: 45.4 us
  starting transfers between devices  18 us (39%)
  waiting for transfers between devices  10.7 us (23%)
  Pallas kernels  10.2 us (22%)
  local copies, waits for them, and re-layouts  5.34 us (12%)
  between operations  0.78 us (2%)
    ppermute x4, starting transfers between devices, across(): return lax.ppermute(block, 'xs', [(i, i ^ mask) for i in range(xs_size)])  13.3 us
    ppermute x4, waiting for transfers between devices, across(): return lax.ppermute(block, 'xs', [(i, i ^ mask) for i in range(xs_size)])  8.98 us
    pallas_call x1, Pallas kernels, on_device(): pl.pallas_call(functools.partial(evolve, n_adj=n_adj, n_rows=n_rows, n_sw...  7.43 us
    unnamed x15, local copies, waits for them, and re-layouts  4.45 us
    ppermute x1, starting transfers between devices, on_device(): lax.ppermute(to_y, 'ys', route)  2.87 us
    ppermute x1, waiting for transfers between devices, on_device(): lax.ppermute(to_y, 'ys', route)  1.69 us
    pallas_call x1, Pallas kernels, on_device(): pl.pallas_call(functools.partial(pack_y, n_rows=n_rows, swap=k), out_shap...  1.63 us
  transfers between devices with their start and end apart: 8, of which 6 were waited for; matrix products, arithmetic and copies ran while one was open for 1% of the time, Pallas kernels for 4%

profile of v1, /device:TPU:0, one launch (start us, length us, event | category | flops | bytes accessed | tf_op | source)
XLA Modules:
  0.0 45.4 jit_solution(6969051548711775584)
XLA Ops:
  0.6 0.7 %copy.10.rest_2_ = s32[4,1]{1,0:T(4,128)S(1)} copy(s32[4,1]{0,1:T(1,128)} %param.9) | data formatting | bytes 32 | tf_op args[3]
  1.4 0.0 copy-start
  1.4 1.4 %copy-done = f32[6,16,32,128]{3,2,1,0:T(8,128)S(1)} copy-done((f32[6,16,32,128]{3,2,1,0:T(8,128)S(1)}, f32[6,16,32,128]{3,2,1,0:T(8,128)}, u32[]{:S(2)}) %copy-start) | copy-done | bytes 1572888
  2.8 0.0 copy-start.2
  2.8 0.9 %copy-done.2 = f32[16,32,128]{2,1,0:T(8,128)S(1)} copy-done((f32[16,32,128]{2,1,0:T(8,128)S(1)}, f32[16,32,128]{2,1,0:T(8,128)}, u32[]{:S(2)}) %copy-start.2) | copy-done | bytes 262168
  3.7 0.0 copy-start.4
  3.7 0.7 %copy-done.4 = f32[4,128]{1,0:T(4,128)S(1)} copy-done((f32[4,128]{1,0:T(4,128)S(1)}, f32[4,128]{1,0:T(4,128)}, u32[]{:S(2)}) %copy-start.4) | copy-done | bytes 2072
  4.4 0.0 copy-start.5
  4.4 0.7 %copy-done.5 = s32[4]{0:T(128)S(1)} copy-done((s32[4]{0:T(128)S(1)}, s32[4]{0:T(128)}, u32[]{:S(2)}) %copy-start.5) | copy-done | bytes 40
  5.1 0.0 copy-start.6
  5.1 0.0 copy-start.1
  5.1 0.0 copy-start.3
  5.1 0.7 %pack_x_edges.1 = (f32[464,128]{1,0:T(8,128)S(1)}, f32[464,128]{1,0:T(8,128)S(1)}, f32[16,128]{1,0:T(8,128)S(1)}) custom-call(f32[6,16,32,128]{3,2,1,0:T(8,128)S(1)} %copy-done, f32[6,16,32,128]{3,2,1,0:T(8,128)S(1)} %copy-done, f32[16,32,128]{2,1,0:T(8,128)S(1)} %copy-done.2, f32[16,32,128]{2,1,0:T(8,128)S(1)} %copy-done.2, f32[4,128]{1,0:T(4,128)S(1)} %copy-done.4, ...), custom_call_target="tpu_custom_call" | custom-call | tf_op jit(solution)/shard_map/pack_x_edges/pallas_call | solution.py:473
  5.8 0.5 %collective-permute-start = (f32[464,128]{1,0:T(8,128)S(1)}, f32[464,128]{1,0:T(8,128)S(1)}, u32[]{:S(2)}, u32[]{:S(2)}) collective-permute-start(f32[464,128]{1,0:T(8,128)S(1)} %get-tuple-element.15), channel_id=1, source_target_pairs={{0,2},{4,6},{8,10},{12,14},{16,18},{20,22},{24,26},{28,30},{2,0},{... | collective-permute-start | bytes 712712 | tf_op jit(solution)/shard_map/ppermute | solution.py:484
  6.3 0.7 %collective-permute-start.1 = (f32[464,128]{1,0:T(8,128)S(1)}, f32[464,128]{1,0:T(8,128)S(1)}, u32[]{:S(2)}, u32[]{:S(2)}) collective-permute-start(f32[464,128]{1,0:T(8,128)S(1)} %get-tuple-element.16), channel_id=1, source_target_pairs={{2,4},{6,8},{10,12},{14,16},{18,20},{22,24},{26,28},{4,2},{8,6},{1... | collective-permute-start | bytes 712712 | tf_op jit(solution)/shard_map/ppermute | solution.py:485
  7.0 0.0 copy-done.6
  7.0 0.1 reshape.161
  7.2 0.1 add_add_fusion
  7.3 0.1 mul.69
  7.4 0.1 collective-permute-done.even.refs_2_
  7.4 0.0 copy-done.1
  7.4 0.0 copy-done.3
  7.5 1.6 %pack_y_edges.1 = (f32[192,128]{1,0:T(8,128)S(1)}, f32[32,128]{1,0:T(8,128)S(1)}) custom-call(f32[6,16,32,128]{3,2,1,0:T(8,128)S(1)} %copy-done.1, f32[16,32,128]{2,1,0:T(8,128)S(1)} %copy-done.3, f32[464,128]{1,0:T(8,128)S(1)} %collective-permute-done.even.refs_2_, f32[16,128]{1,0:T(8,128)S(1)} %get-tuple-element.17.rest_0_.refs_6_), custom_call_target="tpu_custom_call" | custom-call | tf_op jit(solution)/shard_map/pack_y_edges/pallas_call | solution.py:490
  9.1 2.9 %collective-permute-start.2 = (f32[192,128]{1,0:T(8,128)S(1)}, f32[192,128]{1,0:T(8,128)S(1)}, u32[]{:S(2)}, u32[]{:S(2)}) collective-permute-start(f32[192,128]{1,0:T(8,128)S(1)} %get-tuple-element.18), channel_id=1, source_target_pairs={{0,1},{1,0},{2,3},{3,2},{4,5},{5,4},{6,7},{7,6},{8,9},{9,8},{10,11... | collective-permute-start | bytes 294920 | tf_op jit(solution)/shard_map/ppermute | solution.py:500
  11.9 0.7 %collective-permute-start.3 = (f32[32,128]{1,0:T(8,128)S(1)}, f32[32,128]{1,0:T(8,128)S(1)}, u32[]{:S(2)}, u32[]{:S(2)}) collective-permute-start(f32[32,128]{1,0:T(8,128)S(1)} %get-tuple-element.19), channel_id=1, source_target_pairs={{2,5},{3,4},{6,9},{7,8},{10,13},{11,12},{14,17},{15,16},{18,21},{1... | collective-permute-start | bytes 49160 | tf_op jit(solution)/shard_map/ppermute | solution.py:501
  12.6 0.2 cosine_multiply_fusion
  12.8 0.0 collective-permute-done.1.refs_3_
  12.8 0.0 collective-permute-done.3.refs_5_
  12.9 1.7 %collective-permute-done.2.refs_4_ = f32[192,128]{1,0:T(8,128)S(1)} collective-permute-done((f32[192,128]{1,0:T(8,128)S(1)}, f32[192,128]{1,0:T(8,128)S(1)}, u32[]{:S(2)}, u32[]{:S(2)}) %collective-permute-start.2) | collective-permute-done | bytes 98336 | tf_op jit(solution)/shard_map/ppermute | solution.py:500
  14.5 7.4 %time_steps.1 = (f32[6,16,32,128]{3,2,1,0:T(8,128)}, f32[32,512]{1,0:T(8,128)S(1)}) custom-call(f32[6,16,32,128]{3,2,1,0:T(8,128)S(1)} %copy-done.1, f32[16,32,128]{2,1,0:T(8,128)S(1)} %copy-done.3, f32[464,128]{1,0:T(8,128)S(1)} %collective-permute-done.even.refs_2_, f32[464,128]{1,0:T(8,128)S(1)} %collective-permute-done.1.refs_3_, ...), custom_call_target="tpu_custom_call" | custom-call | tf_op jit(solution)/shard_map/time_steps/pallas_call | solution.py:509
  22.0 5.5 %collective-permute-start.4 = (f32[32,512]{1,0:T(8,128)S(1)}, f32[32,512]{1,0:T(8,128)S(1)}, u32[]{:S(2)}, u32[]{:S(2)}) collective-permute-start(f32[32,512]{1,0:T(8,128)S(1)} %get-tuple-element.21.own), channel_id=1, source_target_pairs={{0,2},{2,0},{4,6},{6,4},{8,10},{10,8},{12,14},{14,12},{16,18},{18,... | collective-permute-start | bytes 196616 | tf_op jit(solution)/shard_map/ppermute | solution.py:394
  27.5 0.1 copy.12
  27.6 0.8 %collective-permute-done.4.other = f32[32,512]{1,0:T(8,128)S(1)} collective-permute-done((f32[32,512]{1,0:T(8,128)S(1)}, f32[32,512]{1,0:T(8,128)S(1)}, u32[]{:S(2)}, u32[]{:S(2)}) %collective-permute-start.4) | collective-permute-done | bytes 65568 | tf_op jit(solution)/shard_map/ppermute | solution.py:394
  28.4 0.4 partial_spectrum.1
  28.8 2.5 %collective-permute-start.5 = (f32[64,512]{1,0:T(8,128)S(1)}, f32[64,512]{1,0:T(8,128)S(1)}, u32[]{:S(2)}, u32[]{:S(2)}) collective-permute-start(f32[64,512]{1,0:T(8,128)S(1)} %get-tuple-element.23), channel_id=1, source_target_pairs={{0,4},{2,6},{4,0},{6,2},{8,12},{10,14},{12,8},{14,10},{16,20},{18,... | collective-permute-start | bytes 393224 | tf_op jit(solution)/shard_map/ppermute | solution.py:394
  31.3 4.0 %collective-permute-done.5.second = f32[64,512]{1,0:T(8,128)S(1)} collective-permute-done((f32[64,512]{1,0:T(8,128)S(1)}, f32[64,512]{1,0:T(8,128)S(1)}, u32[]{:S(2)}, u32[]{:S(2)}) %collective-permute-start.5) | collective-permute-done | bytes 131104 | tf_op jit(solution)/shard_map/ppermute | solution.py:394
  35.3 2.2 %collective-permute-start.6 = (f32[32,512]{1,0:T(8,128)S(1)}, f32[32,512]{1,0:T(8,128)S(1)}, u32[]{:S(2)}, u32[]{:S(2)}) collective-permute-start(f32[32,512]{1,0:T(8,128)S(1)} %get-tuple-element.25), channel_id=1, source_target_pairs={{0,8},{2,10},{4,12},{6,14},{8,0},{10,2},{12,4},{14,6},{16,24},{18,... | collective-permute-start | bytes 196616 | tf_op jit(solution)/shard_map/ppermute | solution.py:394
  37.5 2.2 %collective-permute-done.6.second = f32[32,512]{1,0:T(8,128)S(1)} collective-permute-done((f32[32,512]{1,0:T(8,128)S(1)}, f32[32,512]{1,0:T(8,128)S(1)}, u32[]{:S(2)}, u32[]{:S(2)}) %collective-permute-start.6) | collective-permute-done | bytes 65568 | tf_op jit(solution)/shard_map/ppermute | solution.py:394
  39.7 3.1 %collective-permute-start.7 = (f32[16,512]{1,0:T(8,128)S(1)}, f32[16,512]{1,0:T(8,128)S(1)}, u32[]{:S(2)}, u32[]{:S(2)}) collective-permute-start(f32[16,512]{1,0:T(8,128)S(1)} %get-tuple-element.27), channel_id=1, source_target_pairs={{0,16},{2,18},{4,20},{6,22},{8,24},{10,26},{12,28},{14,30},{16,0},... | collective-permute-start | bytes 98312 | tf_op jit(solution)/shard_map/ppermute | solution.py:394
  42.8 1.9 %collective-permute-done.7 = f32[16,512]{1,0:T(8,128)S(1)} collective-permute-done((f32[16,512]{1,0:T(8,128)S(1)}, f32[16,512]{1,0:T(8,128)S(1)}, u32[]{:S(2)}, u32[]{:S(2)}) %collective-permute-start.7) | collective-permute-done | bytes 32800 | tf_op jit(solution)/shard_map/ppermute | solution.py:394
  44.7 0.6 %reshape.163 = f32[8,2,4,128]{3,2,1,0:T(4,128)} reshape(f32[16,512]{1,0:T(8,128)S(1)} %add.53) | data formatting | bytes 65536 | tf_op jit(solution)/shard_map/reshape | solution.py:528
  (11 shorter events, 0.1 us)
Async XLA Ops:
  1.4 1.4 %copy-start = (f32[6,16,32,128]{3,2,1,0:T(8,128)S(1)}, f32[6,16,32,128]{3,2,1,0:T(8,128)}, u32[]{:S(2)}) copy-start(f32[6,16,32,128]{3,2,1,0:T(8,128)} %refs_0_.1) | copy-start | bytes 4718596
  2.8 0.9 %copy-start.2 = (f32[16,32,128]{2,1,0:T(8,128)S(1)}, f32[16,32,128]{2,1,0:T(8,128)}, u32[]{:S(2)}) copy-start(f32[16,32,128]{2,1,0:T(8,128)} %refs_1_.1) | copy-start | bytes 786436
  3.7 0.7 %copy-start.4 = (f32[4,128]{1,0:T(4,128)S(1)}, f32[4,128]{1,0:T(4,128)}, u32[]{:S(2)}) copy-start(f32[4,128]{1,0:T(4,128)} %rest_0_.1) | copy-start | bytes 6148
  4.4 0.7 %copy-start.5 = (s32[4]{0:T(128)S(1)}, s32[4]{0:T(128)}, u32[]{:S(2)}) copy-start(s32[4]{0:T(128)} %rest_1_.1) | copy-start | bytes 52
  5.1 1.9 %copy-start.6 = (s32[128]{0:T(128)S(1)}, s32[128]{0:T(128)}, u32[]{:S(2)}) copy-start(s32[128]{0:T(128)} %param.11) | copy-start | bytes 1540
  5.1 2.4 %copy-start.1 = (f32[6,16,32,128]{3,2,1,0:T(8,128)S(1)}, f32[6,16,32,128]{3,2,1,0:T(8,128)}, u32[]{:S(2)}) copy-start(f32[6,16,32,128]{3,2,1,0:T(8,128)} %refs_0_.1) | copy-start | bytes 4718596
  5.1 2.4 %copy-start.3 = (f32[16,32,128]{2,1,0:T(8,128)S(1)}, f32[16,32,128]{2,1,0:T(8,128)}, u32[]{:S(2)}) copy-start(f32[16,32,128]{2,1,0:T(8,128)} %refs_1_.1) | copy-start | bytes 786436
  5.8 1.6 %collective-permute-start = (f32[464,128]{1,0:T(8,128)S(1)}, f32[464,128]{1,0:T(8,128)S(1)}, u32[]{:S(2)}, u32[]{:S(2)}) collective-permute-start(f32[464,128]{1,0:T(8,128)S(1)} %get-tuple-element.15), channel_id=1, source_target_pairs={{0,2},{4,6},{8,10},{12,14},{16,18},{20,22},{24,26},{28,30},{2,0},{... | collective-permute-start | bytes 712712 | tf_op jit(solution)/shard_map/ppermute | solution.py:484
  6.3 6.5 %collective-permute-start.1 = (f32[464,128]{1,0:T(8,128)S(1)}, f32[464,128]{1,0:T(8,128)S(1)}, u32[]{:S(2)}, u32[]{:S(2)}) collective-permute-start(f32[464,128]{1,0:T(8,128)S(1)} %get-tuple-element.16), channel_id=1, source_target_pairs={{2,4},{6,8},{10,12},{14,16},{18,20},{22,24},{26,28},{4,2},{8,6},{1... | collective-permute-start | bytes 712712 | tf_op jit(solution)/shard_map/ppermute | solution.py:485
  9.1 5.5 %collective-permute-start.2 = (f32[192,128]{1,0:T(8,128)S(1)}, f32[192,128]{1,0:T(8,128)S(1)}, u32[]{:S(2)}, u32[]{:S(2)}) collective-permute-start(f32[192,128]{1,0:T(8,128)S(1)} %get-tuple-element.18), channel_id=1, source_target_pairs={{0,1},{1,0},{2,3},{3,2},{4,5},{5,4},{6,7},{7,6},{8,9},{9,8},{10,11... | collective-permute-start | bytes 294920 | tf_op jit(solution)/shard_map/ppermute | solution.py:500
  11.9 0.9 %collective-permute-start.3 = (f32[32,128]{1,0:T(8,128)S(1)}, f32[32,128]{1,0:T(8,128)S(1)}, u32[]{:S(2)}, u32[]{:S(2)}) collective-permute-start(f32[32,128]{1,0:T(8,128)S(1)} %get-tuple-element.19), channel_id=1, source_target_pairs={{2,5},{3,4},{6,9},{7,8},{10,13},{11,12},{14,17},{15,16},{18,21},{1... | collective-permute-start | bytes 49160 | tf_op jit(solution)/shard_map/ppermute | solution.py:501
  22.0 6.5 %collective-permute-start.4 = (f32[32,512]{1,0:T(8,128)S(1)}, f32[32,512]{1,0:T(8,128)S(1)}, u32[]{:S(2)}, u32[]{:S(2)}) collective-permute-start(f32[32,512]{1,0:T(8,128)S(1)} %get-tuple-element.21.own), channel_id=1, source_target_pairs={{0,2},{2,0},{4,6},{6,4},{8,10},{10,8},{12,14},{14,12},{16,18},{18,... | collective-permute-start | bytes 196616 | tf_op jit(solution)/shard_map/ppermute | solution.py:394
  28.8 6.5 %collective-permute-start.5 = (f32[64,512]{1,0:T(8,128)S(1)}, f32[64,512]{1,0:T(8,128)S(1)}, u32[]{:S(2)}, u32[]{:S(2)}) collective-permute-start(f32[64,512]{1,0:T(8,128)S(1)} %get-tuple-element.23), channel_id=1, source_target_pairs={{0,4},{2,6},{4,0},{6,2},{8,12},{10,14},{12,8},{14,10},{16,20},{18,... | collective-permute-start | bytes 393224 | tf_op jit(solution)/shard_map/ppermute | solution.py:394
  35.3 4.4 %collective-permute-start.6 = (f32[32,512]{1,0:T(8,128)S(1)}, f32[32,512]{1,0:T(8,128)S(1)}, u32[]{:S(2)}, u32[]{:S(2)}) collective-permute-start(f32[32,512]{1,0:T(8,128)S(1)} %get-tuple-element.25), channel_id=1, source_target_pairs={{0,8},{2,10},{4,12},{6,14},{8,0},{10,2},{12,4},{14,6},{16,24},{18,... | collective-permute-start | bytes 196616 | tf_op jit(solution)/shard_map/ppermute | solution.py:394
  39.7 5.0 %collective-permute-start.7 = (f32[16,512]{1,0:T(8,128)S(1)}, f32[16,512]{1,0:T(8,128)S(1)}, u32[]{:S(2)}, u32[]{:S(2)}) collective-permute-start(f32[16,512]{1,0:T(8,128)S(1)} %get-tuple-element.27), channel_id=1, source_target_pairs={{0,16},{2,18},{4,20},{6,22},{8,24},{10,26},{12,28},{14,30},{16,0},... | collective-permute-start | bytes 98312 | tf_op jit(solution)/shard_map/ppermute | solution.py:394

commit v2 on v1

v2 whole, which is shorter than its diff:
```python
import functools
import math

import jax
import jax.numpy as jnp
from jax import lax
from jax.experimental import pallas as pl
from jax.experimental.pallas import tpu as pltpu
from jax.sharding import PartitionSpec as P

STEPS = 3
CAP = 4
GRID_X = 5000
X0 = 2000
ZS = 8

time_step = 0.5

TILE = 8
REACH = 4
SLOT = 8
PARTS = 7
PAIRS = (PARTS + 1) // 2

VMEM = pl.BlockSpec(memory_space=pltpu.VMEM)
HBM = pl.BlockSpec(memory_space=pl.ANY)
PARAMS = pltpu.CompilerParams(vmem_limit_bytes=24 * 1024 * 1024)


def lanes_of(shape):
    return lax.broadcasted_iota(jnp.int32, shape, len(shape) - 1)


def rows_of(shape):
    return lax.broadcasted_iota(jnp.int32, shape, len(shape) - 2)


def swaps(size):
    found = []
    for first in (0, 1):
        pairs = [(i, i + 1) for i in range(first, size - 1, 2)]
        if pairs:
            found.append(pairs + [(j, i) for i, j in pairs])
    return found


def halo_tile(even, odd, px, c, z, layers):
    at = pl.ds((c * (layers // 2) + z // 2) * TILE, TILE)
    from_even, from_odd = even[at, :], odd[at, :]
    same = px == z % 2
    from_even = jnp.where(same, from_even, pltpu.roll(from_even, REACH, 0))
    from_odd = jnp.where(same, pltpu.roll(from_odd, REACH, 0), from_odd)
    odd_half = (rows_of(from_even.shape) >= REACH) == (px == 0)
    return jnp.where(odd_half, from_odd, from_even)


def pack_x(*refs, n_adj):
    fields, permittivity = refs[:2]
    if n_adj:
        values, rows, owners, to_even, to_odd, blocks = refs[2:8]
        edges, edge_perm, rows_s, owners_s, sems = refs[8:]
    else:
        to_even, to_odd, edges, edge_perm, sems = refs[2:]
    px = lax.axis_index("xs") % 2
    layers, cells_x = fields.shape[1:3]
    copies = []
    for k, start in enumerate((0, cells_x - TILE)):
        rows_at = pl.ds(start, TILE)
        copies.append((fields.at[:, :, rows_at, :], edges.at[k]))
        copies.append((permittivity.at[:, rows_at, :], edge_perm.at[k]))
    if n_adj:
        blocks[...] = jnp.zeros(blocks.shape, jnp.float32)
        copies.append((values, blocks.at[pl.ds(0, n_adj), :]))
        copies.append((rows, rows_s))
        copies.append((owners, owners_s))
    copies = [pltpu.make_async_copy(s, d, sems.at[k]) for k, (s, d) in enumerate(copies)]
    for copy in copies:
        copy.start()
    for copy in copies:
        copy.wait()
    for c in range(PARTS):
        for pair in range(layers // 2):
            if c < 6:
                lo = [edges[0, c, 2 * pair + k] for k in (0, 1)]
                hi = [edges[1, c, 2 * pair + k] for k in (0, 1)]
            else:
                lo = [time_step / edge_perm[0, 2 * pair + k] for k in (0, 1)]
                hi = [time_step / edge_perm[1, 2 * pair + k] for k in (0, 1)]
            upper = rows_of(lo[0].shape) >= REACH
            first = jnp.where(upper, pltpu.roll(lo[1], REACH, 0), lo[0])
            last = jnp.where(upper, hi[1], pltpu.roll(hi[0], REACH, 0))
            at = pl.ds((c * (layers // 2) + pair) * TILE, TILE)
            to_even[at, :] = jnp.where(px == 0, last, first)
            to_odd[at, :] = jnp.where(px == 0, first, last)
    if n_adj:
        for b in range(n_adj):
            one = (1, blocks.shape[1])
            row, owner = n_adj + b, 2 * n_adj + b
            blocks[row : row + 1, :] = jnp.full(one, rows_s[b], jnp.int32).astype(jnp.float32)
            blocks[owner : owner + 1, :] = jnp.full(one, owners_s[b], jnp.int32).astype(
                jnp.float32
            )
        end = PARTS * (layers // 2) * TILE
        to_even[end:, :] = blocks[...]
        to_odd[end:, :] = blocks[...]


def pack_columns(tile_of, layers, offset, width):
    quad = ((lanes_of((TILE, width)) + offset) % width) // 4
    total = jnp.zeros((TILE, width), jnp.float32)
    for b in range(2):
        for z in range(layers):
            block = tile_of(b, z)
            if block is None:
                continue
            shift = SLOT * z + 4 * b
            if shift:
                block = pltpu.roll(block, shift, 1)
            total = jnp.where(quad == 2 * z + b, block, total)
    return pltpu.roll(total, offset, 1)


def column_offset(swap):
    return jnp.where(lax.axis_index("ys") % 2 == swap, 3, 0)


def pack_y(fields, permittivity, to_y, *, swap):
    layers, cells_x, width = fields.shape[1:]
    ring = cells_x + TILE
    offset = column_offset(swap)
    for q in range(PAIRS):
        for r in range(cells_x // TILE):
            rows = slice(r * TILE, (r + 1) * TILE)

            def tile_of(b, z):
                c = 2 * q + b
                if c < 6:
                    return fields[c, z, rows, :]
                return time_step / permittivity[z, rows, :] if c < PARTS else None

            at = slice(q * ring + r * TILE, q * ring + (r + 1) * TILE)
            to_y[at, :] = pack_columns(tile_of, layers, offset, width)


def pack_corners(unused, even, odd, *rest, layers, n_rows, swap):
    blocks, to_y = rest if n_rows else (None, rest[0])
    px = lax.axis_index("xs") % 2
    offset = column_offset(swap)
    width = to_y.shape[1]
    ring = (to_y.shape[0] - 3 * n_rows) // PAIRS
    for q in range(PAIRS):

        def tile_of(b, z):
            c = 2 * q + b
            return halo_tile(even, odd, px, c, z, layers) if c < PARTS else None

        to_y[(q + 1) * ring - TILE : (q + 1) * ring, :] = pack_columns(
            tile_of, layers, offset, width
        )
    if n_rows:
        end = PAIRS * ring
        x_end = PARTS * (layers // 2) * TILE
        to_y[end : end + n_rows, :] = blocks[...]
        to_y[end + n_rows : end + 2 * n_rows, :] = even[x_end:, :]
        to_y[end + 2 * n_rows : end + 3 * n_rows, :] = odd[x_end:, :]


def gather_sources(sets, px, me, source, n_adj):
    ring, width = source.shape[1:]
    row_at = rows_of((ring, width)).astype(jnp.float32)
    mine = jnp.zeros((ring, width), jnp.float32)
    other = jnp.zeros((ring, width), jnp.float32)
    own_index = jnp.where(me == 0, 0.0, 1.0)
    cells_x = ring - TILE
    for ref, start, is_next in sets:
        for b in range(n_adj):
            value = ref[start + b : start + b + 1, :]
            row = ref[start + n_adj + b : start + n_adj + b + 1, :]
            owner = ref[start + 2 * n_adj + b : start + 2 * n_adj + b + 1, :]
            if is_next is not None:
                after = jnp.where(row < REACH, row + cells_x, -1.0)
                before = jnp.where(row >= cells_x - REACH, row + TILE, -1.0)
                row = jnp.where(is_next, after, before)
            is_mine = owner == own_index
            mine = mine + jnp.where(row_at == jnp.where(is_mine, row, -1.0), value, 0.0)
            other = other + jnp.where(row_at == jnp.where(is_mine, -1.0, row), value, 0.0)
    lane = lanes_of((ring, width))
    slot = (lane >= SLOT * ZS) & (lane < SLOT * (ZS + 1))
    place = lane - SLOT * ZS
    shift = SLOT * ZS + 3
    before = jnp.where(me == 0, 0.0, pltpu.roll(other, shift, 1))
    source[0] = mine
    source[1] = jnp.where(slot, jnp.where(place < 3, before, pltpu.roll(mine, shift, 1)), 0.0)
    shift = SLOT * ZS + 5
    after = jnp.where(me == 0, pltpu.roll(other, shift, 1), 0.0)
    source[2] = jnp.where(slot, jnp.where(place < 5, pltpu.roll(mine, shift, 1), after), 0.0)


def evolve(*refs, n_adj, n_rows, n_swaps, surface):
    fields, permittivity, even, odd = refs[:4]
    y_halos = refs[4 : 4 + n_swaps]
    given, out, grid, coeffs, strip, strip_coeffs, source, edge_e, edge_h = refs[-9:]
    px = lax.axis_index("xs") % 2
    me = lax.axis_index("ys")
    layers, cells_x, width = fields.shape[1:]
    ring = cells_x + TILE
    full = (ring, width)
    lane, row = lanes_of(full), rows_of(full)
    used = range(layers)
    if surface:
        used = range(max(ZS - STEPS, 0), min(ZS + STEPS + 1, layers))

    for z in used:
        for c in range(6):
            grid[c, z, 0:cells_x, :] = fields[c, z]
            grid[c, z, cells_x:ring, :] = halo_tile(even, odd, px, c, z, layers)
        coeffs[z, 0:cells_x, :] = time_step / permittivity[z]
        coeffs[z, cells_x:ring, :] = halo_tile(even, odd, px, 6, z, layers)

    if n_adj:
        end = PARTS * (layers // 2) * TILE
        y_end = PAIRS * ring
        sets = [
            (given, 0, None),
            (even, end, px == 0),
            (odd, end, px == 1),
            (y_halos[0], y_end, None),
            (y_halos[0], y_end + n_rows, px == 0),
            (y_halos[0], y_end + 2 * n_rows, px == 1),
        ]
        gather_sources(sets, px, me, source, n_adj)
    else:
        source[...] = given[...]

    place = lane % SLOT
    for q in range(PAIRS):
        before = jnp.zeros(full, jnp.float32)
        after = jnp.zeros(full, jnp.float32)
        for k, y_ref in enumerate(y_halos):
            block = y_ref[q * ring : (q + 1) * ring, :]
            is_next = me % 2 == k
            after = jnp.where(is_next, block, after)
            before = jnp.where(is_next, before, block)
        for b in range(2):
            c = 2 * q + b
            if c >= PARTS:
                continue
            halo = (
                pltpu.roll(before, width - 4, 1) if b else before,
                pltpu.roll(after, 1 if b else 5, 1),
            )
            for side in (0, 1):
                total = jnp.zeros(full, jnp.float32)
                for z in used:
                    block = grid[c, z] if c < 6 else coeffs[z]
                    shift = (SLOT * z + (5 if side else 3)) % width
                    total = jnp.where(lane // SLOT == z, pltpu.roll(block, shift, 1), total)
                total = jnp.where((place >= 5) if side else (place < 3), halo[side], total)
                if c < 6:
                    strip[side, c] = total
                else:
                    strip_coeffs[side] = total

    no_prev_x = (row >= ring - REACH) & (lax.axis_index("xs") == 0)
    step_main = jnp.where(no_prev_x, 0.0, time_step)
    step_strip = (
        jnp.where((place < 3) & (me == 0), 0.0, step_main),
        step_main,
    )

    def next_x(v):
        return pltpu.roll(v, ring - 1, 0)

    def prev_x(v):
        return pltpu.roll(v, 1, 0)

    for step in range(STEPS):
        for side in (0, 1):
            ex, ey, ez, hx, hy, hz = [strip[side, c] for c in range(6)]
            dt, co = step_strip[side], strip_coeffs[side]
            if side:
                edge_e[step, 0], edge_e[step, 1] = ex, ez

            def next_y(v):
                return pltpu.roll(v, width - 1, 1)

            def prev_y(v):
                return pltpu.roll(v, 1, 1)

            def next_z(v):
                return jnp.where(lane < width - SLOT, pltpu.roll(v, width - SLOT, 1), 0.0)

            def prev_z(v):
                return jnp.where(lane >= SLOT, pltpu.roll(v, SLOT, 1), 0.0)

            hx = hx - dt * (next_y(ez) - ez - (next_z(ey) - ey))
            hy = hy - dt * (next_z(ex) - ex - (next_x(ez) - ez))
            hz = hz - dt * (next_x(ey) - ey - (next_y(ex) - ex))
            if not side:
                edge_h[step, 0], edge_h[step, 1] = hx, hz
            if step + 1 == STEPS:
                continue
            ex = ex + co * (hz - prev_y(hz) - (hy - prev_z(hy)))
            ey = ey + co * (hx - prev_z(hx) - (hz - prev_x(hz)))
            ez = ez + co * (hy - prev_x(hy) - (hx - prev_y(hx)) - source[1 + side])
            for c, v in enumerate((ex, ey, ez, hx, hy, hz)):
                strip[side, c] = v

    for step in range(STEPS):
        final = step + 1 == STEPS
        low, high = 0, layers - 1
        if surface:
            low, high = max(ZS - STEPS + step, 0), min(ZS + STEPS - 1 - step, layers - 1)
        below = None
        for z in range(low, high + 1):
            ex, ey, ez, hx, hy, hz = [grid[c, z] for c in range(6)]
            co = coeffs[z]
            if z + 1 < layers:
                ex_z, ey_z = grid[0, z + 1] - ex, grid[1, z + 1] - ey
            else:
                ex_z, ey_z = 0.0 - ex, 0.0 - ey

            def next_y(v, edge):
                shift = (width - 1 - (SLOT * z + 5)) % width
                return jnp.where(
                    lane == width - 1, pltpu.roll(edge, shift, 1), pltpu.roll(v, width - 1, 1)
                )

            def prev_y(v, edge):
                shift = (width - (SLOT * z + 2)) % width
                return jnp.where(lane == 0, pltpu.roll(edge, shift, 1), pltpu.roll(v, 1, 1))

            hx = hx - step_main * (next_y(ez, edge_e[step, 1]) - ez - ey_z)
            hy = hy - step_main * (ex_z - (next_x(ez) - ez))
            hz = hz - step_main * (next_x(ey) - ey - (next_y(ex, edge_e[step, 0]) - ex))
            if z == 0 or below:
                hx_z = hx - below[0] if z else hx
                hy_z = hy - below[1] if z else hy
                hx_y = hx - prev_y(hx, edge_h[step, 0])
                ex = ex + co * (hz - prev_y(hz, edge_h[step, 1]) - hy_z)
                ey = ey + co * (hx_z - (hz - prev_x(hz)))
                ez_change = hy - prev_x(hy) - hx_y
                if z == ZS:
                    ez_change = ez_change - source[0]
                ez = ez + co * ez_change
            below = (hx, hy)
            if not final:
                for c, v in enumerate((ex, ey, ez, hx, hy, hz)):
                    grid[c, z] = v
            elif not surface:
                for c, v in enumerate((ex, ey, ez, hx, hy, hz)):
                    out[c, z] = v[0:cells_x]
            elif z == ZS:
                for k, v in enumerate((-hy, hx, ey, -ex)):
                    out[:, k * width : (k + 1) * width] = v[0:cells_x]


def multiply(weights, *refs, n_tiles):
    tiles, parts = refs[:n_tiles], refs[n_tiles:]
    total = jnp.dot(
        weights[...],
        jnp.concatenate([tile[...] for tile in tiles], 0),
        precision=lax.Precision.HIGHEST,
        preferred_element_type=jnp.float32,
    )
    rows = parts[0].shape[0]
    for k, part in enumerate(parts):
        part[...] = total[k * rows : (k + 1) * rows]


def add_parts(*refs):
    parts, out = refs[:-1], refs[-1]
    total = parts[0][...]
    for part in parts[1:]:
        total = total + part[...]
    width = out.shape[2]
    for k in range(out.shape[1]):
        out[:, k, :] = total[:, k * width : (k + 1) * width]


def shape_of(*dims):
    return jax.ShapeDtypeStruct(dims, jnp.float32)


def far_field_weights(angle_wave, xs_size, cells_x, near):
    me = lax.axis_index("xs")
    per_block = angle_wave.shape[0] // xs_size
    far = xs_size // near
    bits = far.bit_length() - 1
    view = angle_wave.reshape(far, near, per_block)
    pick = jnp.arange(near, dtype=jnp.int32)[None, :, None] == me % near
    view = jnp.sum(jnp.where(pick, view, 0), axis=1).reshape((2,) * bits + (per_block,))
    for k in range(bits):
        bit = (me // near >> (bits - 1 - k)) & 1
        view = jnp.where(bit == 1, jnp.flip(view, k), view)
    angles = view.reshape(-1)
    owners = me ^ jnp.arange(near, dtype=jnp.int32)
    within = jnp.arange(cells_x, dtype=jnp.int32)
    positions = X0 + (owners[:, None] * cells_x + within[None, :]).reshape(-1)
    phase = angles[:, None] * positions[None, :] % GRID_X
    angle = phase.astype(jnp.float32) * (2.0 * math.pi / GRID_X)
    scale = 1.0 / math.sqrt(cells_x * xs_size)
    both = jnp.stack([jnp.cos(angle) * scale, -jnp.sin(angle) * scale], axis=1)
    return both.reshape(-1, near * cells_x)


def far_field_exchange(tile, angle_wave, xs_size):
    cells_x, columns = tile.shape
    near = 4
    weights = far_field_weights(angle_wave, xs_size, cells_x, near)

    def across(block, mask):
        return lax.ppermute(block, "xs", [(i, i ^ mask) for i in range(xs_size)])

    third = across(tile, 2)
    second = across(tile, 1)
    fourth = across(third, 1)
    far = xs_size // near
    rows = weights.shape[0] // far
    parts = pl.pallas_call(
        functools.partial(multiply, n_tiles=near),
        out_shape=(shape_of(rows, columns),) * far,
        in_specs=[VMEM] * (near + 1),
        out_specs=(VMEM,) * far,
        compiler_params=PARAMS,
        name="partial_spectrum",
    )(weights, tile, second, third, fourth)
    arrived = [across(parts[k], k * near) for k in range(far - 1, 0, -1)]
    return pl.pallas_call(
        add_parts,
        out_shape=shape_of(rows, 4, columns // 4),
        in_specs=[VMEM] * far,
        out_specs=VMEM,
        compiler_params=PARAMS,
        name="add_arrived",
    )(parts[0], *arrived)


def gathered_sources(adj_values, adj_owner, adj_row, cells_x, cells_y):
    groups = lax.axis_size("ys")
    owners = adj_owner[:, 0]
    hits = (owners[:, None] == jnp.arange(groups, dtype=jnp.int32)[None, :]).astype(jnp.int32)
    before = jnp.cumsum(hits, axis=0) - hits
    slot_index = owners * CAP + jnp.sum(before * hits, axis=1)
    placing = (jnp.arange(groups * CAP, dtype=jnp.int32)[:, None] == slot_index[None, :]).astype(
        jnp.float32
    )
    rows = jnp.broadcast_to(adj_row.astype(jnp.float32)[:, None], (adj_row.shape[0], 1))
    outgoing = jnp.dot(
        placing, jnp.concatenate([adj_values, rows], 1), precision=lax.Precision.HIGHEST
    ).reshape(groups, CAP, cells_y + 1)
    incoming = lax.all_to_all(outgoing, "ys", split_axis=0, concat_axis=0, tiled=True)
    incoming = incoming.reshape(groups * CAP, cells_y + 1)
    landing = (
        jnp.arange(cells_x, dtype=jnp.float32)[:, None] == incoming[:, cells_y][None, :]
    ).astype(jnp.float32)
    current = jnp.dot(landing, incoming[:, :cells_y], precision=lax.Precision.HIGHEST)

    def shifted(block, axis, distance):
        size = lax.axis_size(axis)
        route = [(i, i + distance) for i in range(size) if 0 <= i + distance < size]
        return lax.ppermute(block, axis, route)

    after = shifted(current[:REACH], "xs", -1)
    before = shifted(current[-REACH:], "xs", 1)
    ringed = jnp.concatenate([current, after, before], 0)
    right = shifted(ringed[:, :3], "ys", -1)
    left = shifted(ringed[:, -3:], "ys", 1)
    start, end = SLOT * ZS, cells_y - SLOT * (ZS + 1)
    first = jnp.pad(jnp.concatenate([left, ringed[:, :5]], 1), ((0, 0), (start, end)))
    second = jnp.pad(jnp.concatenate([ringed[:, -5:], right], 1), ((0, 0), (start, end)))
    return jnp.stack([ringed, first, second])


def on_device(fields, permittivity, adj_values, adj_owner, adj_row, angle_wave):
    layers, cells_x, cells_y = fields.shape[1:]
    xs_size, ys_size = lax.axis_size("xs"), lax.axis_size("ys")
    raw = ys_size == 2
    n_adj = adj_values.shape[0] if raw else 0
    n_rows = -(-3 * n_adj // TILE) * TILE
    ring = cells_x + TILE
    x_rows = PARTS * (layers // 2) * TILE + n_rows
    y_rows = PAIRS * ring + 3 * n_rows

    extra = (adj_values, adj_row, adj_owner.reshape(-1)) if raw else ()
    packed = pl.pallas_call(
        functools.partial(pack_x, n_adj=n_adj),
        out_shape=(shape_of(x_rows, cells_y),) * 2 + ((shape_of(n_rows, cells_y),) if raw else ()),
        in_specs=[HBM] * (2 + len(extra)),
        out_specs=(VMEM,) * (3 if raw else 2),
        scratch_shapes=[
            pltpu.VMEM((2, 6, layers, TILE, cells_y), jnp.float32),
            pltpu.VMEM((2, layers, TILE, cells_y), jnp.float32),
        ]
        + ([pltpu.SMEM((n_adj,), jnp.int32)] * 2 if raw else [])
        + [pltpu.SemaphoreType.DMA((4 + len(extra),))],
        compiler_params=PARAMS,
        name="pack_x_edges",
    )(*[pltpu.with_memory_space_constraint(x, pltpu.HBM) for x in (fields, permittivity, *extra)])
    blocks = packed[2:]
    x_even, x_odd = swaps(xs_size)
    from_even = lax.ppermute(packed[0], "xs", x_even)
    from_odd = lax.ppermute(packed[1], "xs", x_odd)

    y_halos = []
    y_swaps = swaps(ys_size)
    for k, route in enumerate(y_swaps):
        to_y = pl.pallas_call(
            functools.partial(pack_y, swap=k),
            out_shape=shape_of(y_rows, cells_y),
            in_specs=[VMEM] * 2,
            out_specs=VMEM,
            compiler_params=PARAMS,
            name="pack_y_edges",
        )(fields, permittivity)
        to_y = pl.pallas_call(
            functools.partial(pack_corners, layers=layers, n_rows=n_rows, swap=k),
            out_shape=shape_of(y_rows, cells_y),
            in_specs=[VMEM] * (3 + len(blocks)),
            out_specs=VMEM,
            input_output_aliases={0: 0},
            compiler_params=PARAMS,
            name="pack_corners",
        )(to_y, from_even, from_odd, *blocks)
        y_halos.append(lax.ppermute(to_y, "ys", route))

    if raw:
        sources = blocks
    else:
        sources = (gathered_sources(adj_values, adj_owner, adj_row, cells_x, cells_y),)

    def steps(surface, shape, name, *after):
        return pl.pallas_call(
            lambda *refs: evolve(
                *refs[: len(operands)],
                *refs[len(operands) + len(after) :],
                n_adj=n_adj,
                n_rows=n_rows,
                n_swaps=len(y_swaps),
                surface=surface,
            ),
            out_shape=shape,
            in_specs=[VMEM] * len(operands) + [pl.BlockSpec(memory_space=pl.ANY)] * len(after),
            out_specs=VMEM,
            scratch_shapes=[
                pltpu.VMEM((6, layers, ring, cells_y), jnp.float32),
                pltpu.VMEM((layers, ring, cells_y), jnp.float32),
                pltpu.VMEM((2, 6, ring, cells_y), jnp.float32),
                pltpu.VMEM((2, ring, cells_y), jnp.float32),
                pltpu.VMEM((3, ring, cells_y), jnp.float32),
                pltpu.VMEM((STEPS, 2, ring, cells_y), jnp.float32),
                pltpu.VMEM((STEPS, 2, ring, cells_y), jnp.float32),
            ],
            compiler_params=PARAMS,
            name=name,
        )(*operands, *after)

    operands = (fields, permittivity, from_even, from_odd, *y_halos, *sources)
    tile = steps(True, shape_of(cells_x, 4 * cells_y), "surface_steps")
    new_fields = steps(False, shape_of(*fields.shape), "time_steps", tile)
    far = far_field_exchange(tile, angle_wave, xs_size)
    per_block = angle_wave.shape[0] // xs_size
    return (new_fields, far.reshape(per_block, 2, 4, cells_y))


def solution(mesh):
    placed = (
        P(None, None, "xs", "ys"),
        P(None, "xs", "ys"),
        P(("xs", "ys"), None),
        P(("xs", "ys"), None),
        P(("xs", "ys")),
        P(),
    )
    return jax.shard_map(
        on_device,
        mesh=mesh,
        in_specs=placed,
        out_specs=(P(None, None, "xs", "ys"), P("xs", None, None, "ys")),
        check_vma=False,
    )
```

time: 45.6 us -> 38.5 us (0.84)
  waiting for transfers between devices: 10.7 us -> 5.67 us
  local copies, waits for them, and re-layouts: 5.34 us -> 0.33 us
  Pallas kernels: 10.2 us -> 13.2 us
    ppermute x4 -> x6, waiting for transfers between devices: 8.98 us -> 3.22 us  [across(): return lax.ppermute(block, 'xs', [(i, i ^ mask) for i in range(xs_size)])]
    unnamed x15 -> x6, local copies, waits for them, and re-layouts: 4.45 us -> 0.01 us
    pallas_call x6 -> x7, Pallas kernels: 10.2 us -> 13.2 us  [the longest x2 9.33 us: steps(): pl.pallas_call(lambda *refs: evolve(*refs[:len(operands)], *refs[len(oper...]
    ppermute x4 -> x6, starting transfers between devices: 13.3 us -> 14.3 us  [across(): return lax.ppermute(block, 'xs', [(i, i ^ mask) for i in range(xs_size)])]
    ppermute x2 -> x1, starting transfers between devices: 3.52 us -> 2.51 us  [on_device(): y_halos.append(lax.ppermute(to_y, 'ys', route))]
    ppermute x2 -> x1, waiting for transfers between devices: 1.7 us -> 2.44 us  [on_device(): y_halos.append(lax.ppermute(to_y, 'ys', route))]
    reshape x2 -> x1, local copies, waits for them, and re-layouts: 0.72 us -> 0.09 us  [far_field_weights(): view = angle_wave.reshape(far, near, per_block)]
  transfers between devices with their start and end apart: 8 -> 9, of which waited for: 6 -> 3; matrix products, arithmetic and copies ran while one was open for 1% -> 2% of each run, Pallas kernels for 4% -> 23%
where the time goes in v2:
time: 38.5 us; the launch traced here: 38.4 us
  starting transfers between devices  18 us (47%)
  Pallas kernels  13.2 us (34%)
  waiting for transfers between devices  5.67 us (15%)
  between operations  0.81 us (2%)
    ppermute x6, starting transfers between devices, across(): return lax.ppermute(block, 'xs', [(i, i ^ mask) for i in range(xs_size)])  14.3 us
    pallas_call x2, Pallas kernels, steps(): pl.pallas_call(lambda *refs: evolve(*refs[:len(operands)], *refs[len(oper...  9.33 us
    ppermute x6, waiting for transfers between devices, across(): return lax.ppermute(block, 'xs', [(i, i ^ mask) for i in range(xs_size)])  3.22 us
    ppermute x1, starting transfers between devices, on_device(): y_halos.append(lax.ppermute(to_y, 'ys', route))  2.51 us
    ppermute x1, waiting for transfers between devices, on_device(): y_halos.append(lax.ppermute(to_y, 'ys', route))  2.44 us
    pallas_call x1, Pallas kernels, on_device(): pl.pallas_call(functools.partial(pack_x, n_adj=n_adj), out_shape=(shape_o...  1.44 us
    pallas_call x1, Pallas kernels, on_device(): pl.pallas_call(functools.partial(pack_y, swap=k), out_shape=shape_of(y_ro...  1.24 us
  transfers between devices with their start and end apart: 9, of which 3 were waited for; matrix products, arithmetic and copies ran while one was open for 2% of the time, Pallas kernels for 23%

profile of v2, /device:TPU:0, one launch (start us, length us, event | category | flops | bytes accessed | tf_op | source)
XLA Modules:
  0.0 38.4 jit_solution(6870246465819126449)
XLA Ops:
  0.6 0.0 copy-start
  0.6 0.0 copy-start.1
  0.7 0.0 copy-start.2
  0.7 1.4 %pack_x_edges.1 = (f32[464,128]{1,0:T(8,128)S(1)}, f32[464,128]{1,0:T(8,128)S(1)}, f32[16,128]{1,0:T(8,128)S(1)}) custom-call(f32[6,16,32,128]{3,2,1,0:T(8,128)} %refs_0_.5, f32[16,32,128]{2,1,0:T(8,128)} %refs_1_.5, f32[4,128]{1,0:T(4,128)} %refs_2_.1, s32[4]{0:T(128)} %refs_3_.1, s32[4]{0:T(128)} %bitcast.8), custom_call_target="tpu_custom_call" | custom-call | tf_op jit(solution)/shard_map/pack_x_edges/pallas_call | solution.py:486
  2.1 0.5 %collective-permute-start = (f32[464,128]{1,0:T(8,128)S(1)}, f32[464,128]{1,0:T(8,128)S(1)}, u32[]{:S(2)}, u32[]{:S(2)}) collective-permute-start(f32[464,128]{1,0:T(8,128)S(1)} %get-tuple-element.9), channel_id=1, source_target_pairs={{0,2},{4,6},{8,10},{12,14},{16,18},{20,22},{24,26},{28,30},{2,0},{... | collective-permute-start | bytes 712712 | tf_op jit(solution)/shard_map/ppermute | solution.py:502
  2.6 0.7 %collective-permute-start.1 = (f32[464,128]{1,0:T(8,128)S(1)}, f32[464,128]{1,0:T(8,128)S(1)}, u32[]{:S(2)}, u32[]{:S(2)}) collective-permute-start(f32[464,128]{1,0:T(8,128)S(1)} %get-tuple-element.10), channel_id=1, source_target_pairs={{2,4},{6,8},{10,12},{14,16},{18,20},{22,24},{26,28},{4,2},{8,6},{1... | collective-permute-start | bytes 712712 | tf_op jit(solution)/shard_map/ppermute | solution.py:503
  3.3 0.0 copy-done.2
  3.3 0.1 reshape.182
  3.5 0.1 select_reduce_fusion
  3.6 0.0 copy-done
  3.6 0.0 copy-done.1
  3.6 1.2 %pack_y_edges.1.unused = f32[208,128]{1,0:T(8,128)S(1)} custom-call(f32[6,16,32,128]{3,2,1,0:T(8,128)S(1)} %copy-done, f32[16,32,128]{2,1,0:T(8,128)S(1)} %copy-done.1), custom_call_target="tpu_custom_call" | custom-call | tf_op jit(solution)/shard_map/pack_y_edges/pallas_call | solution.py:508
  4.8 0.0 collective-permute-done.even.refs_2_
  4.9 0.0 collective-permute-done.1.odd.refs_3_
  4.9 0.3 pack_corners.1
  5.1 2.5 %collective-permute-start.2 = (f32[208,128]{1,0:T(8,128)S(1)}, f32[208,128]{1,0:T(8,128)S(1)}, u32[]{:S(2)}, u32[]{:S(2)}) collective-permute-start(f32[208,128]{1,0:T(8,128)S(1)} %pack_corners.1), channel_id=1, source_target_pairs={{0,1},{1,0},{2,3},{3,2},{4,5},{5,4},{6,7},{7,6},{8,9},{9,8},{10,11... | collective-permute-start | bytes 319496 | tf_op jit(solution)/shard_map/ppermute | solution.py:525
  7.7 0.1 add_add_fusion
  7.7 0.1 add.60
  7.8 0.1 mul.71
  7.9 2.4 %collective-permute-done.2.refs_4_ = f32[208,128]{1,0:T(8,128)S(1)} collective-permute-done((f32[208,128]{1,0:T(8,128)S(1)}, f32[208,128]{1,0:T(8,128)S(1)}, u32[]{:S(2)}, u32[]{:S(2)}) %collective-permute-start.2) | collective-permute-done | bytes 106528 | tf_op jit(solution)/shard_map/ppermute | solution.py:525
  10.3 1.9 %surface_steps.1.refs_6_.refs_0_ = f32[32,512]{1,0:T(8,128)S(1)} custom-call(f32[6,16,32,128]{3,2,1,0:T(8,128)S(1)} %copy-done, f32[16,32,128]{2,1,0:T(8,128)S(1)} %copy-done.1, f32[464,128]{1,0:T(8,128)S(1)} %collective-permute-done.even.refs_2_, f32[464,128]{1,0:T(8,128)S(1)} %collective-permute-done.1.odd.refs_3_, ...), custom_call_target="tpu_custom_call" | custom-call | tf_op jit(solution)/shard_map/surface_steps/pallas_call | solution.py:533
  12.2 9.8 %collective-permute-start.4 = (f32[32,512]{1,0:T(8,128)S(1)}, f32[32,512]{1,0:T(8,128)S(1)}, u32[]{:S(2)}, u32[]{:S(2)}) collective-permute-start(f32[32,512]{1,0:T(8,128)S(1)} %surface_steps.1.refs_6_.refs_0_), channel_id=1, source_target_pairs={{0,4},{2,6},{4,0},{6,2},{8,12},{10,14},{12,8},{14,10},{16,20},{18,... | collective-permute-start | bytes 196616 | tf_op jit(solution)/shard_map/ppermute | solution.py:413
  22.1 0.2 cosine_multiply_fusion
  22.2 0.1 collective-permute-start.3
  22.3 2.0 %collective-permute-done.4.refs_2_ = f32[32,512]{1,0:T(8,128)S(1)} collective-permute-done((f32[32,512]{1,0:T(8,128)S(1)}, f32[32,512]{1,0:T(8,128)S(1)}, u32[]{:S(2)}, u32[]{:S(2)}) %collective-permute-start.4) | collective-permute-done | bytes 65568 | tf_op jit(solution)/shard_map/ppermute | solution.py:413
  24.3 0.0 collective-permute-start.5
  24.4 0.0 collective-permute-done.3.refs_1_
  24.4 1.2 %collective-permute-done.5.refs_3_ = f32[32,512]{1,0:T(8,128)S(1)} collective-permute-done((f32[32,512]{1,0:T(8,128)S(1)}, f32[32,512]{1,0:T(8,128)S(1)}, u32[]{:S(2)}, u32[]{:S(2)}) %collective-permute-start.5) | collective-permute-done | bytes 65568 | tf_op jit(solution)/shard_map/ppermute | solution.py:413
  25.6 0.3 partial_spectrum.1
  25.8 3.3 %collective-permute-start.6 = (f32[16,512]{1,0:T(8,128)S(1)}, f32[16,512]{1,0:T(8,128)S(1)}, u32[]{:S(2)}, u32[]{:S(2)}) collective-permute-start(f32[16,512]{1,0:T(8,128)S(1)} %get-tuple-element.13), channel_id=1, source_target_pairs={{0,24},{2,26},{4,28},{6,30},{8,16},{10,18},{12,20},{14,22},{16,8},... | collective-permute-start | bytes 98312 | tf_op jit(solution)/shard_map/ppermute | solution.py:413
  29.2 0.0 collective-permute-start.7
  29.2 1.1 %collective-permute-start.8 = (f32[16,512]{1,0:T(8,128)S(1)}, f32[16,512]{1,0:T(8,128)S(1)}, u32[]{:S(2)}, u32[]{:S(2)}) collective-permute-start(f32[16,512]{1,0:T(8,128)S(1)} %get-tuple-element.15), channel_id=1, source_target_pairs={{0,8},{2,10},{4,12},{6,14},{8,0},{10,2},{12,4},{14,6},{16,24},{18,... | collective-permute-start | bytes 98312 | tf_op jit(solution)/shard_map/ppermute | solution.py:413
  30.3 7.4 %time_steps.1 = f32[6,16,32,128]{3,2,1,0:T(8,128)} custom-call(f32[6,16,32,128]{3,2,1,0:T(8,128)S(1)} %copy-done, f32[16,32,128]{2,1,0:T(8,128)S(1)} %copy-done.1, f32[464,128]{1,0:T(8,128)S(1)} %collective-permute-done.even.refs_2_, f32[464,128]{1,0:T(8,128)S(1)} %collective-permute-done.1.odd.refs_3_, f32[208,128]{1,0:T(8,128)S(1)} %collective-permute-done.2.refs_4_, ...), custom_call_target="tpu_custom_call" | custom-call | tf_op jit(solution)/shard_map/time_steps/pallas_call | solution.py:533
  37.7 0.0 collective-permute-done.6.refs_1_
  37.7 0.0 collective-permute-done.7.refs_2_
  37.7 0.0 collective-permute-done.8.refs_3_
  37.7 0.6 %add_arrived.1 = f32[16,4,128]{2,1,0:T(4,128)} custom-call(f32[16,512]{1,0:T(8,128)S(1)} %get-tuple-element.12.refs_0_, f32[16,512]{1,0:T(8,128)S(1)} %collective-permute-done.6.refs_1_, f32[16,512]{1,0:T(8,128)S(1)} %collective-permute-done.7.refs_2_, f32[16,512]{1,0:T(8,128)S(1)} %collective-permute-done.8.refs_3_), custom_call_target="tpu_custom_call" | custom-call | tf_op jit(solution)/shard_map/add_arrived/pallas_call | solution.py:429
  (7 shorter events, 0.1 us)
Async XLA Ops:
  0.6 2.9 %copy-start = (f32[6,16,32,128]{3,2,1,0:T(8,128)S(1)}, f32[6,16,32,128]{3,2,1,0:T(8,128)}, u32[]{:S(2)}) copy-start(f32[6,16,32,128]{3,2,1,0:T(8,128)} %refs_0_.5) | copy-start | bytes 4718596
  0.6 2.9 %copy-start.1 = (f32[16,32,128]{2,1,0:T(8,128)S(1)}, f32[16,32,128]{2,1,0:T(8,128)}, u32[]{:S(2)}) copy-start(f32[16,32,128]{2,1,0:T(8,128)} %refs_1_.5) | copy-start | bytes 786436
  0.7 2.7 %copy-start.2 = (s32[128]{0:T(128)S(1)}, s32[128]{0:T(128)}, u32[]{:S(2)}) copy-start(s32[128]{0:T(128)} %param.11) | copy-start | bytes 1540
  2.1 2.7 %collective-permute-start = (f32[464,128]{1,0:T(8,128)S(1)}, f32[464,128]{1,0:T(8,128)S(1)}, u32[]{:S(2)}, u32[]{:S(2)}) collective-permute-start(f32[464,128]{1,0:T(8,128)S(1)} %get-tuple-element.9), channel_id=1, source_target_pairs={{0,2},{4,6},{8,10},{12,14},{16,18},{20,22},{24,26},{28,30},{2,0},{... | collective-permute-start | bytes 712712 | tf_op jit(solution)/shard_map/ppermute | solution.py:502
  2.6 2.2 %collective-permute-start.1 = (f32[464,128]{1,0:T(8,128)S(1)}, f32[464,128]{1,0:T(8,128)S(1)}, u32[]{:S(2)}, u32[]{:S(2)}) collective-permute-start(f32[464,128]{1,0:T(8,128)S(1)} %get-tuple-element.10), channel_id=1, source_target_pairs={{2,4},{6,8},{10,12},{14,16},{18,20},{22,24},{26,28},{4,2},{8,6},{1... | collective-permute-start | bytes 712712 | tf_op jit(solution)/shard_map/ppermute | solution.py:503
  5.1 5.2 %collective-permute-start.2 = (f32[208,128]{1,0:T(8,128)S(1)}, f32[208,128]{1,0:T(8,128)S(1)}, u32[]{:S(2)}, u32[]{:S(2)}) collective-permute-start(f32[208,128]{1,0:T(8,128)S(1)} %pack_corners.1), channel_id=1, source_target_pairs={{0,1},{1,0},{2,3},{3,2},{4,5},{5,4},{6,7},{7,6},{8,9},{9,8},{10,11... | collective-permute-start | bytes 319496 | tf_op jit(solution)/shard_map/ppermute | solution.py:525
  12.2 12.1 %collective-permute-start.4 = (f32[32,512]{1,0:T(8,128)S(1)}, f32[32,512]{1,0:T(8,128)S(1)}, u32[]{:S(2)}, u32[]{:S(2)}) collective-permute-start(f32[32,512]{1,0:T(8,128)S(1)} %surface_steps.1.refs_6_.refs_0_), channel_id=1, source_target_pairs={{0,4},{2,6},{4,0},{6,2},{8,12},{10,14},{12,8},{14,10},{16,20},{18,... | collective-permute-start | bytes 196616 | tf_op jit(solution)/shard_map/ppermute | solution.py:413
  22.2 2.1 %collective-permute-start.3 = (f32[32,512]{1,0:T(8,128)S(1)}, f32[32,512]{1,0:T(8,128)S(1)}, u32[]{:S(2)}, u32[]{:S(2)}) collective-permute-start(f32[32,512]{1,0:T(8,128)S(1)} %surface_steps.1.refs_6_.refs_0_), channel_id=1, source_target_pairs={{0,2},{2,0},{4,6},{6,4},{8,10},{10,8},{12,14},{14,12},{16,18},{18,... | collective-permute-start | bytes 196616 | tf_op jit(solution)/shard_map/ppermute | solution.py:413
  24.3 1.3 %collective-permute-start.5 = (f32[32,512]{1,0:T(8,128)S(1)}, f32[32,512]{1,0:T(8,128)S(1)}, u32[]{:S(2)}, u32[]{:S(2)}) collective-permute-start(f32[32,512]{1,0:T(8,128)S(1)} %collective-permute-done.4.refs_2_), channel_id=1, source_target_pairs={{0,2},{2,0},{4,6},{6,4},{8,10},{10,8},{12,14},{14,12},{16,18},{18,... | collective-permute-start | bytes 196616 | tf_op jit(solution)/shard_map/ppermute | solution.py:413
  25.8 11.9 %collective-permute-start.6 = (f32[16,512]{1,0:T(8,128)S(1)}, f32[16,512]{1,0:T(8,128)S(1)}, u32[]{:S(2)}, u32[]{:S(2)}) collective-permute-start(f32[16,512]{1,0:T(8,128)S(1)} %get-tuple-element.13), channel_id=1, source_target_pairs={{0,24},{2,26},{4,28},{6,30},{8,16},{10,18},{12,20},{14,22},{16,8},... | collective-permute-start | bytes 98312 | tf_op jit(solution)/shard_map/ppermute | solution.py:413
  29.2 8.6 %collective-permute-start.7 = (f32[16,512]{1,0:T(8,128)S(1)}, f32[16,512]{1,0:T(8,128)S(1)}, u32[]{:S(2)}, u32[]{:S(2)}) collective-permute-start(f32[16,512]{1,0:T(8,128)S(1)} %get-tuple-element.14), channel_id=1, source_target_pairs={{0,16},{2,18},{4,20},{6,22},{8,24},{10,26},{12,28},{14,30},{16,0},... | collective-permute-start | bytes 98312 | tf_op jit(solution)/shard_map/ppermute | solution.py:413
  29.2 8.6 %collective-permute-start.8 = (f32[16,512]{1,0:T(8,128)S(1)}, f32[16,512]{1,0:T(8,128)S(1)}, u32[]{:S(2)}, u32[]{:S(2)}) collective-permute-start(f32[16,512]{1,0:T(8,128)S(1)} %get-tuple-element.15), channel_id=1, source_target_pairs={{0,8},{2,10},{4,12},{6,14},{8,0},{10,2},{12,4},{14,6},{16,24},{18,... | collective-permute-start | bytes 98312 | tf_op jit(solution)/shard_map/ppermute | solution.py:413

commit v3 on v2

v3 whole, which is shorter than its diff:
```python
import functools
import math

import jax
import jax.numpy as jnp
from jax import lax
from jax.experimental import pallas as pl
from jax.experimental.pallas import tpu as pltpu
from jax.sharding import PartitionSpec as P

STEPS = 3
CAP = 4
GRID_X = 5000
X0 = 2000
ZS = 8

time_step = 0.5

TILE = 8
REACH = 4
SLOT = 8
PARTS = 7
PAIRS = (PARTS + 1) // 2
TOGETHER = 8

VMEM = pl.BlockSpec(memory_space=pltpu.VMEM)
ANY = pl.BlockSpec(memory_space=pl.ANY)
PARAMS = pltpu.CompilerParams(vmem_limit_bytes=24 * 1024 * 1024)


def lanes_of(shape):
    return lax.broadcasted_iota(jnp.int32, shape, len(shape) - 1)


def rows_of(shape):
    return lax.broadcasted_iota(jnp.int32, shape, len(shape) - 2)


def swaps(size):
    found = []
    for first in (0, 1):
        pairs = [(i, i + 1) for i in range(first, size - 1, 2)]
        if pairs:
            found.append(pairs + [(j, i) for i, j in pairs])
    return found


def halo_tile(even, odd, px, c, z, layers):
    at = pl.ds(pl.multiple_of((c * (layers // 2) + z // 2) * TILE, TILE), TILE)
    from_even, from_odd = even[at, :], odd[at, :]
    same = px == z % 2
    turned_even, turned_odd = pltpu.roll(from_even, REACH, 0), pltpu.roll(from_odd, REACH, 0)
    odd_half = (rows_of(from_even.shape) >= REACH) == (px == 0)
    return jnp.where(
        same,
        jnp.where(odd_half, turned_odd, from_even),
        jnp.where(odd_half, from_odd, turned_even),
    )


def repeat(first, last, body, together=1):
    count = last - first
    if together >= count:
        for i in range(first, last):
            body(i)
        return
    rounds = count // together

    def several(n, _):
        for k in range(together):
            body(first + n * together + k)

    lax.fori_loop(0, rounds, several, None)
    for i in range(first + rounds * together, last):
        body(i)


def pack_x(*refs, n_adj):
    fields, permittivity = refs[:2]
    if n_adj:
        values, rows, owners, to_even, to_odd, blocks = refs[2:8]
        edges, edge_perm, rows_s, owners_s, sems = refs[8:]
    else:
        to_even, to_odd, edges, edge_perm, sems = refs[2:]
    px = lax.axis_index("xs") % 2
    layers, cells_x = fields.shape[1:3]
    copies = []
    for k, start in enumerate((0, cells_x - TILE)):
        rows_at = pl.ds(start, TILE)
        copies.append((fields.at[:, :, rows_at, :], edges.at[k]))
        copies.append((permittivity.at[:, rows_at, :], edge_perm.at[k]))
    if n_adj:
        blocks[...] = jnp.zeros(blocks.shape, jnp.float32)
        copies.append((values, blocks.at[pl.ds(0, n_adj), :]))
        copies.append((rows, rows_s))
        copies.append((owners, owners_s))
    copies = [pltpu.make_async_copy(s, d, sems.at[k]) for k, (s, d) in enumerate(copies)]
    for copy in copies:
        copy.start()
    for copy in copies:
        copy.wait()
    for c in range(PARTS):
        for pair in range(layers // 2):
            if c < 6:
                lo = [edges[0, c, 2 * pair + k] for k in (0, 1)]
                hi = [edges[1, c, 2 * pair + k] for k in (0, 1)]
            else:
                lo = [time_step / edge_perm[0, 2 * pair + k] for k in (0, 1)]
                hi = [time_step / edge_perm[1, 2 * pair + k] for k in (0, 1)]
            upper = rows_of(lo[0].shape) >= REACH
            first = jnp.where(upper, pltpu.roll(lo[1], REACH, 0), lo[0])
            last = jnp.where(upper, hi[1], pltpu.roll(hi[0], REACH, 0))
            at = pl.ds((c * (layers // 2) + pair) * TILE, TILE)
            to_even[at, :] = jnp.where(px == 0, last, first)
            to_odd[at, :] = jnp.where(px == 0, first, last)
    if n_adj:
        for b in range(n_adj):
            one = (1, blocks.shape[1])
            row, owner = n_adj + b, 2 * n_adj + b
            blocks[row : row + 1, :] = jnp.full(one, rows_s[b], jnp.int32).astype(jnp.float32)
            blocks[owner : owner + 1, :] = jnp.full(one, owners_s[b], jnp.int32).astype(
                jnp.float32
            )
        end = PARTS * (layers // 2) * TILE
        to_even[end:, :] = blocks[...]
        to_odd[end:, :] = blocks[...]


def pack_strips(tile_of, layers):
    first = second = None
    for z in layers:
        block = tile_of(z)
        here = lanes_of(block.shape) // SLOT == z
        lower = pltpu.roll(block, (SLOT * z + 3) % block.shape[1], 1)
        upper = pltpu.roll(block, (SLOT * z + 5) % block.shape[1], 1)
        first = lower if first is None else jnp.where(here, lower, first)
        second = upper if second is None else jnp.where(here, upper, second)
    return first, second


def pack_pair(first, second, to_next):
    edges = [jnp.where(to_next, second[b], first[b]) for b in range(len(first))]
    width = edges[0].shape[1]
    total = pltpu.roll(edges[0], jnp.where(to_next, width - 2, width - 3), 1)
    if len(edges) > 1:
        other = pltpu.roll(edges[1], jnp.where(to_next, 2, 1), 1)
        total = jnp.where(lanes_of(total.shape) % SLOT < 4, total, other)
    return total


def pack_y(fields, permittivity, strips, *to_y):
    layers, cells_x, width = fields.shape[1:]
    ring = cells_x + TILE
    for r in range(cells_x // TILE):
        rows = slice(r * TILE, (r + 1) * TILE)
        for q in range(PAIRS):
            pair = []
            for c in range(2 * q, min(2 * q + 2, PARTS)):

                def tile_of(z):
                    return fields[c, z, rows, :] if c < 6 else time_step / permittivity[z, rows, :]

                pair.append(pack_strips(tile_of, range(layers)))
                for side in (0, 1):
                    strips[side, c, rows, :] = pair[-1][side]
            for swap, message in enumerate(to_y):
                to_next = lax.axis_index("ys") % 2 == swap
                at = slice(q * ring + r * TILE, q * ring + (r + 1) * TILE)
                message[at, :] = pack_pair([p[0] for p in pair], [p[1] for p in pair], to_next)


def pack_corners(*refs, layers, n_rows, n_swaps):
    even, odd = refs[1 + n_swaps : 3 + n_swaps]
    strips, to_y = refs[-1 - n_swaps], refs[-n_swaps:]
    px = lax.axis_index("xs") % 2
    ring = (to_y[0].shape[0] - 3 * n_rows) // PAIRS
    for q in range(PAIRS):
        pair = []
        for c in range(2 * q, min(2 * q + 2, PARTS)):

            def tile_of(z):
                return halo_tile(even, odd, px, c, z, layers)

            pair.append(pack_strips(tile_of, range(layers)))
            for side in (0, 1):
                strips[side, c, ring - TILE : ring, :] = pair[-1][side]
        for swap, message in enumerate(to_y):
            to_next = lax.axis_index("ys") % 2 == swap
            at = slice((q + 1) * ring - TILE, (q + 1) * ring)
            message[at, :] = pack_pair([p[0] for p in pair], [p[1] for p in pair], to_next)
    if n_rows:
        blocks = refs[3 + n_swaps]
        end = PAIRS * ring
        x_end = PARTS * (layers // 2) * TILE
        to_y[0][end : end + n_rows, :] = blocks[...]
        to_y[0][end + n_rows : end + 2 * n_rows, :] = even[x_end:, :]
        to_y[0][end + 2 * n_rows : end + 3 * n_rows, :] = odd[x_end:, :]


def row_index(shape):
    fold = lax.broadcasted_iota(jnp.int32, shape, 0)
    return lax.broadcasted_iota(jnp.int32, shape, 1) * shape[0] + fold


def gather_sources(sets, px, me, source, n_adj, cells_x):
    full = source.shape[1:]
    row_at = row_index(full).astype(jnp.float32)
    mine = jnp.zeros(full, jnp.float32)
    other = jnp.zeros(full, jnp.float32)
    own_index = jnp.where(me == 0, 0.0, 1.0)
    for ref, start, is_next in sets:
        for b in range(n_adj):
            value = ref[start + b : start + b + 1, :]
            row = ref[start + n_adj + b : start + n_adj + b + 1, :]
            owner = ref[start + 2 * n_adj + b : start + 2 * n_adj + b + 1, :]
            if is_next is not None:
                after = jnp.where(row < REACH, row + cells_x, -1.0)
                before = jnp.where(row >= cells_x - REACH, row + TILE, -1.0)
                row = jnp.where(is_next, after, before)
            is_mine = owner == own_index
            mine = mine + jnp.where(row_at == jnp.where(is_mine, row, -1.0), value, 0.0)
            other = other + jnp.where(row_at == jnp.where(is_mine, -1.0, row), value, 0.0)
    lane = lanes_of(full)
    slot = (lane >= SLOT * ZS) & (lane < SLOT * (ZS + 1))
    place = lane - SLOT * ZS
    shift = SLOT * ZS + 3
    before = jnp.where(me == 0, 0.0, pltpu.roll(other, shift, 2))
    source[0] = mine
    source[1] = jnp.where(slot, jnp.where(place < 3, before, pltpu.roll(mine, shift, 2)), 0.0)
    shift = SLOT * ZS + 5
    after = jnp.where(me == 0, pltpu.roll(other, shift, 2), 0.0)
    source[2] = jnp.where(slot, jnp.where(place < 5, pltpu.roll(mine, shift, 2), after), 0.0)


def next_x(v):
    return jnp.concatenate([v[1:], pltpu.roll(v[0:1], v.shape[1] - 1, 1)], 0)


def prev_x(v):
    return jnp.concatenate([pltpu.roll(v[-1:], 1, 1), v[:-1]], 0)


def lane_roll(v, shift):
    return pltpu.roll(v, shift % v.shape[2], 2)


def zeros(shape):
    return jnp.zeros(shape, jnp.float32)


def unfold(ref, fold):
    return jnp.stack([ref[pl.ds(j, TILE, stride=fold), :] for j in range(fold)])


def fold_back(ref, v):
    for j in range(v.shape[0]):
        ref[pl.ds(j, TILE, stride=v.shape[0]), :] = v[j]


def step_size(full):
    outside = (row_index(full) >= full[0] * TILE - REACH) & (lax.axis_index("xs") == 0)
    return jnp.where(outside, 0.0, time_step)


def evolve_strips(strips, y_halos, source, strip, edge_e, edge_h):
    me = lax.axis_index("ys")
    ring, width = strips.shape[2:]
    fold = ring // TILE
    full = (fold, TILE, width)
    for q in range(PAIRS):
        for r in range(fold):
            before = jnp.zeros((TILE, width), jnp.float32)
            after = jnp.zeros((TILE, width), jnp.float32)
            at = q * ring + r * TILE
            for k, y_ref in enumerate(y_halos):
                block = y_ref[at : at + TILE, :]
                is_next = me % 2 == k
                after = jnp.where(is_next, block, after)
                before = jnp.where(is_next, before, block)
            place = lanes_of(before.shape) % SLOT
            rows = slice(r * TILE, (r + 1) * TILE)
            for c in range(2 * q, min(2 * q + 2, PARTS)):
                b = c % 2
                lower = pltpu.roll(before, width - 4, 1) if b else before
                upper = pltpu.roll(after, 1 if b else 5, 1)
                strip[0, c, rows, :] = jnp.where(place < 3, lower, strips[0, c, rows, :])
                strip[1, c, rows, :] = jnp.where(place >= 5, upper, strips[1, c, rows, :])
    lane = lanes_of(full)
    place = lane % SLOT
    for side in (0, 1):
        ex, ey, ez, hx, hy, hz, co = [unfold(strip.at[side, c], fold) for c in range(PARTS)]
        dt = step_size(full)
        if not side:
            dt = jnp.where((place < 3) & (me == 0), 0.0, dt)
        for step in range(STEPS):

            def next_z(v):
                return jnp.where(lane < width - SLOT, lane_roll(v, -SLOT), 0.0)

            def prev_z(v):
                return jnp.where(lane >= SLOT, lane_roll(v, SLOT), 0.0)

            if side:
                edge_e[step] = jnp.where(place == 5, ex, lane_roll(ez, 1))
                if step + 1 == STEPS:
                    continue
            hx = hx - dt * (lane_roll(ez, -1) - ez - (next_z(ey) - ey))
            hy = hy - dt * (next_z(ex) - ex - (next_x(ez) - ez))
            hz = hz - dt * (next_x(ey) - ey - (lane_roll(ex, -1) - ex))
            if not side:
                edge_h[step] = jnp.where(place == 2, hz, lane_roll(hx, 1))
                if step + 1 == STEPS:
                    continue
            ex = ex + co * (hz - lane_roll(hz, 1) - (hy - prev_z(hy)))
            ey = ey + co * (hx - prev_z(hx) - (hz - prev_x(hz)))
            ez = ez + co * (hy - prev_x(hy) - (hx - lane_roll(hx, 1)) - source[1 + side])


def surface_steps(*refs, n_adj, n_rows, n_swaps):
    fields, permittivity, even, odd = refs[:4]
    strips, y_halos, given = refs[4], refs[5 : 5 + n_swaps], refs[5 + n_swaps]
    out, source, edge_e, edge_h, grid, coeffs, state, strip = refs[6 + n_swaps :]
    px = lax.axis_index("xs") % 2
    layers, cells_x, width = fields.shape[1:]
    ring = cells_x + TILE
    fold = ring // TILE
    full = (fold, TILE, width)
    lane = lanes_of(full)
    used = range(max(ZS - STEPS, 0), min(ZS + STEPS + 1, layers))

    for z in used:
        for c in range(PARTS):
            ref = grid.at[c, z] if c < 6 else coeffs.at[z]
            ref[0:cells_x, :] = fields[c, z] if c < 6 else time_step / permittivity[z]
            ref[cells_x:ring, :] = halo_tile(even, odd, px, c, z, layers)

    if n_adj:
        end = PARTS * (layers // 2) * TILE
        y_end = PAIRS * ring
        sets = [
            (given, 0, None),
            (even, end, px == 0),
            (odd, end, px == 1),
            (y_halos[0], y_end, None),
            (y_halos[0], y_end + n_rows, px == 0),
            (y_halos[0], y_end + 2 * n_rows, px == 1),
        ]
        gather_sources(sets, px, lax.axis_index("ys"), source, n_adj, cells_x)
    else:
        source[...] = given[...]
    evolve_strips(strips, y_halos, source, strip, edge_e, edge_h)

    dt = step_size(full)
    for step in range(STEPS):
        final = step + 1 == STEPS
        low, high = max(ZS - STEPS + step, 0), min(ZS + STEPS - 1 - step, layers - 1)

        def load(c, z):
            return state[c, z] if step else unfold(grid.at[c, z], fold)

        def store(c, z, v):
            if final:
                fold_back(grid.at[c, z], v)
            else:
                state[c, z] = v

        below = None
        ex, ey = load(0, low), load(1, low)
        for z in range(low, high + 1):
            ez, hx, hy, hz = [load(c, z) for c in range(2, 6)]
            if z + 1 < layers:
                ex_above, ey_above = load(0, z + 1), load(1, z + 1)
            else:
                ex_above, ey_above = jnp.zeros(full, jnp.float32), jnp.zeros(full, jnp.float32)
            edge = lane_roll(edge_e[step], width - 1 - (SLOT * z + 5))
            ex_y = jnp.where(lane == width - 1, edge, lane_roll(ex, -1))
            ez_y = lane_roll(jnp.where(lane == 0, edge, ez), -1)
            hx = hx - dt * (ez_y - ez - (ey_above - ey))
            hy = hy - dt * (ex_above - ex - (next_x(ez) - ez))
            hz = hz - dt * (next_x(ey) - ey - (ex_y - ex))
            for c, v in ((3, hx), (4, hy), (5, hz)):
                store(c, z, v)
            if z == 0 or below:
                if step:
                    co = coeffs[z, 0:ring, :].reshape(full)
                else:
                    co = unfold(coeffs.at[z], fold)
                    coeffs[z, 0:ring, :] = co.reshape(ring, width)
                hx_z = hx - below[0] if z else hx
                hy_z = hy - below[1] if z else hy
                edge = lane_roll(edge_h[step], width - 1 - (SLOT * z + 2))
                hx_y = jnp.where(lane == 0, edge, lane_roll(hx, 1))
                hz_y = lane_roll(jnp.where(lane == width - 1, edge, hz), 1)
                store(0, z, ex + co * (hz - hz_y - hy_z))
                store(1, z, ey + co * (hx_z - (hz - prev_x(hz))))
                change = hy - prev_x(hy) - (hx - hx_y)
                if z == ZS:
                    change = change - source[0]
                store(2, z, ez + co * change)
            below = (hx, hy)
            ex, ey = ex_above, ey_above
    for k, (c, sign) in enumerate(((4, -1.0), (3, 1.0), (1, 1.0), (0, -1.0))):
        out[:, k * width : (k + 1) * width] = sign * grid[c, ZS, 0:cells_x, :]


def take_steps(first, last, layers, refs, load, store, load_coeff, after_layer=None):
    source, edge_e, edge_h = refs
    full = source.shape[1:]
    width = full[2]
    lane = lanes_of(full)
    dt = step_size(full)
    for step in range(first, last):

        def advance_h(z):
            ex, ey, ez, hx, hy, hz = [load(step, c, z) for c in range(6)]
            edge = lane_roll(edge_e[step], 2 * width - 1 - (SLOT * z + 5))
            ex_y = jnp.where(lane == width - 1, edge, lane_roll(ex, -1))
            ez_y = lane_roll(jnp.where(lane == 0, edge, ez), -1)
            store(step, 3, z, hx - dt * (ez_y - ez - (load(step, 1, z + 1) - ey)))
            store(step, 4, z, hy - dt * (load(step, 0, z + 1) - ex - (next_x(ez) - ez)))
            store(step, 5, z, hz - dt * (next_x(ey) - ey - (ex_y - ex)))

        def advance_e(z):
            hx, hy, hz = [load(step + 1, c, z) for c in range(3, 6)]
            co = load_coeff(z)
            edge = lane_roll(edge_h[step], 2 * width - 1 - (SLOT * z + 2))
            hx_y = jnp.where(lane == 0, edge, lane_roll(hx, 1))
            hz_y = lane_roll(jnp.where(lane == width - 1, edge, hz), 1)
            change = hz - hz_y - (hy - load(step + 1, 4, z - 1))
            store(step, 0, z, load(step, 0, z) + co * change)
            change = hx - load(step + 1, 3, z - 1) - (hz - prev_x(hz))
            store(step, 1, z, load(step, 1, z) + co * change)
            change = hy - prev_x(hy) - (hx - hx_y) - jnp.where(z == ZS, source[0], 0.0)
            store(step, 2, z, load(step, 2, z) + co * change)
            if after_layer and step + 1 == last:
                after_layer(z)

        repeat(0, layers, advance_h, TOGETHER)
        repeat(0, layers, advance_e, TOGETHER)


def zero_outside(ref, layers):
    for c in (0, 1):
        ref[c, layers + 1] = zeros(ref.shape[2:])
        ref[c + 3, 0] = zeros(ref.shape[2:])


def first_step(*refs):
    fields, permittivity, even, odd, *carried = refs[:7]
    state, coeffs, grid, coeff_rows = refs[7:]
    px = lax.axis_index("xs") % 2
    layers, cells_x, width = fields.shape[1:]
    ring = cells_x + TILE
    fold = ring // TILE

    def build(z):
        for c in range(PARTS):
            ref = grid.at[c, z + 1] if c < 6 else coeff_rows.at[z]
            ref[0:cells_x, :] = fields[c, z] if c < 6 else time_step / permittivity[z]
            ref[cells_x:ring, :] = halo_tile(even, odd, px, c, z, layers)
        coeffs[z] = unfold(coeff_rows.at[z], fold)

    repeat(0, layers, build, TOGETHER // 2)
    for c in (0, 1):
        grid[c, layers + 1] = zeros((ring, width))
    zero_outside(state, layers)

    def load(step, c, z):
        return state[c, z + 1] if step else unfold(grid.at[c, z + 1], fold)

    def store(step, c, z, v):
        state[c, z + 1] = v

    take_steps(0, 1, layers, carried, load, store, lambda z: coeffs[z])


def later_steps(*refs):
    before, coeffs, *carried = refs[:5]
    out, state, grid, sems = refs[5:]
    layers, cells_x = out.shape[1:3]

    def copy_out(z):
        done = grid.at[:, z, pl.ds(0, cells_x), :]
        return pltpu.make_async_copy(done, out.at[:, z], sems.at[z])

    zero_outside(state, layers)

    def load(step, c, z):
        return (before if step == 1 else state)[c, z + 1]

    def store(step, c, z, v):
        if step + 1 < STEPS or c >= 3:
            state[c, z + 1] = v
        if step + 1 == STEPS:
            fold_back(grid.at[c, z], v)

    take_steps(
        1,
        STEPS,
        layers,
        carried,
        lambda step, c, z: load(1 if step == 1 else 2, c, z),
        store,
        lambda z: coeffs[z],
        lambda z: copy_out(z).start(),
    )
    repeat(0, layers, lambda z: copy_out(z).wait())


def multiply(weights, *refs, n_tiles):
    tiles, parts = refs[:n_tiles], refs[n_tiles:]
    total = jnp.dot(
        weights[...],
        jnp.concatenate([tile[...] for tile in tiles], 0),
        precision=lax.Precision.HIGHEST,
        preferred_element_type=jnp.float32,
    )
    rows = parts[0].shape[0]
    for k, part in enumerate(parts):
        part[...] = total[k * rows : (k + 1) * rows]


def add_parts(*refs):
    parts, out = refs[:-1], refs[-1]
    total = parts[0][...]
    for part in parts[1:]:
        total = total + part[...]
    width = out.shape[2]
    for k in range(out.shape[1]):
        out[:, k, :] = total[:, k * width : (k + 1) * width]


def shape_of(*dims):
    return jax.ShapeDtypeStruct(dims, jnp.float32)


def far_field_weights(angle_wave, xs_size, cells_x, near):
    me = lax.axis_index("xs")
    per_block = angle_wave.shape[0] // xs_size
    far = xs_size // near
    bits = far.bit_length() - 1
    view = angle_wave.reshape(far, near, per_block)
    pick = jnp.arange(near, dtype=jnp.int32)[None, :, None] == me % near
    view = jnp.sum(jnp.where(pick, view, 0), axis=1).reshape((2,) * bits + (per_block,))
    for k in range(bits):
        bit = (me // near >> (bits - 1 - k)) & 1
        view = jnp.where(bit == 1, jnp.flip(view, k), view)
    angles = view.reshape(-1)
    owners = me ^ jnp.arange(near, dtype=jnp.int32)
    within = jnp.arange(cells_x, dtype=jnp.int32)
    positions = X0 + (owners[:, None] * cells_x + within[None, :]).reshape(-1)
    phase = angles[:, None] * positions[None, :] % GRID_X
    angle = phase.astype(jnp.float32) * (2.0 * math.pi / GRID_X)
    scale = 1.0 / math.sqrt(cells_x * xs_size)
    both = jnp.stack([jnp.cos(angle) * scale, -jnp.sin(angle) * scale], axis=1)
    return both.reshape(-1, near * cells_x)


def far_field_exchange(tile, angle_wave, xs_size, beside, finish):
    cells_x, columns = tile.shape
    near = 4
    weights = far_field_weights(angle_wave, xs_size, cells_x, near)

    def across(block, mask):
        return lax.ppermute(block, "xs", [(i, i ^ mask) for i in range(xs_size)])

    third = across(tile, 2)
    second = across(tile, 1)
    third, beside = lax.optimization_barrier((third, beside))
    fourth = across(third, 1)
    far = xs_size // near
    rows = weights.shape[0] // far
    parts = pl.pallas_call(
        functools.partial(multiply, n_tiles=near),
        out_shape=(shape_of(rows, columns),) * far,
        in_specs=[VMEM] * (near + 1),
        out_specs=(VMEM,) * far,
        compiler_params=PARAMS,
        name="partial_spectrum",
    )(weights, tile, second, third, fourth)
    arrived = [across(parts[k], k * near) for k in range(far - 1, 0, -1)]
    finished = finish(beside)
    far_field = pl.pallas_call(
        add_parts,
        out_shape=shape_of(rows, 4, columns // 4),
        in_specs=[VMEM] * far,
        out_specs=VMEM,
        compiler_params=PARAMS,
        name="add_arrived",
    )(parts[0], *arrived)
    return far_field, finished


def gathered_sources(adj_values, adj_owner, adj_row, cells_x, cells_y):
    groups = lax.axis_size("ys")
    owners = adj_owner[:, 0]
    hits = (owners[:, None] == jnp.arange(groups, dtype=jnp.int32)[None, :]).astype(jnp.int32)
    before = jnp.cumsum(hits, axis=0) - hits
    slot_index = owners * CAP + jnp.sum(before * hits, axis=1)
    placing = (jnp.arange(groups * CAP, dtype=jnp.int32)[:, None] == slot_index[None, :]).astype(
        jnp.float32
    )
    rows = jnp.broadcast_to(adj_row.astype(jnp.float32)[:, None], (adj_row.shape[0], 1))
    outgoing = jnp.dot(
        placing, jnp.concatenate([adj_values, rows], 1), precision=lax.Precision.HIGHEST
    ).reshape(groups, CAP, cells_y + 1)
    incoming = lax.all_to_all(outgoing, "ys", split_axis=0, concat_axis=0, tiled=True)
    incoming = incoming.reshape(groups * CAP, cells_y + 1)
    landing = (
        jnp.arange(cells_x, dtype=jnp.float32)[:, None] == incoming[:, cells_y][None, :]
    ).astype(jnp.float32)
    current = jnp.dot(landing, incoming[:, :cells_y], precision=lax.Precision.HIGHEST)

    def shifted(block, axis, distance):
        size = lax.axis_size(axis)
        route = [(i, i + distance) for i in range(size) if 0 <= i + distance < size]
        return lax.ppermute(block, axis, route)

    after = shifted(current[:REACH], "xs", -1)
    before = shifted(current[-REACH:], "xs", 1)
    ringed = jnp.concatenate([current, after, before], 0)
    right = shifted(ringed[:, :3], "ys", -1)
    left = shifted(ringed[:, -3:], "ys", 1)
    start, end = SLOT * ZS, cells_y - SLOT * (ZS + 1)
    first = jnp.pad(jnp.concatenate([left, ringed[:, :5]], 1), ((0, 0), (start, end)))
    second = jnp.pad(jnp.concatenate([ringed[:, -5:], right], 1), ((0, 0), (start, end)))
    folded = jnp.stack([ringed, first, second]).reshape(3, TILE, -1, cells_y)
    return folded.transpose(0, 2, 1, 3)


def on_device(fields, permittivity, adj_values, adj_owner, adj_row, angle_wave):
    layers, cells_x, cells_y = fields.shape[1:]
    xs_size, ys_size = lax.axis_size("xs"), lax.axis_size("ys")
    raw = ys_size == 2
    n_adj = adj_values.shape[0] if raw else 0
    n_rows = -(-3 * n_adj // TILE) * TILE
    ring = cells_x + TILE
    x_rows = PARTS * (layers // 2) * TILE + n_rows
    y_rows = PAIRS * ring + 3 * n_rows

    extra = (adj_values, adj_row, adj_owner.reshape(-1)) if raw else ()
    packed = pl.pallas_call(
        functools.partial(pack_x, n_adj=n_adj),
        out_shape=(shape_of(x_rows, cells_y),) * 2 + ((shape_of(n_rows, cells_y),) if raw else ()),
        in_specs=[ANY] * (2 + len(extra)),
        out_specs=(VMEM,) * (3 if raw else 2),
        scratch_shapes=[
            pltpu.VMEM((2, 6, layers, TILE, cells_y), jnp.float32),
            pltpu.VMEM((2, layers, TILE, cells_y), jnp.float32),
        ]
        + ([pltpu.SMEM((n_adj,), jnp.int32)] * 2 if raw else [])
        + [pltpu.SemaphoreType.DMA((4 + len(extra),))],
        compiler_params=PARAMS,
        name="pack_x_edges",
    )(*[pltpu.with_memory_space_constraint(x, pltpu.HBM) for x in (fields, permittivity, *extra)])
    blocks = packed[2:]
    x_even, x_odd = swaps(xs_size)
    from_even = lax.ppermute(packed[0], "xs", x_even)
    from_odd = lax.ppermute(packed[1], "xs", x_odd)

    y_swaps = swaps(ys_size)
    strips_shape = shape_of(2, PARTS, ring, cells_y)
    made = (strips_shape,) + (shape_of(y_rows, cells_y),) * len(y_swaps)
    packed = pl.pallas_call(
        pack_y,
        out_shape=made,
        in_specs=[VMEM] * 2,
        out_specs=(VMEM,) * len(made),
        compiler_params=PARAMS,
        name="pack_y_edges",
    )(fields, permittivity)
    strips, *to_y = pl.pallas_call(
        functools.partial(pack_corners, layers=layers, n_rows=n_rows, n_swaps=len(y_swaps)),
        out_shape=made,
        in_specs=[VMEM] * (len(made) + 2 + len(blocks)),
        out_specs=(VMEM,) * len(made),
        input_output_aliases={k: k for k in range(len(made))},
        compiler_params=PARAMS,
        name="pack_corners",
    )(*packed, from_even, from_odd, *blocks)
    y_halos = [lax.ppermute(message, "ys", route) for message, route in zip(to_y, y_swaps)]

    if raw:
        sources = blocks
    else:
        sources = (gathered_sources(adj_values, adj_owner, adj_row, cells_x, cells_y),)

    fold = ring // TILE
    folded = (fold, TILE, cells_y)
    operands = (fields, permittivity, from_even, from_odd, strips, *y_halos, *sources)
    tile, *carried = pl.pallas_call(
        functools.partial(surface_steps, n_adj=n_adj, n_rows=n_rows, n_swaps=len(y_swaps)),
        out_shape=(
            shape_of(cells_x, 4 * cells_y),
            shape_of(3, *folded),
            shape_of(STEPS, *folded),
            shape_of(STEPS, *folded),
        ),
        in_specs=[VMEM] * len(operands),
        out_specs=(VMEM,) * 4,
        scratch_shapes=[
            pltpu.VMEM((6, layers, ring, cells_y), jnp.float32),
            pltpu.VMEM((layers, ring, cells_y), jnp.float32),
            pltpu.VMEM((6, layers, *folded), jnp.float32),
            pltpu.VMEM((2, PARTS, ring, cells_y), jnp.float32),
        ],
        compiler_params=PARAMS,
        name="surface_steps",
    )(*operands)

    state_shape = (6, layers + 2, *folded)
    operands = (fields, permittivity, from_even, from_odd, *carried)
    stepped = pl.pallas_call(
        first_step,
        out_shape=(shape_of(*state_shape), shape_of(layers, *folded)),
        in_specs=[VMEM] * len(operands),
        out_specs=(VMEM, VMEM),
        scratch_shapes=[
            pltpu.VMEM((6, layers + 2, ring, cells_y), jnp.float32),
            pltpu.VMEM((layers, ring, cells_y), jnp.float32),
        ],
        compiler_params=PARAMS,
        name="first_step",
    )(*operands)

    def finish(stepped):
        return pl.pallas_call(
            later_steps,
            out_shape=shape_of(*fields.shape),
            in_specs=[VMEM] * 5,
            out_specs=ANY,
            scratch_shapes=[
                pltpu.VMEM(state_shape, jnp.float32),
                pltpu.VMEM((6, layers, ring, cells_y), jnp.float32),
                pltpu.SemaphoreType.DMA((layers,)),
            ],
            compiler_params=PARAMS,
            name="later_steps",
        )(*stepped, *carried)

    far, new_fields = far_field_exchange(tile, angle_wave, xs_size, stepped, finish)
    per_block = angle_wave.shape[0] // xs_size
    return (new_fields, far.reshape(per_block, 2, 4, cells_y))


def solution(mesh):
    placed = (
        P(None, None, "xs", "ys"),
        P(None, "xs", "ys"),
        P(("xs", "ys"), None),
        P(("xs", "ys"), None),
        P(("xs", "ys")),
        P(),
    )
    return jax.shard_map(
        on_device,
        mesh=mesh,
        in_specs=placed,
        out_specs=(P(None, None, "xs", "ys"), P("xs", None, None, "ys")),
        check_vma=False,
    )
```

time: 38.5 us -> 34.5 us (0.90)
  Pallas kernels: 13.2 us -> 10.3 us
  starting transfers between devices: 18 us -> 17.3 us
    pallas_call x3 -> x4, Pallas kernels: 10.6 us -> 7.47 us  [the longest x1 2.79 us: finish(): pl.pallas_call(later_steps, out_shape=shape_of(*fields.shape), in_specs=[...]
    ppermute x6, starting transfers between devices: 14.3 us -> 13.6 us  [across(): return lax.ppermute(block, 'xs', [(i, i ^ mask) for i in range(xs_size)])]
  transfers between devices with their start and end apart: 9 -> 9, of which waited for: 3 -> 4; matrix products, arithmetic and copies ran while one was open for 2% -> 2% of each run, Pallas kernels for 23% -> 18%
where the time goes in v3:
time: 34.5 us; the launch traced here: 34.4 us
  starting transfers between devices  17.3 us (50%)
  Pallas kernels  10.3 us (30%)
  waiting for transfers between devices  5.33 us (15%)
  between operations  0.82 us (2%)
    ppermute x6, starting transfers between devices, across(): return lax.ppermute(block, 'xs', [(i, i ^ mask) for i in range(xs_size)])  13.6 us
    ppermute x6, waiting for transfers between devices, across(): return lax.ppermute(block, 'xs', [(i, i ^ mask) for i in range(xs_size)])  2.88 us
    pallas_call x1, Pallas kernels, finish(): pl.pallas_call(later_steps, out_shape=shape_of(*fields.shape), in_specs=[...  2.79 us
    ppermute x1, starting transfers between devices, on_device(): lax.ppermute(message, 'ys', route)  2.52 us
    ppermute x1, waiting for transfers between devices, on_device(): lax.ppermute(message, 'ys', route)  2.45 us
    pallas_call x1, Pallas kernels, on_device(): pl.pallas_call(pack_y, out_shape=made, in_specs=[VMEM] * 2, out_specs=(VM...  2.02 us
    pallas_call x1, Pallas kernels, on_device(): pl.pallas_call(functools.partial(surface_steps, n_adj=n_adj, n_rows=n_row...  1.45 us
    pallas_call x1, Pallas kernels, on_device(): pl.pallas_call(functools.partial(pack_x, n_adj=n_adj), out_shape=(shape_o...  1.44 us
  transfers between devices with their start and end apart: 9, of which 4 were waited for; matrix products, arithmetic and copies ran while one was open for 2% of the time, Pallas kernels for 18%

profile of v3, /device:TPU:0, one launch (start us, length us, event | category | flops | bytes accessed | tf_op | source)
XLA Modules:
  0.0 34.4 jit_solution(14154588818572868057)
XLA Ops:
  0.6 0.0 copy-start
  0.6 0.0 copy-start.1
  0.7 0.0 copy-start.2
  0.7 1.4 %pack_x_edges.1 = (f32[464,128]{1,0:T(8,128)S(1)}, f32[464,128]{1,0:T(8,128)S(1)}, f32[16,128]{1,0:T(8,128)S(1)}) custom-call(f32[6,16,32,128]{3,2,1,0:T(8,128)} %refs_0_.5, f32[16,32,128]{2,1,0:T(8,128)} %refs_1_.5, f32[4,128]{1,0:T(4,128)} %refs_2_.1, s32[4]{0:T(128)} %refs_3_.1, s32[4]{0:T(128)} %bitcast.8), custom_call_target="tpu_custom_call" | custom-call | tf_op jit(solution)/shard_map/pack_x_edges/pallas_call | solution.py:642
  2.1 0.5 %collective-permute-start = (f32[464,128]{1,0:T(8,128)S(1)}, f32[464,128]{1,0:T(8,128)S(1)}, u32[]{:S(2)}, u32[]{:S(2)}) collective-permute-start(f32[464,128]{1,0:T(8,128)S(1)} %get-tuple-element.22), channel_id=1, source_target_pairs={{0,2},{4,6},{8,10},{12,14},{16,18},{20,22},{24,26},{28,30},{2,0},{... | collective-permute-start | bytes 712712 | tf_op jit(solution)/shard_map/ppermute | solution.py:658
  2.6 0.7 %collective-permute-start.1 = (f32[464,128]{1,0:T(8,128)S(1)}, f32[464,128]{1,0:T(8,128)S(1)}, u32[]{:S(2)}, u32[]{:S(2)}) collective-permute-start(f32[464,128]{1,0:T(8,128)S(1)} %get-tuple-element.23), channel_id=1, source_target_pairs={{2,4},{6,8},{10,12},{14,16},{18,20},{22,24},{26,28},{4,2},{8,6},{1... | collective-permute-start | bytes 712712 | tf_op jit(solution)/shard_map/ppermute | solution.py:659
  3.3 0.0 copy-done.2
  3.3 0.1 reshape.182
  3.4 0.1 select_reduce_fusion
  3.5 0.0 copy-done
  3.6 0.0 copy-done.1
  3.6 2.0 %pack_y_edges.1 = (f32[2,7,40,128]{3,2,1,0:T(8,128)S(1)}, f32[208,128]{1,0:T(8,128)S(1)}) custom-call(f32[6,16,32,128]{3,2,1,0:T(8,128)S(1)} %copy-done, f32[16,32,128]{2,1,0:T(8,128)S(1)} %copy-done.1), custom_call_target="tpu_custom_call" | custom-call | tf_op jit(solution)/shard_map/pack_y_edges/pallas_call | solution.py:664
  5.6 0.0 collective-permute-done.refs_2_
  5.6 0.0 collective-permute-done.1.refs_3_
  5.6 0.5 %pack_corners.1 = (f32[2,7,40,128]{3,2,1,0:T(8,128)S(1)}, f32[208,128]{1,0:T(8,128)S(1)}) custom-call(f32[2,7,40,128]{3,2,1,0:T(8,128)S(1)} %get-tuple-element.24.refs_0_, f32[208,128]{1,0:T(8,128)S(1)} %get-tuple-element.25.refs_1_, f32[464,128]{1,0:T(8,128)S(1)} %collective-permute-done.refs_2_, ...), custom_call_target="tpu_custom_call", output_to_operand_aliasing={{0}: (0, {}), {1}: (1, {})} | custom-call | tf_op jit(solution)/shard_map/pack_corners/pallas_call | solution.py:672
  6.1 2.5 %collective-permute-start.2 = (f32[208,128]{1,0:T(8,128)S(1)}, f32[208,128]{1,0:T(8,128)S(1)}, u32[]{:S(2)}, u32[]{:S(2)}) collective-permute-start(f32[208,128]{1,0:T(8,128)S(1)} %get-tuple-element.28), channel_id=1, source_target_pairs={{0,1},{1,0},{2,3},{3,2},{4,5},{5,4},{6,7},{7,6},{8,9},{9,8},{10,11... | collective-permute-start | bytes 319496 | tf_op jit(solution)/shard_map/ppermute | solution.py:681
  8.7 0.1 add_add_fusion
  8.7 0.1 mul.71
  8.8 0.1 add.60
  8.9 2.4 %collective-permute-done.2.refs_5_ = f32[208,128]{1,0:T(8,128)S(1)} collective-permute-done((f32[208,128]{1,0:T(8,128)S(1)}, f32[208,128]{1,0:T(8,128)S(1)}, u32[]{:S(2)}, u32[]{:S(2)}) %collective-permute-start.2) | collective-permute-done | bytes 106528 | tf_op jit(solution)/shard_map/ppermute | solution.py:681
  11.3 1.4 %surface_steps.1 = (f32[32,512]{1,0:T(8,128)S(1)}, f32[3,5,8,128]{3,2,1,0:T(8,128)S(1)}, f32[3,5,8,128]{3,2,1,0:T(8,128)S(1)}, f32[3,5,8,128]{3,2,1,0:T(8,128)S(1)}) custom-call(f32[6,16,32,128]{3,2,1,0:T(8,128)S(1)} %copy-done, f32[16,32,128]{2,1,0:T(8,128)S(1)} %copy-done.1, f32[464,128]{1,0:T(8,128)S(1)} %collective-permute-done.refs_2_, ...), custom_call_target="tpu_custom_call" | custom-call | tf_op jit(solution)/shard_map/surface_steps/pallas_call | solution.py:691
  12.8 9.0 %collective-permute-start.3 = (f32[32,512]{1,0:T(8,128)S(1)}, f32[32,512]{1,0:T(8,128)S(1)}, u32[]{:S(2)}, u32[]{:S(2)}) collective-permute-start(f32[32,512]{1,0:T(8,128)S(1)} %get-tuple-element.29.refs_0_), channel_id=1, source_target_pairs={{0,4},{2,6},{4,0},{6,2},{8,12},{10,14},{12,8},{14,10},{16,20},{18,... | collective-permute-start | bytes 196616 | tf_op jit(solution)/shard_map/ppermute | solution.py:565
  21.8 0.2 cosine_multiply_fusion
  22.0 0.1 collective-permute-start.4
  22.1 1.2 %first_step.1 = (f32[6,18,5,8,128]{4,3,2,1,0:T(8,128)S(1)}, f32[16,5,8,128]{3,2,1,0:T(8,128)S(1)}) custom-call(f32[6,16,32,128]{3,2,1,0:T(8,128)S(1)} %copy-done, f32[16,32,128]{2,1,0:T(8,128)S(1)} %copy-done.1, f32[464,128]{1,0:T(8,128)S(1)} %collective-permute-done.refs_2_, f32[464,128]{1,0:T(8,128)S(1)} %collective-permute-done.1.refs_3_, ...), custom_call_target="tpu_custom_call" | custom-call | tf_op jit(solution)/shard_map/first_step/pallas_call | solution.py:713
  23.3 0.8 %collective-permute-done.3.refs_2_ = f32[32,512]{1,0:T(8,128)S(1)} collective-permute-done((f32[32,512]{1,0:T(8,128)S(1)}, f32[32,512]{1,0:T(8,128)S(1)}, u32[]{:S(2)}, u32[]{:S(2)}) %collective-permute-start.3) | collective-permute-done | bytes 65568 | tf_op jit(solution)/shard_map/ppermute | solution.py:565
  24.1 0.0 collective-permute-start.5
  24.1 0.0 collective-permute-done.4.refs_1_
  24.1 1.2 %collective-permute-done.5.refs_3_ = f32[32,512]{1,0:T(8,128)S(1)} collective-permute-done((f32[32,512]{1,0:T(8,128)S(1)}, f32[32,512]{1,0:T(8,128)S(1)}, u32[]{:S(2)}, u32[]{:S(2)}) %collective-permute-start.5) | collective-permute-done | bytes 65568 | tf_op jit(solution)/shard_map/ppermute | solution.py:565
  25.3 0.3 partial_spectrum.1
  25.6 3.3 %collective-permute-start.6 = (f32[16,512]{1,0:T(8,128)S(1)}, f32[16,512]{1,0:T(8,128)S(1)}, u32[]{:S(2)}, u32[]{:S(2)}) collective-permute-start(f32[16,512]{1,0:T(8,128)S(1)} %get-tuple-element.39), channel_id=1, source_target_pairs={{0,24},{2,26},{4,28},{6,30},{8,16},{10,18},{12,20},{14,22},{16,8},... | collective-permute-start | bytes 98312 | tf_op jit(solution)/shard_map/ppermute | solution.py:565
  28.9 0.0 collective-permute-start.7
  28.9 1.1 %collective-permute-start.8 = (f32[16,512]{1,0:T(8,128)S(1)}, f32[16,512]{1,0:T(8,128)S(1)}, u32[]{:S(2)}, u32[]{:S(2)}) collective-permute-start(f32[16,512]{1,0:T(8,128)S(1)} %get-tuple-element.41), channel_id=1, source_target_pairs={{0,8},{2,10},{4,12},{6,14},{8,0},{10,2},{12,4},{14,6},{16,24},{18,... | collective-permute-start | bytes 98312 | tf_op jit(solution)/shard_map/ppermute | solution.py:565
  30.1 2.8 %later_steps.1 = f32[6,16,32,128]{3,2,1,0:T(8,128)} custom-call(f32[6,18,5,8,128]{4,3,2,1,0:T(8,128)S(1)} %get-tuple-element.35.refs_0_, f32[16,5,8,128]{3,2,1,0:T(8,128)S(1)} %get-tuple-element.36.refs_1_, f32[3,5,8,128]{3,2,1,0:T(8,128)S(1)} %get-tuple-element.30.refs_4_.refs_2_, f32[3,5,8,128]{3,2,1,0:T(8,128)S(1)} %get-tuple-element.31.refs_5_.refs_3_, ...), custom_call_target="tpu_custom_call" | custom-call | tf_op jit(solution)/shard_map/later_steps/pallas_call | solution.py:727
  32.9 0.0 collective-permute-done.6.refs_1_
  32.9 0.9 %collective-permute-done.7.refs_2_ = f32[16,512]{1,0:T(8,128)S(1)} collective-permute-done((f32[16,512]{1,0:T(8,128)S(1)}, f32[16,512]{1,0:T(8,128)S(1)}, u32[]{:S(2)}, u32[]{:S(2)}) %collective-permute-start.7) | collective-permute-done | bytes 32800 | tf_op jit(solution)/shard_map/ppermute | solution.py:565
  33.7 0.0 collective-permute-done.8.refs_3_
  33.8 0.6 %add_arrived.1 = f32[16,4,128]{2,1,0:T(4,128)} custom-call(f32[16,512]{1,0:T(8,128)S(1)} %get-tuple-element.38.refs_0_, f32[16,512]{1,0:T(8,128)S(1)} %collective-permute-done.6.refs_1_, f32[16,512]{1,0:T(8,128)S(1)} %collective-permute-done.7.refs_2_, f32[16,512]{1,0:T(8,128)S(1)} %collective-permute-done.8.refs_3_), custom_call_target="tpu_custom_call" | custom-call | tf_op jit(solution)/shard_map/add_arrived/pallas_call | solution.py:583
  (7 shorter events, 0.1 us)
Async XLA Ops:
  0.6 2.9 %copy-start = (f32[6,16,32,128]{3,2,1,0:T(8,128)S(1)}, f32[6,16,32,128]{3,2,1,0:T(8,128)}, u32[]{:S(2)}) copy-start(f32[6,16,32,128]{3,2,1,0:T(8,128)} %refs_0_.5) | copy-start | bytes 4718596
  0.6 2.9 %copy-start.1 = (f32[16,32,128]{2,1,0:T(8,128)S(1)}, f32[16,32,128]{2,1,0:T(8,128)}, u32[]{:S(2)}) copy-start(f32[16,32,128]{2,1,0:T(8,128)} %refs_1_.5) | copy-start | bytes 786436
  0.7 2.7 %copy-start.2 = (s32[128]{0:T(128)S(1)}, s32[128]{0:T(128)}, u32[]{:S(2)}) copy-start(s32[128]{0:T(128)} %param.11) | copy-start | bytes 1540
  2.1 3.5 %collective-permute-start = (f32[464,128]{1,0:T(8,128)S(1)}, f32[464,128]{1,0:T(8,128)S(1)}, u32[]{:S(2)}, u32[]{:S(2)}) collective-permute-start(f32[464,128]{1,0:T(8,128)S(1)} %get-tuple-element.22), channel_id=1, source_target_pairs={{0,2},{4,6},{8,10},{12,14},{16,18},{20,22},{24,26},{28,30},{2,0},{... | collective-permute-start | bytes 712712 | tf_op jit(solution)/shard_map/ppermute | solution.py:658
  2.6 3.0 %collective-permute-start.1 = (f32[464,128]{1,0:T(8,128)S(1)}, f32[464,128]{1,0:T(8,128)S(1)}, u32[]{:S(2)}, u32[]{:S(2)}) collective-permute-start(f32[464,128]{1,0:T(8,128)S(1)} %get-tuple-element.23), channel_id=1, source_target_pairs={{2,4},{6,8},{10,12},{14,16},{18,20},{22,24},{26,28},{4,2},{8,6},{1... | collective-permute-start | bytes 712712 | tf_op jit(solution)/shard_map/ppermute | solution.py:659
  6.1 5.2 %collective-permute-start.2 = (f32[208,128]{1,0:T(8,128)S(1)}, f32[208,128]{1,0:T(8,128)S(1)}, u32[]{:S(2)}, u32[]{:S(2)}) collective-permute-start(f32[208,128]{1,0:T(8,128)S(1)} %get-tuple-element.28), channel_id=1, source_target_pairs={{0,1},{1,0},{2,3},{3,2},{4,5},{5,4},{6,7},{7,6},{8,9},{9,8},{10,11... | collective-permute-start | bytes 319496 | tf_op jit(solution)/shard_map/ppermute | solution.py:681
  12.8 11.3 %collective-permute-start.3 = (f32[32,512]{1,0:T(8,128)S(1)}, f32[32,512]{1,0:T(8,128)S(1)}, u32[]{:S(2)}, u32[]{:S(2)}) collective-permute-start(f32[32,512]{1,0:T(8,128)S(1)} %get-tuple-element.29.refs_0_), channel_id=1, source_target_pairs={{0,4},{2,6},{4,0},{6,2},{8,12},{10,14},{12,8},{14,10},{16,20},{18,... | collective-permute-start | bytes 196616 | tf_op jit(solution)/shard_map/ppermute | solution.py:565
  22.0 2.1 %collective-permute-start.4 = (f32[32,512]{1,0:T(8,128)S(1)}, f32[32,512]{1,0:T(8,128)S(1)}, u32[]{:S(2)}, u32[]{:S(2)}) collective-permute-start(f32[32,512]{1,0:T(8,128)S(1)} %get-tuple-element.29.refs_0_), channel_id=1, source_target_pairs={{0,2},{2,0},{4,6},{6,4},{8,10},{10,8},{12,14},{14,12},{16,18},{18,... | collective-permute-start | bytes 196616 | tf_op jit(solution)/shard_map/ppermute | solution.py:565
  24.1 1.3 %collective-permute-start.5 = (f32[32,512]{1,0:T(8,128)S(1)}, f32[32,512]{1,0:T(8,128)S(1)}, u32[]{:S(2)}, u32[]{:S(2)}) collective-permute-start(f32[32,512]{1,0:T(8,128)S(1)} %collective-permute-done.3.refs_2_), channel_id=1, source_target_pairs={{0,2},{2,0},{4,6},{6,4},{8,10},{10,8},{12,14},{14,12},{16,18},{18,... | collective-permute-start | bytes 196616 | tf_op jit(solution)/shard_map/ppermute | solution.py:565
  25.6 7.3 %collective-permute-start.6 = (f32[16,512]{1,0:T(8,128)S(1)}, f32[16,512]{1,0:T(8,128)S(1)}, u32[]{:S(2)}, u32[]{:S(2)}) collective-permute-start(f32[16,512]{1,0:T(8,128)S(1)} %get-tuple-element.39), channel_id=1, source_target_pairs={{0,24},{2,26},{4,28},{6,30},{8,16},{10,18},{12,20},{14,22},{16,8},... | collective-permute-start | bytes 98312 | tf_op jit(solution)/shard_map/ppermute | solution.py:565
  28.9 4.8 %collective-permute-start.7 = (f32[16,512]{1,0:T(8,128)S(1)}, f32[16,512]{1,0:T(8,128)S(1)}, u32[]{:S(2)}, u32[]{:S(2)}) collective-permute-start(f32[16,512]{1,0:T(8,128)S(1)} %get-tuple-element.40), channel_id=1, source_target_pairs={{0,16},{2,18},{4,20},{6,22},{8,24},{10,26},{12,28},{14,30},{16,0},... | collective-permute-start | bytes 98312 | tf_op jit(solution)/shard_map/ppermute | solution.py:565
  28.9 4.8 %collective-permute-start.8 = (f32[16,512]{1,0:T(8,128)S(1)}, f32[16,512]{1,0:T(8,128)S(1)}, u32[]{:S(2)}, u32[]{:S(2)}) collective-permute-start(f32[16,512]{1,0:T(8,128)S(1)} %get-tuple-element.41), channel_id=1, source_target_pairs={{0,8},{2,10},{4,12},{6,14},{8,0},{10,2},{12,4},{14,6},{16,24},{18,... | collective-permute-start | bytes 98312 | tf_op jit(solution)/shard_map/ppermute | solution.py:565

commit v4 on v3

--- a/solution.py
+++ b/solution.py
@@ -20,7 +20,8 @@
 REACH = 4
 SLOT = 8
 PARTS = 7
-PAIRS = (PARTS + 1) // 2
+X_GROUPS = ((0, 1, 3), (2, 4, 6), (5,))
+Y_GROUPS = ((0, 2, 4), (1, 3, 6), (5,))
 TOGETHER = 8
 
 VMEM = pl.BlockSpec(memory_space=pltpu.VMEM)
@@ -45,17 +46,34 @@
     return found
 
 
+def x_message_rows(layers):
+    return (2 * layers + layers // 2) * TILE
+
+
 def halo_tile(even, odd, px, c, z, layers):
-    at = pl.ds(pl.multiple_of((c * (layers // 2) + z // 2) * TILE, TILE), TILE)
+    group = [c in parts for parts in X_GROUPS].index(True)
+    slot = X_GROUPS[group].index(c)
+    tile = 2 * z + group if group < 2 else 2 * layers + z // 2
+    at = pl.ds(tile * TILE if isinstance(z, int) else pl.multiple_of(tile * TILE, TILE), TILE)
     from_even, from_odd = even[at, :], odd[at, :]
-    same = px == z % 2
-    turned_even, turned_odd = pltpu.roll(from_even, REACH, 0), pltpu.roll(from_odd, REACH, 0)
-    odd_half = (rows_of(from_even.shape) >= REACH) == (px == 0)
-    return jnp.where(
-        same,
-        jnp.where(odd_half, turned_odd, from_even),
-        jnp.where(odd_half, from_odd, turned_even),
-    )
+    after = jnp.where(px == 0, from_even, from_odd)
+    before = jnp.where(px == 0, from_odd, from_even)
+    lower = rows_of(after.shape) < REACH
+
+    def placed(first, count):
+        back = (TILE - first) % TILE
+        to_end = (TILE - count - first) % TILE
+        return jnp.where(
+            lower,
+            pltpu.roll(after, back, 0) if back else after,
+            pltpu.roll(before, to_end, 0) if to_end else before,
+        )
+
+    if group < 2:
+        return placed(3 * slot, 3 if slot < 2 else 2)
+    if isinstance(z, int):
+        return placed(4 * (z % 2), 3)
+    return jnp.where(z % 2 == 0, placed(0, 3), placed(4, 3))
 
 
 def repeat(first, last, body, together=1):
@@ -99,20 +117,32 @@
         copy.start()
     for copy in copies:
         copy.wait()
-    for c in range(PARTS):
-        for pair in range(layers // 2):
-            if c < 6:
-                lo = [edges[0, c, 2 * pair + k] for k in (0, 1)]
-                hi = [edges[1, c, 2 * pair + k] for k in (0, 1)]
-            else:
-                lo = [time_step / edge_perm[0, 2 * pair + k] for k in (0, 1)]
-                hi = [time_step / edge_perm[1, 2 * pair + k] for k in (0, 1)]
-            upper = rows_of(lo[0].shape) >= REACH
-            first = jnp.where(upper, pltpu.roll(lo[1], REACH, 0), lo[0])
-            last = jnp.where(upper, hi[1], pltpu.roll(hi[0], REACH, 0))
-            at = pl.ds((c * (layers // 2) + pair) * TILE, TILE)
-            to_even[at, :] = jnp.where(px == 0, last, first)
-            to_odd[at, :] = jnp.where(px == 0, first, last)
+
+    def both(c, z):
+        if c < 6:
+            return edges[0, c, z], edges[1, c, z]
+        return time_step / edge_perm[0, z], time_step / edge_perm[1, z]
+
+    def send(tile, first, last):
+        at = slice(tile * TILE, (tile + 1) * TILE)
+        to_even[at, :] = jnp.where(px == 0, last, first)
+        to_odd[at, :] = jnp.where(px == 0, first, last)
+
+    def turn(v, shift):
+        return pltpu.roll(v, shift, 0)
+
+    row = rows_of((TILE, fields.shape[3]))
+    for z in range(layers):
+        for g in range(2):
+            (lo0, hi0), (lo1, hi1), (lo2, hi2) = [both(c, z) for c in X_GROUPS[g]]
+            first = jnp.where(row < 3, lo0, jnp.where(row < 6, turn(lo1, 3), turn(lo2, 6)))
+            last = jnp.where(row < 3, turn(hi0, 3), jnp.where(row < 6, turn(hi1, 6), hi2))
+            send(2 * z + g, first, last)
+    for pair in range(layers // 2):
+        (lo0, hi0), (lo1, hi1) = [both(X_GROUPS[2][0], 2 * pair + k) for k in (0, 1)]
+        first = jnp.where(row < 4, lo0, turn(lo1, 4))
+        last = jnp.where(row < 4, turn(hi0, 3), turn(hi1, 7))
+        send(2 * layers + pair, first, last)
     if n_adj:
         for b in range(n_adj):
             one = (1, blocks.shape[1])
@@ -121,7 +151,7 @@
             blocks[owner : owner + 1, :] = jnp.full(one, owners_s[b], jnp.int32).astype(
                 jnp.float32
             )
-        end = PARTS * (layers // 2) * TILE
+        end = x_message_rows(layers)
         to_even[end:, :] = blocks[...]
         to_odd[end:, :] = blocks[...]
 
@@ -138,14 +168,21 @@
     return first, second
 
 
-def pack_pair(first, second, to_next):
-    edges = [jnp.where(to_next, second[b], first[b]) for b in range(len(first))]
+def pack_group(first, second, to_next):
+    edges = [jnp.where(to_next, upper, lower) for lower, upper in zip(first, second)]
     width = edges[0].shape[1]
+    place = lanes_of(edges[0].shape) % SLOT
     total = pltpu.roll(edges[0], jnp.where(to_next, width - 2, width - 3), 1)
     if len(edges) > 1:
-        other = pltpu.roll(edges[1], jnp.where(to_next, 2, 1), 1)
-        total = jnp.where(lanes_of(total.shape) % SLOT < 4, total, other)
+        middle = pltpu.roll(edges[1], jnp.where(to_next, 1, 0), 1)
+        total = jnp.where(place < 3, total, jnp.where(place < 6, middle, pltpu.roll(edges[2], 3, 1)))
     return total
+
+
+def place_group(before, after, slot):
+    width = before.shape[1]
+    lower, upper = ((0, 5), (width - 3, 2), (width - 5, width - 1))[slot]
+    return (pltpu.roll(before, lower, 1) if lower else before), pltpu.roll(after, upper, 1)
 
 
 def pack_y(fields, permittivity, strips, *to_y):
@@ -153,45 +190,45 @@
     ring = cells_x + TILE
     for r in range(cells_x // TILE):
         rows = slice(r * TILE, (r + 1) * TILE)
-        for q in range(PAIRS):
-            pair = []
-            for c in range(2 * q, min(2 * q + 2, PARTS)):
+        for g, parts in enumerate(Y_GROUPS):
+            packed = []
+            for c in parts:
 
                 def tile_of(z):
                     return fields[c, z, rows, :] if c < 6 else time_step / permittivity[z, rows, :]
 
-                pair.append(pack_strips(tile_of, range(layers)))
+                packed.append(pack_strips(tile_of, range(layers)))
                 for side in (0, 1):
-                    strips[side, c, rows, :] = pair[-1][side]
+                    strips[side, c, rows, :] = packed[-1][side]
             for swap, message in enumerate(to_y):
                 to_next = lax.axis_index("ys") % 2 == swap
-                at = slice(q * ring + r * TILE, q * ring + (r + 1) * TILE)
-                message[at, :] = pack_pair([p[0] for p in pair], [p[1] for p in pair], to_next)
+                at = slice(g * ring + r * TILE, g * ring + (r + 1) * TILE)
+                message[at, :] = pack_group([p[0] for p in packed], [p[1] for p in packed], to_next)
 
 
 def pack_corners(*refs, layers, n_rows, n_swaps):
     even, odd = refs[1 + n_swaps : 3 + n_swaps]
     strips, to_y = refs[-1 - n_swaps], refs[-n_swaps:]
     px = lax.axis_index("xs") % 2
-    ring = (to_y[0].shape[0] - 3 * n_rows) // PAIRS
-    for q in range(PAIRS):
-        pair = []
-        for c in range(2 * q, min(2 * q + 2, PARTS)):
+    ring = (to_y[0].shape[0] - 3 * n_rows) // len(Y_GROUPS)
+    for g, parts in enumerate(Y_GROUPS):
+        packed = []
+        for c in parts:
 
             def tile_of(z):
                 return halo_tile(even, odd, px, c, z, layers)
 
-            pair.append(pack_strips(tile_of, range(layers)))
+            packed.append(pack_strips(tile_of, range(layers)))
             for side in (0, 1):
-                strips[side, c, ring - TILE : ring, :] = pair[-1][side]
+                strips[side, c, ring - TILE : ring, :] = packed[-1][side]
         for swap, message in enumerate(to_y):
             to_next = lax.axis_index("ys") % 2 == swap
-            at = slice((q + 1) * ring - TILE, (q + 1) * ring)
-            message[at, :] = pack_pair([p[0] for p in pair], [p[1] for p in pair], to_next)
+            at = slice((g + 1) * ring - TILE, (g + 1) * ring)
+            message[at, :] = pack_group([p[0] for p in packed], [p[1] for p in packed], to_next)
     if n_rows:
         blocks = refs[3 + n_swaps]
-        end = PAIRS * ring
-        x_end = PARTS * (layers // 2) * TILE
+        end = len(Y_GROUPS) * ring
+        x_end = x_message_rows(layers)
         to_y[0][end : end + n_rows, :] = blocks[...]
         to_y[0][end + n_rows : end + 2 * n_rows, :] = even[x_end:, :]
         to_y[0][end + 2 * n_rows : end + 3 * n_rows, :] = odd[x_end:, :]
@@ -267,11 +304,10 @@
     ring, width = strips.shape[2:]
     fold = ring // TILE
     full = (fold, TILE, width)
-    for q in range(PAIRS):
+    for g, parts in enumerate(Y_GROUPS):
         for r in range(fold):
-            before = jnp.zeros((TILE, width), jnp.float32)
-            after = jnp.zeros((TILE, width), jnp.float32)
-            at = q * ring + r * TILE
+            before, after = zeros((TILE, width)), zeros((TILE, width))
+            at = g * ring + r * TILE
             for k, y_ref in enumerate(y_halos):
                 block = y_ref[at : at + TILE, :]
                 is_next = me % 2 == k
@@ -279,10 +315,8 @@
                 before = jnp.where(is_next, before, block)
             place = lanes_of(before.shape) % SLOT
             rows = slice(r * TILE, (r + 1) * TILE)
-            for c in range(2 * q, min(2 * q + 2, PARTS)):
-                b = c % 2
-                lower = pltpu.roll(before, width - 4, 1) if b else before
-                upper = pltpu.roll(after, 1 if b else 5, 1)
+            for slot, c in enumerate(parts):
+                lower, upper = place_group(before, after, slot)
                 strip[0, c, rows, :] = jnp.where(place < 3, lower, strips[0, c, rows, :])
                 strip[1, c, rows, :] = jnp.where(place >= 5, upper, strips[1, c, rows, :])
     lane = lanes_of(full)
@@ -335,8 +369,8 @@
             ref[cells_x:ring, :] = halo_tile(even, odd, px, c, z, layers)
 
     if n_adj:
-        end = PARTS * (layers // 2) * TILE
-        y_end = PAIRS * ring
+        end = x_message_rows(layers)
+        y_end = len(Y_GROUPS) * ring
         sets = [
             (given, 0, None),
             (even, end, px == 0),
@@ -635,8 +669,8 @@
     n_adj = adj_values.shape[0] if raw else 0
     n_rows = -(-3 * n_adj // TILE) * TILE
     ring = cells_x + TILE
-    x_rows = PARTS * (layers // 2) * TILE + n_rows
-    y_rows = PAIRS * ring + 3 * n_rows
+    x_rows = x_message_rows(layers) + n_rows
+    y_rows = len(Y_GROUPS) * ring + 3 * n_rows
 
     extra = (adj_values, adj_row, adj_owner.reshape(-1)) if raw else ()
     packed = pl.pallas_call(
@@ -655,8 +689,8 @@
     )(*[pltpu.with_memory_space_constraint(x, pltpu.HBM) for x in (fields, permittivity, *extra)])
     blocks = packed[2:]
     x_even, x_odd = swaps(xs_size)
+    from_odd = lax.ppermute(packed[1], "xs", x_odd)
     from_even = lax.ppermute(packed[0], "xs", x_even)
-    from_odd = lax.ppermute(packed[1], "xs", x_odd)
 
     y_swaps = swaps(ys_size)
     strips_shape = shape_of(2, PARTS, ring, cells_y)

time: 34.5 us -> 33.6 us (0.974)
  starting transfers between devices: 17.3 us -> 16.3 us
    ppermute x6, starting transfers between devices: 13.6 us -> 12.6 us  [across(): return lax.ppermute(block, 'xs', [(i, i ^ mask) for i in range(xs_size)])]
    ppermute x6, waiting for transfers between devices: 2.88 us -> 3.42 us  [across(): return lax.ppermute(block, 'xs', [(i, i ^ mask) for i in range(xs_size)])]
  transfers between devices with their start and end apart: 9 -> 9, of which waited for: 4 -> 4; matrix products, arithmetic and copies ran while one was open for 2% -> 2% of each run, Pallas kernels for 18% -> 17%
where the time goes in v4:
time: 33.6 us; the launch traced here: 33.5 us
  starting transfers between devices  16.3 us (49%)
  Pallas kernels  10 us (30%)
  waiting for transfers between devices  5.66 us (17%)
  between operations  0.79 us (2%)
  other arithmetic  0.34 us (1%)
    ppermute x6, starting transfers between devices, across(): return lax.ppermute(block, 'xs', [(i, i ^ mask) for i in range(xs_size)])  12.6 us
    ppermute x6, waiting for transfers between devices, across(): return lax.ppermute(block, 'xs', [(i, i ^ mask) for i in range(xs_size)])  3.42 us
    pallas_call x1, Pallas kernels, finish(): pl.pallas_call(later_steps, out_shape=shape_of(*fields.shape), in_specs=[...  2.79 us
    ppermute x1, starting transfers between devices, on_device(): lax.ppermute(message, 'ys', route)  2.52 us
    ppermute x1, waiting for transfers between devices, on_device(): lax.ppermute(message, 'ys', route)  2.23 us
    pallas_call x1, Pallas kernels, on_device(): pl.pallas_call(pack_y, out_shape=made, in_specs=[VMEM] * 2, out_specs=(VM...  1.75 us
    pallas_call x1, Pallas kernels, on_device(): pl.pallas_call(functools.partial(surface_steps, n_adj=n_adj, n_rows=n_row...  1.51 us
    pallas_call x1, Pallas kernels, on_device(): pl.pallas_call(functools.partial(pack_x, n_adj=n_adj), out_shape=(shape_o...  1.44 us
  transfers between devices with their start and end apart: 9, of which 4 were waited for; matrix products, arithmetic and copies ran while one was open for 2% of the time, Pallas kernels for 17%

profile of v4, /device:TPU:0, one launch (start us, length us, event | category | flops | bytes accessed | tf_op | source)
XLA Modules:
  0.0 33.5 jit_solution(1214574611192542674)
XLA Ops:
  0.6 0.0 copy-start
  0.6 0.0 copy-start.1
  0.7 0.0 copy-start.2
  0.7 1.4 %pack_x_edges.1 = (f32[336,128]{1,0:T(8,128)S(1)}, f32[336,128]{1,0:T(8,128)S(1)}, f32[16,128]{1,0:T(8,128)S(1)}) custom-call(f32[6,16,32,128]{3,2,1,0:T(8,128)} %refs_0_.5, f32[16,32,128]{2,1,0:T(8,128)} %refs_1_.5, f32[4,128]{1,0:T(4,128)} %refs_2_.1, s32[4]{0:T(128)} %refs_3_.1, s32[4]{0:T(128)} %bitcast.8), custom_call_target="tpu_custom_call" | custom-call | tf_op jit(solution)/shard_map/pack_x_edges/pallas_call | solution.py:676
  2.1 0.5 %collective-permute-start = (f32[336,128]{1,0:T(8,128)S(1)}, f32[336,128]{1,0:T(8,128)S(1)}, u32[]{:S(2)}, u32[]{:S(2)}) collective-permute-start(f32[336,128]{1,0:T(8,128)S(1)} %get-tuple-element.22), channel_id=1, source_target_pairs={{0,2},{4,6},{8,10},{12,14},{16,18},{20,22},{24,26},{28,30},{2,0},{... | collective-permute-start | bytes 516104 | tf_op jit(solution)/shard_map/ppermute | solution.py:693
  2.6 0.7 %collective-permute-start.1 = (f32[336,128]{1,0:T(8,128)S(1)}, f32[336,128]{1,0:T(8,128)S(1)}, u32[]{:S(2)}, u32[]{:S(2)}) collective-permute-start(f32[336,128]{1,0:T(8,128)S(1)} %get-tuple-element.23), channel_id=1, source_target_pairs={{2,4},{6,8},{10,12},{14,16},{18,20},{22,24},{26,28},{4,2},{8,6},{1... | collective-permute-start | bytes 516104 | tf_op jit(solution)/shard_map/ppermute | solution.py:692
  3.3 0.0 copy-done
  3.3 0.0 copy-done.1
  3.3 1.8 %pack_y_edges.1 = (f32[2,7,40,128]{3,2,1,0:T(8,128)S(1)}, f32[168,128]{1,0:T(8,128)S(1)}) custom-call(f32[6,16,32,128]{3,2,1,0:T(8,128)S(1)} %copy-done, f32[16,32,128]{2,1,0:T(8,128)S(1)} %copy-done.1), custom_call_target="tpu_custom_call" | custom-call | tf_op jit(solution)/shard_map/pack_y_edges/pallas_call | solution.py:698
  5.1 0.0 copy-done.2
  5.1 0.1 reshape.182
  5.2 0.1 select_reduce_fusion
  5.3 0.0 collective-permute-done.refs_2_
  5.3 0.0 collective-permute-done.1.refs_3_
  5.3 0.5 %pack_corners.1 = (f32[2,7,40,128]{3,2,1,0:T(8,128)S(1)}, f32[168,128]{1,0:T(8,128)S(1)}) custom-call(f32[2,7,40,128]{3,2,1,0:T(8,128)S(1)} %get-tuple-element.24.refs_0_, f32[168,128]{1,0:T(8,128)S(1)} %get-tuple-element.25.refs_1_, f32[336,128]{1,0:T(8,128)S(1)} %collective-permute-done.refs_2_, ...), custom_call_target="tpu_custom_call", output_to_operand_aliasing={{0}: (0, {}), {1}: (1, {})} | custom-call | tf_op jit(solution)/shard_map/pack_corners/pallas_call | solution.py:706
  5.8 2.5 %collective-permute-start.2 = (f32[168,128]{1,0:T(8,128)S(1)}, f32[168,128]{1,0:T(8,128)S(1)}, u32[]{:S(2)}, u32[]{:S(2)}) collective-permute-start(f32[168,128]{1,0:T(8,128)S(1)} %get-tuple-element.28), channel_id=1, source_target_pairs={{0,1},{1,0},{2,3},{3,2},{4,5},{5,4},{6,7},{7,6},{8,9},{9,8},{10,11... | collective-permute-start | bytes 258056 | tf_op jit(solution)/shard_map/ppermute | solution.py:715
  8.3 0.1 add_add_fusion
  8.4 0.1 mul.71
  8.5 0.1 add.60
  8.6 2.2 %collective-permute-done.2.refs_5_ = f32[168,128]{1,0:T(8,128)S(1)} collective-permute-done((f32[168,128]{1,0:T(8,128)S(1)}, f32[168,128]{1,0:T(8,128)S(1)}, u32[]{:S(2)}, u32[]{:S(2)}) %collective-permute-start.2) | collective-permute-done | bytes 86048 | tf_op jit(solution)/shard_map/ppermute | solution.py:715
  10.8 1.5 %surface_steps.1 = (f32[32,512]{1,0:T(8,128)S(1)}, f32[3,5,8,128]{3,2,1,0:T(8,128)S(1)}, f32[3,5,8,128]{3,2,1,0:T(8,128)S(1)}, f32[3,5,8,128]{3,2,1,0:T(8,128)S(1)}) custom-call(f32[6,16,32,128]{3,2,1,0:T(8,128)S(1)} %copy-done, f32[16,32,128]{2,1,0:T(8,128)S(1)} %copy-done.1, f32[336,128]{1,0:T(8,128)S(1)} %collective-permute-done.refs_2_, ...), custom_call_target="tpu_custom_call" | custom-call | tf_op jit(solution)/shard_map/surface_steps/pallas_call | solution.py:725
  12.3 7.9 %collective-permute-start.3 = (f32[32,512]{1,0:T(8,128)S(1)}, f32[32,512]{1,0:T(8,128)S(1)}, u32[]{:S(2)}, u32[]{:S(2)}) collective-permute-start(f32[32,512]{1,0:T(8,128)S(1)} %get-tuple-element.29.refs_0_), channel_id=1, source_target_pairs={{0,4},{2,6},{4,0},{6,2},{8,12},{10,14},{12,8},{14,10},{16,20},{18,... | collective-permute-start | bytes 196616 | tf_op jit(solution)/shard_map/ppermute | solution.py:599
  20.2 0.2 cosine_multiply_fusion
  20.4 0.1 collective-permute-start.4
  20.5 1.2 %first_step.1 = (f32[6,18,5,8,128]{4,3,2,1,0:T(8,128)S(1)}, f32[16,5,8,128]{3,2,1,0:T(8,128)S(1)}) custom-call(f32[6,16,32,128]{3,2,1,0:T(8,128)S(1)} %copy-done, f32[16,32,128]{2,1,0:T(8,128)S(1)} %copy-done.1, f32[336,128]{1,0:T(8,128)S(1)} %collective-permute-done.refs_2_, f32[336,128]{1,0:T(8,128)S(1)} %collective-permute-done.1.refs_3_, ...), custom_call_target="tpu_custom_call" | custom-call | tf_op jit(solution)/shard_map/first_step/pallas_call | solution.py:747
  21.6 0.8 %collective-permute-done.3.refs_2_ = f32[32,512]{1,0:T(8,128)S(1)} collective-permute-done((f32[32,512]{1,0:T(8,128)S(1)}, f32[32,512]{1,0:T(8,128)S(1)}, u32[]{:S(2)}, u32[]{:S(2)}) %collective-permute-start.3) | collective-permute-done | bytes 65568 | tf_op jit(solution)/shard_map/ppermute | solution.py:599
  22.5 0.0 collective-permute-start.5
  22.5 0.0 collective-permute-done.4.refs_1_
  22.5 1.2 %collective-permute-done.5.refs_3_ = f32[32,512]{1,0:T(8,128)S(1)} collective-permute-done((f32[32,512]{1,0:T(8,128)S(1)}, f32[32,512]{1,0:T(8,128)S(1)}, u32[]{:S(2)}, u32[]{:S(2)}) %collective-permute-start.5) | collective-permute-done | bytes 65568 | tf_op jit(solution)/shard_map/ppermute | solution.py:599
  23.7 0.3 partial_spectrum.1
  24.0 4.0 %collective-permute-start.6 = (f32[16,512]{1,0:T(8,128)S(1)}, f32[16,512]{1,0:T(8,128)S(1)}, u32[]{:S(2)}, u32[]{:S(2)}) collective-permute-start(f32[16,512]{1,0:T(8,128)S(1)} %get-tuple-element.39), channel_id=1, source_target_pairs={{0,24},{2,26},{4,28},{6,30},{8,16},{10,18},{12,20},{14,22},{16,8},... | collective-permute-start | bytes 98312 | tf_op jit(solution)/shard_map/ppermute | solution.py:599
  28.0 0.0 collective-permute-start.7
  28.0 0.6 %collective-permute-start.8 = (f32[16,512]{1,0:T(8,128)S(1)}, f32[16,512]{1,0:T(8,128)S(1)}, u32[]{:S(2)}, u32[]{:S(2)}) collective-permute-start(f32[16,512]{1,0:T(8,128)S(1)} %get-tuple-element.41), channel_id=1, source_target_pairs={{0,8},{2,10},{4,12},{6,14},{8,0},{10,2},{12,4},{14,6},{16,24},{18,... | collective-permute-start | bytes 98312 | tf_op jit(solution)/shard_map/ppermute | solution.py:599
  28.6 2.8 %later_steps.1 = f32[6,16,32,128]{3,2,1,0:T(8,128)} custom-call(f32[6,18,5,8,128]{4,3,2,1,0:T(8,128)S(1)} %get-tuple-element.35.refs_0_, f32[16,5,8,128]{3,2,1,0:T(8,128)S(1)} %get-tuple-element.36.refs_1_, f32[3,5,8,128]{3,2,1,0:T(8,128)S(1)} %get-tuple-element.30.refs_4_.refs_2_, f32[3,5,8,128]{3,2,1,0:T(8,128)S(1)} %get-tuple-element.31.refs_5_.refs_3_, ...), custom_call_target="tpu_custom_call" | custom-call | tf_op jit(solution)/shard_map/later_steps/pallas_call | solution.py:761
  31.4 0.0 collective-permute-done.6.refs_1_
  31.5 1.4 %collective-permute-done.7.refs_2_ = f32[16,512]{1,0:T(8,128)S(1)} collective-permute-done((f32[16,512]{1,0:T(8,128)S(1)}, f32[16,512]{1,0:T(8,128)S(1)}, u32[]{:S(2)}, u32[]{:S(2)}) %collective-permute-start.7) | collective-permute-done | bytes 32800 | tf_op jit(solution)/shard_map/ppermute | solution.py:599
  32.8 0.0 collective-permute-done.8.refs_3_
  32.8 0.6 %add_arrived.1 = f32[16,4,128]{2,1,0:T(4,128)} custom-call(f32[16,512]{1,0:T(8,128)S(1)} %get-tuple-element.38.refs_0_, f32[16,512]{1,0:T(8,128)S(1)} %collective-permute-done.6.refs_1_, f32[16,512]{1,0:T(8,128)S(1)} %collective-permute-done.7.refs_2_, f32[16,512]{1,0:T(8,128)S(1)} %collective-permute-done.8.refs_3_), custom_call_target="tpu_custom_call" | custom-call | tf_op jit(solution)/shard_map/add_arrived/pallas_call | solution.py:617
  (7 shorter events, 0.1 us)
Async XLA Ops:
  0.6 2.7 %copy-start = (f32[6,16,32,128]{3,2,1,0:T(8,128)S(1)}, f32[6,16,32,128]{3,2,1,0:T(8,128)}, u32[]{:S(2)}) copy-start(f32[6,16,32,128]{3,2,1,0:T(8,128)} %refs_0_.5) | copy-start | bytes 4718596
  0.6 2.7 %copy-start.1 = (f32[16,32,128]{2,1,0:T(8,128)S(1)}, f32[16,32,128]{2,1,0:T(8,128)}, u32[]{:S(2)}) copy-start(f32[16,32,128]{2,1,0:T(8,128)} %refs_1_.5) | copy-start | bytes 786436
  0.7 4.4 %copy-start.2 = (s32[128]{0:T(128)S(1)}, s32[128]{0:T(128)}, u32[]{:S(2)}) copy-start(s32[128]{0:T(128)} %param.11) | copy-start | bytes 1540
  2.1 3.2 %collective-permute-start = (f32[336,128]{1,0:T(8,128)S(1)}, f32[336,128]{1,0:T(8,128)S(1)}, u32[]{:S(2)}, u32[]{:S(2)}) collective-permute-start(f32[336,128]{1,0:T(8,128)S(1)} %get-tuple-element.22), channel_id=1, source_target_pairs={{0,2},{4,6},{8,10},{12,14},{16,18},{20,22},{24,26},{28,30},{2,0},{... | collective-permute-start | bytes 516104 | tf_op jit(solution)/shard_map/ppermute | solution.py:693
  2.6 2.7 %collective-permute-start.1 = (f32[336,128]{1,0:T(8,128)S(1)}, f32[336,128]{1,0:T(8,128)S(1)}, u32[]{:S(2)}, u32[]{:S(2)}) collective-permute-start(f32[336,128]{1,0:T(8,128)S(1)} %get-tuple-element.23), channel_id=1, source_target_pairs={{2,4},{6,8},{10,12},{14,16},{18,20},{22,24},{26,28},{4,2},{8,6},{1... | collective-permute-start | bytes 516104 | tf_op jit(solution)/shard_map/ppermute | solution.py:692
  5.8 5.0 %collective-permute-start.2 = (f32[168,128]{1,0:T(8,128)S(1)}, f32[168,128]{1,0:T(8,128)S(1)}, u32[]{:S(2)}, u32[]{:S(2)}) collective-permute-start(f32[168,128]{1,0:T(8,128)S(1)} %get-tuple-element.28), channel_id=1, source_target_pairs={{0,1},{1,0},{2,3},{3,2},{4,5},{5,4},{6,7},{7,6},{8,9},{9,8},{10,11... | collective-permute-start | bytes 258056 | tf_op jit(solution)/shard_map/ppermute | solution.py:715
  12.3 10.2 %collective-permute-start.3 = (f32[32,512]{1,0:T(8,128)S(1)}, f32[32,512]{1,0:T(8,128)S(1)}, u32[]{:S(2)}, u32[]{:S(2)}) collective-permute-start(f32[32,512]{1,0:T(8,128)S(1)} %get-tuple-element.29.refs_0_), channel_id=1, source_target_pairs={{0,4},{2,6},{4,0},{6,2},{8,12},{10,14},{12,8},{14,10},{16,20},{18,... | collective-permute-start | bytes 196616 | tf_op jit(solution)/shard_map/ppermute | solution.py:599
  20.4 2.1 %collective-permute-start.4 = (f32[32,512]{1,0:T(8,128)S(1)}, f32[32,512]{1,0:T(8,128)S(1)}, u32[]{:S(2)}, u32[]{:S(2)}) collective-permute-start(f32[32,512]{1,0:T(8,128)S(1)} %get-tuple-element.29.refs_0_), channel_id=1, source_target_pairs={{0,2},{2,0},{4,6},{6,4},{8,10},{10,8},{12,14},{14,12},{16,18},{18,... | collective-permute-start | bytes 196616 | tf_op jit(solution)/shard_map/ppermute | solution.py:599
  22.5 1.3 %collective-permute-start.5 = (f32[32,512]{1,0:T(8,128)S(1)}, f32[32,512]{1,0:T(8,128)S(1)}, u32[]{:S(2)}, u32[]{:S(2)}) collective-permute-start(f32[32,512]{1,0:T(8,128)S(1)} %collective-permute-done.3.refs_2_), channel_id=1, source_target_pairs={{0,2},{2,0},{4,6},{6,4},{8,10},{10,8},{12,14},{14,12},{16,18},{18,... | collective-permute-start | bytes 196616 | tf_op jit(solution)/shard_map/ppermute | solution.py:599
  24.0 7.4 %collective-permute-start.6 = (f32[16,512]{1,0:T(8,128)S(1)}, f32[16,512]{1,0:T(8,128)S(1)}, u32[]{:S(2)}, u32[]{:S(2)}) collective-permute-start(f32[16,512]{1,0:T(8,128)S(1)} %get-tuple-element.39), channel_id=1, source_target_pairs={{0,24},{2,26},{4,28},{6,30},{8,16},{10,18},{12,20},{14,22},{16,8},... | collective-permute-start | bytes 98312 | tf_op jit(solution)/shard_map/ppermute | solution.py:599
  28.0 4.8 %collective-permute-start.7 = (f32[16,512]{1,0:T(8,128)S(1)}, f32[16,512]{1,0:T(8,128)S(1)}, u32[]{:S(2)}, u32[]{:S(2)}) collective-permute-start(f32[16,512]{1,0:T(8,128)S(1)} %get-tuple-element.40), channel_id=1, source_target_pairs={{0,16},{2,18},{4,20},{6,22},{8,24},{10,26},{12,28},{14,30},{16,0},... | collective-permute-start | bytes 98312 | tf_op jit(solution)/shard_map/ppermute | solution.py:599
  28.0 4.8 %collective-permute-start.8 = (f32[16,512]{1,0:T(8,128)S(1)}, f32[16,512]{1,0:T(8,128)S(1)}, u32[]{:S(2)}, u32[]{:S(2)}) collective-permute-start(f32[16,512]{1,0:T(8,128)S(1)} %get-tuple-element.41), channel_id=1, source_target_pairs={{0,8},{2,10},{4,12},{6,14},{8,0},{10,2},{12,4},{14,6},{16,24},{18,... | collective-permute-start | bytes 98312 | tf_op jit(solution)/shard_map/ppermute | solution.py:599

commit v5 on v4

--- a/solution.py
+++ b/solution.py
@@ -23,6 +23,7 @@
 X_GROUPS = ((0, 1, 3), (2, 4, 6), (5,))
 Y_GROUPS = ((0, 2, 4), (1, 3, 6), (5,))
 TOGETHER = 8
+EARLY = 2
 
 VMEM = pl.BlockSpec(memory_space=pltpu.VMEM)
 ANY = pl.BlockSpec(memory_space=pl.ANY)
@@ -91,6 +92,25 @@
     lax.fori_loop(0, rounds, several, None)
     for i in range(first + rounds * together, last):
         body(i)
+
+
+def pack_edge(tile_of, message, layers, last):
+    def turn(v, shift):
+        return pltpu.roll(v, shift, 0) if shift else v
+
+    def send(tile, v):
+        message[tile * TILE : (tile + 1) * TILE, :] = v
+
+    row = rows_of((TILE, message.shape[1]))
+    shifts = (3, 6, 0) if last else (0, 3, 6)
+    for z in range(layers):
+        for g in range(2):
+            a, b, c = [turn(tile_of(c, z), shift) for c, shift in zip(X_GROUPS[g], shifts)]
+            send(2 * z + g, jnp.where(row < 3, a, jnp.where(row < 6, b, c)))
+    shifts = (3, 7) if last else (0, 4)
+    for pair in range(layers // 2):
+        a, b = [turn(tile_of(X_GROUPS[2][0], 2 * pair + k), shifts[k]) for k in (0, 1)]
+        send(2 * layers + pair, jnp.where(row < REACH, a, b))
 
 
 def pack_x(*refs, n_adj):
@@ -118,63 +138,45 @@
     for copy in copies:
         copy.wait()
 
-    def both(c, z):
-        if c < 6:
-            return edges[0, c, z], edges[1, c, z]
-        return time_step / edge_perm[0, z], time_step / edge_perm[1, z]
-
-    def send(tile, first, last):
-        at = slice(tile * TILE, (tile + 1) * TILE)
-        to_even[at, :] = jnp.where(px == 0, last, first)
-        to_odd[at, :] = jnp.where(px == 0, first, last)
-
-    def turn(v, shift):
-        return pltpu.roll(v, shift, 0)
-
-    row = rows_of((TILE, fields.shape[3]))
-    for z in range(layers):
-        for g in range(2):
-            (lo0, hi0), (lo1, hi1), (lo2, hi2) = [both(c, z) for c in X_GROUPS[g]]
-            first = jnp.where(row < 3, lo0, jnp.where(row < 6, turn(lo1, 3), turn(lo2, 6)))
-            last = jnp.where(row < 3, turn(hi0, 3), jnp.where(row < 6, turn(hi1, 6), hi2))
-            send(2 * z + g, first, last)
-    for pair in range(layers // 2):
-        (lo0, hi0), (lo1, hi1) = [both(X_GROUPS[2][0], 2 * pair + k) for k in (0, 1)]
-        first = jnp.where(row < 4, lo0, turn(lo1, 4))
-        last = jnp.where(row < 4, turn(hi0, 3), turn(hi1, 7))
-        send(2 * layers + pair, first, last)
+    def edge_of(k):
+        return lambda c, z: edges[k, c, z] if c < 6 else time_step / edge_perm[k, z]
+
+    def pack(first, last):
+        pack_edge(edge_of(0), first, layers, False)
+        pack_edge(edge_of(1), last, layers, True)
+
+    pl.when(px == 0)(lambda: pack(to_odd, to_even))
+    pl.when(px == 1)(lambda: pack(to_even, to_odd))
     if n_adj:
         for b in range(n_adj):
-            one = (1, blocks.shape[1])
-            row, owner = n_adj + b, 2 * n_adj + b
-            blocks[row : row + 1, :] = jnp.full(one, rows_s[b], jnp.int32).astype(jnp.float32)
-            blocks[owner : owner + 1, :] = jnp.full(one, owners_s[b], jnp.int32).astype(
-                jnp.float32
-            )
-        end = x_message_rows(layers)
-        to_even[end:, :] = blocks[...]
-        to_odd[end:, :] = blocks[...]
+            code = rows_s[b] + cells_x * owners_s[b]
+            blocks[n_adj + b : n_adj + b + 1, :] = jnp.full(
+                (1, blocks.shape[1]), code, jnp.int32
+            ).astype(jnp.float32)
+        to_even[x_message_rows(layers) :, :] = blocks[...]
+        to_odd[x_message_rows(layers) :, :] = blocks[...]
+
+
+def pack_strip(tile_of, layers, shift):
+    total = None
+    for z in range(layers):
+        block = tile_of(z)
+        moved = pltpu.roll(block, (SLOT * z + shift) % block.shape[1], 1)
+        total = moved if z == 0 else jnp.where(lanes_of(block.shape) // SLOT == z, moved, total)
+    return total
 
 
 def pack_strips(tile_of, layers):
-    first = second = None
-    for z in layers:
-        block = tile_of(z)
-        here = lanes_of(block.shape) // SLOT == z
-        lower = pltpu.roll(block, (SLOT * z + 3) % block.shape[1], 1)
-        upper = pltpu.roll(block, (SLOT * z + 5) % block.shape[1], 1)
-        first = lower if first is None else jnp.where(here, lower, first)
-        second = upper if second is None else jnp.where(here, upper, second)
-    return first, second
-
-
-def pack_group(first, second, to_next):
-    edges = [jnp.where(to_next, upper, lower) for lower, upper in zip(first, second)]
+    tiles = [tile_of(z) for z in range(layers)]
+    return [pack_strip(lambda z: tiles[z], layers, shift) for shift in (3, 5)]
+
+
+def pack_group(edges, to_next):
     width = edges[0].shape[1]
     place = lanes_of(edges[0].shape) % SLOT
-    total = pltpu.roll(edges[0], jnp.where(to_next, width - 2, width - 3), 1)
+    total = pltpu.roll(edges[0], width - 2 if to_next else width - 3, 1)
     if len(edges) > 1:
-        middle = pltpu.roll(edges[1], jnp.where(to_next, 1, 0), 1)
+        middle = pltpu.roll(edges[1], 1, 1) if to_next else edges[1]
         total = jnp.where(place < 3, total, jnp.where(place < 6, middle, pltpu.roll(edges[2], 3, 1)))
     return total
 
@@ -197,36 +199,41 @@
                 def tile_of(z):
                     return fields[c, z, rows, :] if c < 6 else time_step / permittivity[z, rows, :]
 
-                packed.append(pack_strips(tile_of, range(layers)))
+                packed.append(pack_strips(tile_of, layers))
                 for side in (0, 1):
                     strips[side, c, rows, :] = packed[-1][side]
             for swap, message in enumerate(to_y):
                 to_next = lax.axis_index("ys") % 2 == swap
                 at = slice(g * ring + r * TILE, g * ring + (r + 1) * TILE)
-                message[at, :] = pack_group([p[0] for p in packed], [p[1] for p in packed], to_next)
+                message[at, :] = jnp.where(
+                    to_next,
+                    pack_group([p[1] for p in packed], True),
+                    pack_group([p[0] for p in packed], False),
+                )
 
 
 def pack_corners(*refs, layers, n_rows, n_swaps):
-    even, odd = refs[1 + n_swaps : 3 + n_swaps]
-    strips, to_y = refs[-1 - n_swaps], refs[-n_swaps:]
+    even, odd = refs[n_swaps : 2 + n_swaps]
+    to_y = refs[-n_swaps:]
     px = lax.axis_index("xs") % 2
     ring = (to_y[0].shape[0] - 3 * n_rows) // len(Y_GROUPS)
-    for g, parts in enumerate(Y_GROUPS):
-        packed = []
-        for c in parts:
-
-            def tile_of(z):
-                return halo_tile(even, odd, px, c, z, layers)
-
-            packed.append(pack_strips(tile_of, range(layers)))
-            for side in (0, 1):
-                strips[side, c, ring - TILE : ring, :] = packed[-1][side]
-        for swap, message in enumerate(to_y):
-            to_next = lax.axis_index("ys") % 2 == swap
-            at = slice((g + 1) * ring - TILE, (g + 1) * ring)
-            message[at, :] = pack_group([p[0] for p in packed], [p[1] for p in packed], to_next)
+
+    def fill(message, to_next):
+        for g, parts in enumerate(Y_GROUPS):
+            packed = [
+                pack_strip(
+                    lambda z: halo_tile(even, odd, px, c, z, layers), layers, 5 if to_next else 3
+                )
+                for c in parts
+            ]
+            message[(g + 1) * ring - TILE : (g + 1) * ring, :] = pack_group(packed, to_next)
+
+    for swap, message in enumerate(to_y):
+        is_next = lax.axis_index("ys") % 2 == swap
+        for to_next in (False, True):
+            pl.when(is_next == to_next)(functools.partial(fill, message, to_next))
     if n_rows:
-        blocks = refs[3 + n_swaps]
+        blocks = refs[2 + n_swaps]
         end = len(Y_GROUPS) * ring
         x_end = x_message_rows(layers)
         to_y[0][end : end + n_rows, :] = blocks[...]
@@ -239,17 +246,16 @@
     return lax.broadcasted_iota(jnp.int32, shape, 1) * shape[0] + fold
 
 
-def gather_sources(sets, px, me, source, n_adj, cells_x):
-    full = source.shape[1:]
-    row_at = row_index(full).astype(jnp.float32)
-    mine = jnp.zeros(full, jnp.float32)
-    other = jnp.zeros(full, jnp.float32)
+def gather_sources(sets, px, me, totals, n_adj, cells_x):
+    mine, other = totals[0], totals[1]
+    row_at = row_index(mine.shape).astype(jnp.float32)
     own_index = jnp.where(me == 0, 0.0, 1.0)
     for ref, start, is_next in sets:
         for b in range(n_adj):
             value = ref[start + b : start + b + 1, :]
-            row = ref[start + n_adj + b : start + n_adj + b + 1, :]
-            owner = ref[start + 2 * n_adj + b : start + 2 * n_adj + b + 1, :]
+            code = ref[start + n_adj + b : start + n_adj + b + 1, :]
+            owner = jnp.where(code >= cells_x, 1.0, 0.0)
+            row = code - cells_x * owner
             if is_next is not None:
                 after = jnp.where(row < REACH, row + cells_x, -1.0)
                 before = jnp.where(row >= cells_x - REACH, row + TILE, -1.0)
@@ -257,7 +263,12 @@
             is_mine = owner == own_index
             mine = mine + jnp.where(row_at == jnp.where(is_mine, row, -1.0), value, 0.0)
             other = other + jnp.where(row_at == jnp.where(is_mine, -1.0, row), value, 0.0)
-    lane = lanes_of(full)
+    totals[0], totals[1] = mine, other
+
+
+def place_sources(totals, me, source):
+    mine, other = totals[0], totals[1]
+    lane = lanes_of(mine.shape)
     slot = (lane >= SLOT * ZS) & (lane < SLOT * (ZS + 1))
     place = lane - SLOT * ZS
     shift = SLOT * ZS + 3
@@ -299,9 +310,9 @@
     return jnp.where(outside, 0.0, time_step)
 
 
-def evolve_strips(strips, y_halos, source, strip, edge_e, edge_h):
+def evolve_strips(strips, halo_strips, y_halos, source, strip, edge_e, edge_h):
     me = lax.axis_index("ys")
-    ring, width = strips.shape[2:]
+    ring, width = strips.shape[2] + TILE, strips.shape[3]
     fold = ring // TILE
     full = (fold, TILE, width)
     for g, parts in enumerate(Y_GROUPS):
@@ -317,8 +328,9 @@
             rows = slice(r * TILE, (r + 1) * TILE)
             for slot, c in enumerate(parts):
                 lower, upper = place_group(before, after, slot)
-                strip[0, c, rows, :] = jnp.where(place < 3, lower, strips[0, c, rows, :])
-                strip[1, c, rows, :] = jnp.where(place >= 5, upper, strips[1, c, rows, :])
+                own = [strips[k, c, rows, :] if r + 1 < fold else halo_strips[k, c] for k in (0, 1)]
+                strip[0, c, rows, :] = jnp.where(place < 3, lower, own[0])
+                strip[1, c, rows, :] = jnp.where(place >= 5, upper, own[1])
     lane = lanes_of(full)
     place = lane % SLOT
     for side in (0, 1):
@@ -350,39 +362,63 @@
             ez = ez + co * (hy - prev_x(hy) - (hx - lane_roll(hx, 1)) - source[1 + side])
 
 
-def surface_steps(*refs, n_adj, n_rows, n_swaps):
+def surface_layers(layers):
+    return range(max(ZS - STEPS, 0), min(ZS + STEPS + 1, layers))
+
+
+def prepare_surface(*refs, n_adj, n_rows):
     fields, permittivity, even, odd = refs[:4]
-    strips, y_halos, given = refs[4], refs[5 : 5 + n_swaps], refs[5 + n_swaps]
-    out, source, edge_e, edge_h, grid, coeffs, state, strip = refs[6 + n_swaps :]
+    state, coeffs, halo_strips = refs[4 + bool(n_adj) : 7 + bool(n_adj)]
+    rows = refs[-1]
     px = lax.axis_index("xs") % 2
     layers, cells_x, width = fields.shape[1:]
     ring = cells_x + TILE
     fold = ring // TILE
-    full = (fold, TILE, width)
+    for c in range(PARTS):
+        halos = [halo_tile(even, odd, px, c, z, layers) for z in range(layers)]
+        for side, tile in enumerate(pack_strips(lambda z: halos[z], layers)):
+            halo_strips[side, c] = tile
+        for z in surface_layers(layers):
+            rows[c, z, 0:cells_x, :] = fields[c, z] if c < 6 else time_step / permittivity[z]
+            rows[c, z, cells_x:ring, :] = halos[z]
+            folded = unfold(rows.at[c, z], fold)
+            if c < 6:
+                state[c, z] = folded
+            else:
+                coeffs[z] = folded
+    if n_adj:
+        blocks, totals = refs[4], refs[8]
+        totals[...] = zeros(totals.shape)
+        end = x_message_rows(layers)
+        sets = [(blocks, 0, None), (even, end, px == 0), (odd, end, px == 1)]
+        gather_sources(sets, px, lax.axis_index("ys"), totals, n_adj, cells_x)
+
+
+def surface_steps(*refs, n_adj, n_rows, n_swaps):
+    before, coeffs, halo_strips, strips = refs[:4]
+    y_halos, given = refs[4 : 4 + n_swaps], refs[4 + n_swaps]
+    out, source, edge_e, edge_h, rows, state, strip, totals = refs[5 + n_swaps :]
+    px = lax.axis_index("xs") % 2
+    me = lax.axis_index("ys")
+    layers = before.shape[1]
+    full = before.shape[2:]
+    fold, width = full[0], full[2]
+    cells_x = (fold - 1) * TILE
     lane = lanes_of(full)
-    used = range(max(ZS - STEPS, 0), min(ZS + STEPS + 1, layers))
-
-    for z in used:
-        for c in range(PARTS):
-            ref = grid.at[c, z] if c < 6 else coeffs.at[z]
-            ref[0:cells_x, :] = fields[c, z] if c < 6 else time_step / permittivity[z]
-            ref[cells_x:ring, :] = halo_tile(even, odd, px, c, z, layers)
 
     if n_adj:
-        end = x_message_rows(layers)
-        y_end = len(Y_GROUPS) * ring
+        end = len(Y_GROUPS) * fold * TILE
         sets = [
-            (given, 0, None),
-            (even, end, px == 0),
-            (odd, end, px == 1),
-            (y_halos[0], y_end, None),
-            (y_halos[0], y_end + n_rows, px == 0),
-            (y_halos[0], y_end + 2 * n_rows, px == 1),
+            (y_halos[0], end, None),
+            (y_halos[0], end + n_rows, px == 0),
+            (y_halos[0], end + 2 * n_rows, px == 1),
         ]
-        gather_sources(sets, px, lax.axis_index("ys"), source, n_adj, cells_x)
+        totals[...] = given[...]
+        gather_sources(sets, px, me, totals, n_adj, cells_x)
+        place_sources(totals, me, source)
     else:
         source[...] = given[...]
-    evolve_strips(strips, y_halos, source, strip, edge_e, edge_h)
+    evolve_strips(strips, halo_strips, y_halos, source, strip, edge_e, edge_h)
 
     dt = step_size(full)
     for step in range(STEPS):
@@ -390,13 +426,13 @@
         low, high = max(ZS - STEPS + step, 0), min(ZS + STEPS - 1 - step, layers - 1)
 
         def load(c, z):
-            return state[c, z] if step else unfold(grid.at[c, z], fold)
+            return state[c, z] if step else before[c, z]
 
         def store(c, z, v):
-            if final:
-                fold_back(grid.at[c, z], v)
-            else:
+            if not final:
                 state[c, z] = v
+            elif z == ZS and c in (0, 1, 3, 4):
+                fold_back(rows.at[c], v)
 
         below = None
         ex, ey = load(0, low), load(1, low)
@@ -415,11 +451,7 @@
             for c, v in ((3, hx), (4, hy), (5, hz)):
                 store(c, z, v)
             if z == 0 or below:
-                if step:
-                    co = coeffs[z, 0:ring, :].reshape(full)
-                else:
-                    co = unfold(coeffs.at[z], fold)
-                    coeffs[z, 0:ring, :] = co.reshape(ring, width)
+                co = coeffs[z]
                 hx_z = hx - below[0] if z else hx
                 hy_z = hy - below[1] if z else hy
                 edge = lane_roll(edge_h[step], width - 1 - (SLOT * z + 2))
@@ -434,7 +466,7 @@
             below = (hx, hy)
             ex, ey = ex_above, ey_above
     for k, (c, sign) in enumerate(((4, -1.0), (3, 1.0), (1, 1.0), (0, -1.0))):
-        out[:, k * width : (k + 1) * width] = sign * grid[c, ZS, 0:cells_x, :]
+        out[:, k * width : (k + 1) * width] = sign * rows[c, 0:cells_x, :]
 
 
 def take_steps(first, last, layers, refs, load, store, load_coeff, after_layer=None):
@@ -479,7 +511,7 @@
         ref[c + 3, 0] = zeros(ref.shape[2:])
 
 
-def first_step(*refs):
+def early_steps(*refs):
     fields, permittivity, even, odd, *carried = refs[:7]
     state, coeffs, grid, coeff_rows = refs[7:]
     px = lax.axis_index("xs") % 2
@@ -505,7 +537,7 @@
     def store(step, c, z, v):
         state[c, z + 1] = v
 
-    take_steps(0, 1, layers, carried, load, store, lambda z: coeffs[z])
+    take_steps(0, EARLY, layers, carried, load, store, lambda z: coeffs[z])
 
 
 def later_steps(*refs):
@@ -520,7 +552,7 @@
     zero_outside(state, layers)
 
     def load(step, c, z):
-        return (before if step == 1 else state)[c, z + 1]
+        return (before if step == EARLY else state)[c, z + 1]
 
     def store(step, c, z, v):
         if step + 1 < STEPS or c >= 3:
@@ -529,11 +561,11 @@
             fold_back(grid.at[c, z], v)
 
     take_steps(
-        1,
+        EARLY,
         STEPS,
         layers,
         carried,
-        lambda step, c, z: load(1 if step == 1 else 2, c, z),
+        load,
         store,
         lambda z: coeffs[z],
         lambda z: copy_out(z).start(),
@@ -667,15 +699,16 @@
     xs_size, ys_size = lax.axis_size("xs"), lax.axis_size("ys")
     raw = ys_size == 2
     n_adj = adj_values.shape[0] if raw else 0
-    n_rows = -(-3 * n_adj // TILE) * TILE
+    n_rows = -(-2 * n_adj // TILE) * TILE
     ring = cells_x + TILE
     x_rows = x_message_rows(layers) + n_rows
     y_rows = len(Y_GROUPS) * ring + 3 * n_rows
 
     extra = (adj_values, adj_row, adj_owner.reshape(-1)) if raw else ()
-    packed = pl.pallas_call(
+    x_message = shape_of(x_rows, cells_y)
+    to_even, to_odd, *blocks = pl.pallas_call(
         functools.partial(pack_x, n_adj=n_adj),
-        out_shape=(shape_of(x_rows, cells_y),) * 2 + ((shape_of(n_rows, cells_y),) if raw else ()),
+        out_shape=(x_message,) * 2 + ((shape_of(n_rows, cells_y),) if raw else ()),
         in_specs=[ANY] * (2 + len(extra)),
         out_specs=(VMEM,) * (3 if raw else 2),
         scratch_shapes=[
@@ -687,41 +720,52 @@
         compiler_params=PARAMS,
         name="pack_x_edges",
     )(*[pltpu.with_memory_space_constraint(x, pltpu.HBM) for x in (fields, permittivity, *extra)])
-    blocks = packed[2:]
     x_even, x_odd = swaps(xs_size)
-    from_odd = lax.ppermute(packed[1], "xs", x_odd)
-    from_even = lax.ppermute(packed[0], "xs", x_even)
+    from_even = lax.ppermute(to_even, "xs", x_even)
+    from_odd = lax.ppermute(to_odd, "xs", x_odd)
 
     y_swaps = swaps(ys_size)
-    strips_shape = shape_of(2, PARTS, ring, cells_y)
-    made = (strips_shape,) + (shape_of(y_rows, cells_y),) * len(y_swaps)
-    packed = pl.pallas_call(
+    messages = (shape_of(y_rows, cells_y),) * len(y_swaps)
+    strips, *to_y = pl.pallas_call(
         pack_y,
-        out_shape=made,
+        out_shape=(shape_of(2, PARTS, cells_x, cells_y),) + messages,
         in_specs=[VMEM] * 2,
-        out_specs=(VMEM,) * len(made),
+        out_specs=(VMEM,) * (1 + len(messages)),
         compiler_params=PARAMS,
         name="pack_y_edges",
     )(fields, permittivity)
-    strips, *to_y = pl.pallas_call(
+    to_y = pl.pallas_call(
         functools.partial(pack_corners, layers=layers, n_rows=n_rows, n_swaps=len(y_swaps)),
-        out_shape=made,
-        in_specs=[VMEM] * (len(made) + 2 + len(blocks)),
-        out_specs=(VMEM,) * len(made),
-        input_output_aliases={k: k for k in range(len(made))},
+        out_shape=messages,
+        in_specs=[VMEM] * (len(messages) + 2 + len(blocks)),
+        out_specs=(VMEM,) * len(messages),
+        input_output_aliases={k: k for k in range(len(messages))},
         compiler_params=PARAMS,
         name="pack_corners",
-    )(*packed, from_even, from_odd, *blocks)
+    )(*to_y, from_even, from_odd, *blocks)
     y_halos = [lax.ppermute(message, "ys", route) for message, route in zip(to_y, y_swaps)]
 
+    fold = ring // TILE
+    folded = (fold, TILE, cells_y)
+    made = (
+        shape_of(6, layers, *folded),
+        shape_of(layers, *folded),
+        shape_of(2, PARTS, TILE, cells_y),
+    ) + ((shape_of(2, *folded),) if raw else ())
+    prepared = pl.pallas_call(
+        functools.partial(prepare_surface, n_adj=n_adj, n_rows=n_rows),
+        out_shape=made,
+        in_specs=[VMEM] * (4 + len(blocks)),
+        out_specs=(VMEM,) * len(made),
+        scratch_shapes=[pltpu.VMEM((PARTS, layers, ring, cells_y), jnp.float32)],
+        compiler_params=PARAMS,
+        name="prepare_surface",
+    )(fields, permittivity, from_even, from_odd, *blocks)
     if raw:
-        sources = blocks
+        sources = prepared[3:]
     else:
         sources = (gathered_sources(adj_values, adj_owner, adj_row, cells_x, cells_y),)
-
-    fold = ring // TILE
-    folded = (fold, TILE, cells_y)
-    operands = (fields, permittivity, from_even, from_odd, strips, *y_halos, *sources)
+    operands = (*prepared[:3], strips, *y_halos, *sources)
     tile, *carried = pl.pallas_call(
         functools.partial(surface_steps, n_adj=n_adj, n_rows=n_rows, n_swaps=len(y_swaps)),
         out_shape=(
@@ -733,10 +777,10 @@
         in_specs=[VMEM] * len(operands),
         out_specs=(VMEM,) * 4,
         scratch_shapes=[
-            pltpu.VMEM((6, layers, ring, cells_y), jnp.float32),
-            pltpu.VMEM((layers, ring, cells_y), jnp.float32),
+            pltpu.VMEM((6, ring, cells_y), jnp.float32),
             pltpu.VMEM((6, layers, *folded), jnp.float32),
             pltpu.VMEM((2, PARTS, ring, cells_y), jnp.float32),
+            pltpu.VMEM((2, *folded), jnp.float32),
         ],
         compiler_params=PARAMS,
         name="surface_steps",
@@ -745,7 +789,7 @@
     state_shape = (6, layers + 2, *folded)
     operands = (fields, permittivity, from_even, from_odd, *carried)
     stepped = pl.pallas_call(
-        first_step,
+        early_steps,
         out_shape=(shape_of(*state_shape), shape_of(layers, *folded)),
         in_specs=[VMEM] * len(operands),
         out_specs=(VMEM, VMEM),
@@ -754,7 +798,7 @@
             pltpu.VMEM((layers, ring, cells_y), jnp.float32),
         ],
         compiler_params=PARAMS,
-        name="first_step",
+        name="early_steps",
     )(*operands)
 
     def finish(stepped):

time: 33.6 us -> 33.1 us (0.985)
  waiting for transfers between devices: 5.66 us -> 4.55 us
  local copies, waits for them, and re-layouts: 0.33 us -> 0.98 us
  starting transfers between devices: 16.3 us -> 15.9 us
    pallas_call x3 -> x4, Pallas kernels: 4.35 us -> 5.74 us  [the longest x1 2.11 us: on_device(): pl.pallas_call(early_steps, out_shape=(shape_of(*state_shape), shape_of(l...]
    pallas_call x1, Pallas kernels: 2.79 us -> 1.87 us  [finish(): pl.pallas_call(later_steps, out_shape=shape_of(*fields.shape), in_specs=[...]
    reshape x1, local copies, waits for them, and re-layouts: 0.09 us -> 0.75 us  [far_field_weights(): view = angle_wave.reshape(far, near, per_block)]
    ppermute x1, waiting for transfers between devices: 2.23 us -> 1.67 us  [on_device(): lax.ppermute(message, 'ys', route)]
    ppermute x6, waiting for transfers between devices: 3.42 us -> 2.88 us  [across(): return lax.ppermute(block, 'xs', [(i, i ^ mask) for i in range(xs_size)])]
    ppermute x6, starting transfers between devices: 12.6 us -> 12.2 us  [across(): return lax.ppermute(block, 'xs', [(i, i ^ mask) for i in range(xs_size)])]
  transfers between devices with their start and end apart: 9 -> 9, of which waited for: 4 -> 3; matrix products, arithmetic and copies ran while one was open for 2% -> 4% of each run, Pallas kernels for 17% -> 19%
where the time goes in v5:
time: 33.1 us; the launch traced here: 32.9 us
  starting transfers between devices  15.9 us (48%)
  Pallas kernels  10.3 us (31%)
  waiting for transfers between devices  4.55 us (14%)
  local copies, waits for them, and re-layouts  0.98 us (3%)
  between operations  0.8 us (2%)
  other arithmetic  0.34 us (1%)
    ppermute x6, starting transfers between devices, across(): return lax.ppermute(block, 'xs', [(i, i ^ mask) for i in range(xs_size)])  12.2 us
    ppermute x6, waiting for transfers between devices, across(): return lax.ppermute(block, 'xs', [(i, i ^ mask) for i in range(xs_size)])  2.88 us
    ppermute x1, starting transfers between devices, on_device(): lax.ppermute(message, 'ys', route)  2.52 us
    pallas_call x1, Pallas kernels, on_device(): pl.pallas_call(early_steps, out_shape=(shape_of(*state_shape), shape_of(l...  2.11 us
    pallas_call x1, Pallas kernels, finish(): pl.pallas_call(later_steps, out_shape=shape_of(*fields.shape), in_specs=[...  1.87 us
    pallas_call x1, Pallas kernels, on_device(): pl.pallas_call(pack_y, out_shape=(shape_of(2, PARTS, cells_x, cells_y),)...  1.77 us
    ppermute x1, waiting for transfers between devices, on_device(): lax.ppermute(message, 'ys', route)  1.67 us
    pallas_call x1, Pallas kernels, on_device(): pl.pallas_call(functools.partial(surface_steps, n_adj=n_adj, n_rows=n_row...  1.54 us
  transfers between devices with their start and end apart: 9, of which 3 were waited for; matrix products, arithmetic and copies ran while one was open for 4% of the time, Pallas kernels for 19%

profile of v5, /device:TPU:0, one launch (start us, length us, event | category | flops | bytes accessed | tf_op | source)
XLA Modules:
  0.0 32.9 jit_solution(4294631311192826096)
XLA Ops:
  0.6 0.0 copy-start
  0.6 0.0 copy-start.1
  0.7 1.4 %pack_x_edges.1 = (f32[328,128]{1,0:T(8,128)S(1)}, f32[328,128]{1,0:T(8,128)S(1)}, f32[8,128]{1,0:T(8,128)S(1)}) custom-call(f32[6,16,32,128]{3,2,1,0:T(8,128)} %refs_0_.5, f32[16,32,128]{2,1,0:T(8,128)} %refs_1_.5, f32[4,128]{1,0:T(4,128)} %refs_2_.1, s32[4]{0:T(128)} %refs_3_.1, s32[4]{0:T(128)} %bitcast.8), custom_call_target="tpu_custom_call" | custom-call | tf_op jit(solution)/shard_map/pack_x_edges/pallas_call | solution.py:709
  2.1 0.5 %collective-permute-start = (f32[328,128]{1,0:T(8,128)S(1)}, f32[328,128]{1,0:T(8,128)S(1)}, u32[]{:S(2)}, u32[]{:S(2)}) collective-permute-start(f32[328,128]{1,0:T(8,128)S(1)} %get-tuple-element.24), channel_id=1, source_target_pairs={{0,2},{4,6},{8,10},{12,14},{16,18},{20,22},{24,26},{28,30},{2,0},{... | collective-permute-start | bytes 503816 | tf_op jit(solution)/shard_map/ppermute | solution.py:724
  2.6 0.7 %collective-permute-start.1 = (f32[328,128]{1,0:T(8,128)S(1)}, f32[328,128]{1,0:T(8,128)S(1)}, u32[]{:S(2)}, u32[]{:S(2)}) collective-permute-start(f32[328,128]{1,0:T(8,128)S(1)} %get-tuple-element.25), channel_id=1, source_target_pairs={{2,4},{6,8},{10,12},{14,16},{18,20},{22,24},{26,28},{4,2},{8,6},{1... | collective-permute-start | bytes 503816 | tf_op jit(solution)/shard_map/ppermute | solution.py:725
  3.3 0.7 %reshape.182 = s32[4,4,8]{2,1,0:T(4,128)S(1)} reshape(s32[128]{0:T(128)} %param.11) | data formatting | bytes 1024 | tf_op jit(solution)/shard_map/reshape | solution.py:608
  4.1 0.1 select_reduce_fusion
  4.2 0.0 copy-done
  4.2 0.0 copy-done.1
  4.2 1.8 %pack_y_edges.1 = (f32[2,7,32,128]{3,2,1,0:T(8,128)S(1)}, f32[144,128]{1,0:T(8,128)S(1)}) custom-call(f32[6,16,32,128]{3,2,1,0:T(8,128)S(1)} %copy-done, f32[16,32,128]{2,1,0:T(8,128)S(1)} %copy-done.1), custom_call_target="tpu_custom_call" | custom-call | tf_op jit(solution)/shard_map/pack_y_edges/pallas_call | solution.py:729
  6.0 0.0 collective-permute-done.refs_2_.refs_1_
  6.0 0.0 collective-permute-done.1.refs_3_.refs_2_
  6.0 0.3 pack_corners.1
  6.3 2.5 %collective-permute-start.2 = (f32[144,128]{1,0:T(8,128)S(1)}, f32[144,128]{1,0:T(8,128)S(1)}, u32[]{:S(2)}, u32[]{:S(2)}) collective-permute-start(f32[144,128]{1,0:T(8,128)S(1)} %pack_corners.1), channel_id=1, source_target_pairs={{0,1},{1,0},{2,3},{3,2},{4,5},{5,4},{6,7},{7,6},{8,9},{9,8},{10,11... | collective-permute-start | bytes 221192 | tf_op jit(solution)/shard_map/ppermute | solution.py:746
  8.8 0.1 add_add_fusion
  8.9 0.1 mul.71
  9.0 0.1 add.60
  9.1 0.4 %prepare_surface.1 = (f32[6,16,5,8,128]{4,3,2,1,0:T(8,128)S(1)}, f32[16,5,8,128]{3,2,1,0:T(8,128)S(1)}, f32[2,7,8,128]{3,2,1,0:T(8,128)S(1)}, f32[2,5,8,128]{3,2,1,0:T(8,128)S(1)}) custom-call(f32[6,16,32,128]{3,2,1,0:T(8,128)S(1)} %copy-done, f32[16,32,128]{2,1,0:T(8,128)S(1)} %copy-done.1, f32[328,128]{1,0:T(8,128)S(1)} %collective-permute-done.refs_2_.refs_1_, ...), custom_call_target="tpu_custom_call" | custom-call | tf_op jit(solution)/shard_map/prepare_surface/pallas_call | solution.py:755
  9.5 1.7 %collective-permute-done.2.refs_4_ = f32[144,128]{1,0:T(8,128)S(1)} collective-permute-done((f32[144,128]{1,0:T(8,128)S(1)}, f32[144,128]{1,0:T(8,128)S(1)}, u32[]{:S(2)}, u32[]{:S(2)}) %collective-permute-start.2) | collective-permute-done | bytes 73760 | tf_op jit(solution)/shard_map/ppermute | solution.py:746
  11.1 1.5 %surface_steps.1 = (f32[32,512]{1,0:T(8,128)S(1)}, f32[3,5,8,128]{3,2,1,0:T(8,128)S(1)}, f32[3,5,8,128]{3,2,1,0:T(8,128)S(1)}, f32[3,5,8,128]{3,2,1,0:T(8,128)S(1)}) custom-call(f32[6,16,5,8,128]{4,3,2,1,0:T(8,128)S(1)} %get-tuple-element.27.refs_0_, f32[16,5,8,128]{3,2,1,0:T(8,128)S(1)} %get-tuple-element.28.refs_1_, ...), custom_call_target="tpu_custom_call" | custom-call | tf_op jit(solution)/shard_map/surface_steps/pallas_call | solution.py:769
  12.7 7.2 %collective-permute-start.3 = (f32[32,512]{1,0:T(8,128)S(1)}, f32[32,512]{1,0:T(8,128)S(1)}, u32[]{:S(2)}, u32[]{:S(2)}) collective-permute-start(f32[32,512]{1,0:T(8,128)S(1)} %get-tuple-element.33.refs_0_), channel_id=1, source_target_pairs={{0,4},{2,6},{4,0},{6,2},{8,12},{10,14},{12,8},{14,10},{16,20},{18,... | collective-permute-start | bytes 196616 | tf_op jit(solution)/shard_map/ppermute | solution.py:631
  19.9 0.2 cosine_multiply_fusion
  20.0 0.1 collective-permute-start.4
  20.1 2.1 %early_steps.1 = (f32[6,18,5,8,128]{4,3,2,1,0:T(8,128)S(1)}, f32[16,5,8,128]{3,2,1,0:T(8,128)S(1)}) custom-call(f32[6,16,32,128]{3,2,1,0:T(8,128)S(1)} %copy-done, f32[16,32,128]{2,1,0:T(8,128)S(1)} %copy-done.1, f32[328,128]{1,0:T(8,128)S(1)} %collective-permute-done.refs_2_.refs_1_, f32[328,128]{1,0:T(8,128)S(1)} %collective-permute-done.1.refs_3_.refs_2_, ...), custom_call_target="tpu_custom_call" | custom-call | tf_op jit(solution)/shard_map/early_steps/pallas_call | solution.py:791
  22.2 0.0 collective-permute-done.3.refs_2_
  22.2 0.5 %collective-permute-start.5 = (f32[32,512]{1,0:T(8,128)S(1)}, f32[32,512]{1,0:T(8,128)S(1)}, u32[]{:S(2)}, u32[]{:S(2)}) collective-permute-start(f32[32,512]{1,0:T(8,128)S(1)} %collective-permute-done.3.refs_2_), channel_id=1, source_target_pairs={{0,2},{2,0},{4,6},{6,4},{8,10},{10,8},{12,14},{14,12},{16,18},{18,... | collective-permute-start | bytes 196616 | tf_op jit(solution)/shard_map/ppermute | solution.py:631
  22.8 0.0 collective-permute-done.4.refs_1_
  22.8 0.9 %collective-permute-done.5.refs_3_ = f32[32,512]{1,0:T(8,128)S(1)} collective-permute-done((f32[32,512]{1,0:T(8,128)S(1)}, f32[32,512]{1,0:T(8,128)S(1)}, u32[]{:S(2)}, u32[]{:S(2)}) %collective-permute-start.5) | collective-permute-done | bytes 65568 | tf_op jit(solution)/shard_map/ppermute | solution.py:631
  23.7 0.3 partial_spectrum.1
  23.9 3.5 %collective-permute-start.6 = (f32[16,512]{1,0:T(8,128)S(1)}, f32[16,512]{1,0:T(8,128)S(1)}, u32[]{:S(2)}, u32[]{:S(2)}) collective-permute-start(f32[16,512]{1,0:T(8,128)S(1)} %get-tuple-element.43), channel_id=1, source_target_pairs={{0,24},{2,26},{4,28},{6,30},{8,16},{10,18},{12,20},{14,22},{16,8},... | collective-permute-start | bytes 98312 | tf_op jit(solution)/shard_map/ppermute | solution.py:631
  27.5 0.0 collective-permute-start.7
  27.5 0.9 %collective-permute-start.8 = (f32[16,512]{1,0:T(8,128)S(1)}, f32[16,512]{1,0:T(8,128)S(1)}, u32[]{:S(2)}, u32[]{:S(2)}) collective-permute-start(f32[16,512]{1,0:T(8,128)S(1)} %get-tuple-element.45), channel_id=1, source_target_pairs={{0,8},{2,10},{4,12},{6,14},{8,0},{10,2},{12,4},{14,6},{16,24},{18,... | collective-permute-start | bytes 98312 | tf_op jit(solution)/shard_map/ppermute | solution.py:631
  28.4 1.9 %later_steps.1 = f32[6,16,32,128]{3,2,1,0:T(8,128)} custom-call(f32[6,18,5,8,128]{4,3,2,1,0:T(8,128)S(1)} %get-tuple-element.39.refs_0_, f32[16,5,8,128]{3,2,1,0:T(8,128)S(1)} %get-tuple-element.40.refs_1_, f32[3,5,8,128]{3,2,1,0:T(8,128)S(1)} %get-tuple-element.34.refs_4_.refs_2_, f32[3,5,8,128]{3,2,1,0:T(8,128)S(1)} %get-tuple-element.35.refs_5_.refs_3_, ...), custom_call_target="tpu_custom_call" | custom-call | tf_op jit(solution)/shard_map/later_steps/pallas_call | solution.py:805
  30.3 0.0 collective-permute-done.6.refs_1_
  30.3 2.0 %collective-permute-done.7.refs_2_ = f32[16,512]{1,0:T(8,128)S(1)} collective-permute-done((f32[16,512]{1,0:T(8,128)S(1)}, f32[16,512]{1,0:T(8,128)S(1)}, u32[]{:S(2)}, u32[]{:S(2)}) %collective-permute-start.7) | collective-permute-done | bytes 32800 | tf_op jit(solution)/shard_map/ppermute | solution.py:631
  32.3 0.0 collective-permute-done.8.refs_3_
  32.3 0.6 %add_arrived.1 = f32[16,4,128]{2,1,0:T(4,128)} custom-call(f32[16,512]{1,0:T(8,128)S(1)} %get-tuple-element.42.refs_0_, f32[16,512]{1,0:T(8,128)S(1)} %collective-permute-done.6.refs_1_, f32[16,512]{1,0:T(8,128)S(1)} %collective-permute-done.7.refs_2_, f32[16,512]{1,0:T(8,128)S(1)} %collective-permute-done.8.refs_3_), custom_call_target="tpu_custom_call" | custom-call | tf_op jit(solution)/shard_map/add_arrived/pallas_call | solution.py:649
  (7 shorter events, 0.1 us)
Async XLA Ops:
  0.6 3.6 %copy-start = (f32[6,16,32,128]{3,2,1,0:T(8,128)S(1)}, f32[6,16,32,128]{3,2,1,0:T(8,128)}, u32[]{:S(2)}) copy-start(f32[6,16,32,128]{3,2,1,0:T(8,128)} %refs_0_.5) | copy-start | bytes 4718596
  0.6 3.6 %copy-start.1 = (f32[16,32,128]{2,1,0:T(8,128)S(1)}, f32[16,32,128]{2,1,0:T(8,128)}, u32[]{:S(2)}) copy-start(f32[16,32,128]{2,1,0:T(8,128)} %refs_1_.5) | copy-start | bytes 786436
  2.1 3.9 %collective-permute-start = (f32[328,128]{1,0:T(8,128)S(1)}, f32[328,128]{1,0:T(8,128)S(1)}, u32[]{:S(2)}, u32[]{:S(2)}) collective-permute-start(f32[328,128]{1,0:T(8,128)S(1)} %get-tuple-element.24), channel_id=1, source_target_pairs={{0,2},{4,6},{8,10},{12,14},{16,18},{20,22},{24,26},{28,30},{2,0},{... | collective-permute-start | bytes 503816 | tf_op jit(solution)/shard_map/ppermute | solution.py:724
  2.6 3.4 %collective-permute-start.1 = (f32[328,128]{1,0:T(8,128)S(1)}, f32[328,128]{1,0:T(8,128)S(1)}, u32[]{:S(2)}, u32[]{:S(2)}) collective-permute-start(f32[328,128]{1,0:T(8,128)S(1)} %get-tuple-element.25), channel_id=1, source_target_pairs={{2,4},{6,8},{10,12},{14,16},{18,20},{22,24},{26,28},{4,2},{8,6},{1... | collective-permute-start | bytes 503816 | tf_op jit(solution)/shard_map/ppermute | solution.py:725
  6.3 4.9 %collective-permute-start.2 = (f32[144,128]{1,0:T(8,128)S(1)}, f32[144,128]{1,0:T(8,128)S(1)}, u32[]{:S(2)}, u32[]{:S(2)}) collective-permute-start(f32[144,128]{1,0:T(8,128)S(1)} %pack_corners.1), channel_id=1, source_target_pairs={{0,1},{1,0},{2,3},{3,2},{4,5},{5,4},{6,7},{7,6},{8,9},{9,8},{10,11... | collective-permute-start | bytes 221192 | tf_op jit(solution)/shard_map/ppermute | solution.py:746
  12.7 9.5 %collective-permute-start.3 = (f32[32,512]{1,0:T(8,128)S(1)}, f32[32,512]{1,0:T(8,128)S(1)}, u32[]{:S(2)}, u32[]{:S(2)}) collective-permute-start(f32[32,512]{1,0:T(8,128)S(1)} %get-tuple-element.33.refs_0_), channel_id=1, source_target_pairs={{0,4},{2,6},{4,0},{6,2},{8,12},{10,14},{12,8},{14,10},{16,20},{18,... | collective-permute-start | bytes 196616 | tf_op jit(solution)/shard_map/ppermute | solution.py:631
  20.0 2.8 %collective-permute-start.4 = (f32[32,512]{1,0:T(8,128)S(1)}, f32[32,512]{1,0:T(8,128)S(1)}, u32[]{:S(2)}, u32[]{:S(2)}) collective-permute-start(f32[32,512]{1,0:T(8,128)S(1)} %get-tuple-element.33.refs_0_), channel_id=1, source_target_pairs={{0,2},{2,0},{4,6},{6,4},{8,10},{10,8},{12,14},{14,12},{16,18},{18,... | collective-permute-start | bytes 196616 | tf_op jit(solution)/shard_map/ppermute | solution.py:631
  22.2 1.4 %collective-permute-start.5 = (f32[32,512]{1,0:T(8,128)S(1)}, f32[32,512]{1,0:T(8,128)S(1)}, u32[]{:S(2)}, u32[]{:S(2)}) collective-permute-start(f32[32,512]{1,0:T(8,128)S(1)} %collective-permute-done.3.refs_2_), channel_id=1, source_target_pairs={{0,2},{2,0},{4,6},{6,4},{8,10},{10,8},{12,14},{14,12},{16,18},{18,... | collective-permute-start | bytes 196616 | tf_op jit(solution)/shard_map/ppermute | solution.py:631
  23.9 6.3 %collective-permute-start.6 = (f32[16,512]{1,0:T(8,128)S(1)}, f32[16,512]{1,0:T(8,128)S(1)}, u32[]{:S(2)}, u32[]{:S(2)}) collective-permute-start(f32[16,512]{1,0:T(8,128)S(1)} %get-tuple-element.43), channel_id=1, source_target_pairs={{0,24},{2,26},{4,28},{6,30},{8,16},{10,18},{12,20},{14,22},{16,8},... | collective-permute-start | bytes 98312 | tf_op jit(solution)/shard_map/ppermute | solution.py:631
  27.5 4.8 %collective-permute-start.7 = (f32[16,512]{1,0:T(8,128)S(1)}, f32[16,512]{1,0:T(8,128)S(1)}, u32[]{:S(2)}, u32[]{:S(2)}) collective-permute-start(f32[16,512]{1,0:T(8,128)S(1)} %get-tuple-element.44), channel_id=1, source_target_pairs={{0,16},{2,18},{4,20},{6,22},{8,24},{10,26},{12,28},{14,30},{16,0},... | collective-permute-start | bytes 98312 | tf_op jit(solution)/shard_map/ppermute | solution.py:631
  27.5 4.8 %collective-permute-start.8 = (f32[16,512]{1,0:T(8,128)S(1)}, f32[16,512]{1,0:T(8,128)S(1)}, u32[]{:S(2)}, u32[]{:S(2)}) collective-permute-start(f32[16,512]{1,0:T(8,128)S(1)} %get-tuple-element.45), channel_id=1, source_target_pairs={{0,8},{2,10},{4,12},{6,14},{8,0},{10,2},{12,4},{14,6},{16,24},{18,... | collective-permute-start | bytes 98312 | tf_op jit(solution)/shard_map/ppermute | solution.py:631

commit v6 on v5

--- a/solution.py
+++ b/solution.py
@@ -24,6 +24,7 @@
 Y_GROUPS = ((0, 2, 4), (1, 3, 6), (5,))
 TOGETHER = 8
 EARLY = 2
+NEAR = 4
 
 VMEM = pl.BlockSpec(memory_space=pltpu.VMEM)
 ANY = pl.BlockSpec(memory_space=pl.ANY)
@@ -42,9 +43,25 @@
     found = []
     for first in (0, 1):
         pairs = [(i, i + 1) for i in range(first, size - 1, 2)]
+        if first and size > 2 and size % 2 == 0:
+            pairs.append((size - 1, 0))
         if pairs:
             found.append(pairs + [(j, i) for i, j in pairs])
     return found
+
+
+def odd_route(xs_size, ys_size, y_route):
+    ends = [0] + ([xs_size - 1] if xs_size % 2 == 0 else [])
+    pairs = [(i, i + 1) for i in range(1, xs_size - 1, 2)]
+    pairs += [(j, i) for i, j in pairs]
+    route = [(a * ys_size + s, b * ys_size + t) for a, b in pairs for s, t in y_route]
+    near = swaps(ys_size)[0]
+    return route + [(e * ys_size + s, e * ys_size + t) for e in ends for s, t in near]
+
+
+def at_end(axis):
+    index = lax.axis_index(axis)
+    return (index == 0) | (index == lax.axis_size(axis) - 1)
 
 
 def x_message_rows(layers):
@@ -56,7 +73,7 @@
     slot = X_GROUPS[group].index(c)
     tile = 2 * z + group if group < 2 else 2 * layers + z // 2
     at = pl.ds(tile * TILE if isinstance(z, int) else pl.multiple_of(tile * TILE, TILE), TILE)
-    from_even, from_odd = even[at, :], odd[at, :]
+    from_even, from_odd = even[at, :], jnp.where(at_end("xs"), 0.0, odd[at, :])
     after = jnp.where(px == 0, from_even, from_odd)
     before = jnp.where(px == 0, from_odd, from_even)
     lower = rows_of(after.shape) < REACH
@@ -113,13 +130,16 @@
         send(2 * layers + pair, jnp.where(row < REACH, a, b))
 
 
-def pack_x(*refs, n_adj):
+def pack_x(*refs, n_adj, n_swaps):
     fields, permittivity = refs[:2]
     if n_adj:
         values, rows, owners, to_even, to_odd, blocks = refs[2:8]
-        edges, edge_perm, rows_s, owners_s, sems = refs[8:]
+        to_diag = refs[8 : 8 + n_swaps]
+        edges, edge_perm, rows_s, owners_s, sems = refs[8 + n_swaps :]
     else:
-        to_even, to_odd, edges, edge_perm, sems = refs[2:]
+        to_even, to_odd = refs[2:4]
+        to_diag = refs[4 : 4 + n_swaps]
+        edges, edge_perm, sems = refs[4 + n_swaps :]
     px = lax.axis_index("xs") % 2
     layers, cells_x = fields.shape[1:3]
     copies = []
@@ -147,6 +167,21 @@
 
     pl.when(px == 0)(lambda: pack(to_odd, to_even))
     pl.when(px == 1)(lambda: pack(to_even, to_odd))
+
+    def pack_corner(message, k, to_next):
+        for g, parts in enumerate(Y_GROUPS):
+            packed = [
+                pack_strip(lambda z: edge_of(k)(c, z), layers, 5 if to_next else 3) for c in parts
+            ]
+            message[g * TILE : (g + 1) * TILE, :] = pack_group(packed, to_next)
+
+    for swap, message in enumerate(to_diag):
+        is_next = lax.axis_index("ys") % 2 == swap
+        for k in (0, 1):
+            for to_next in (False, True):
+                pl.when((px == k) & (is_next == to_next))(
+                    functools.partial(pack_corner, message, k, to_next)
+                )
     if n_adj:
         for b in range(n_adj):
             code = rows_s[b] + cells_x * owners_s[b]
@@ -155,6 +190,7 @@
             ).astype(jnp.float32)
         to_even[x_message_rows(layers) :, :] = blocks[...]
         to_odd[x_message_rows(layers) :, :] = blocks[...]
+        to_diag[0][len(Y_GROUPS) * TILE :, :] = blocks[...]
 
 
 def pack_strip(tile_of, layers, shift):
@@ -187,58 +223,43 @@
     return (pltpu.roll(before, lower, 1) if lower else before), pltpu.roll(after, upper, 1)
 
 
-def pack_y(fields, permittivity, strips, *to_y):
+def pack_y(fields, permittivity, even, *refs, n_rows):
+    blocks, refs = (refs[0], refs[1:]) if n_rows else (None, refs)
+    strips, *to_y = refs
     layers, cells_x, width = fields.shape[1:]
     ring = cells_x + TILE
-    for r in range(cells_x // TILE):
-        rows = slice(r * TILE, (r + 1) * TILE)
-        for g, parts in enumerate(Y_GROUPS):
-            packed = []
-            for c in parts:
-
-                def tile_of(z):
-                    return fields[c, z, rows, :] if c < 6 else time_step / permittivity[z, rows, :]
-
-                packed.append(pack_strips(tile_of, layers))
-                for side in (0, 1):
-                    strips[side, c, rows, :] = packed[-1][side]
-            for swap, message in enumerate(to_y):
-                to_next = lax.axis_index("ys") % 2 == swap
+    px = lax.axis_index("xs") % 2
+
+    def fill(message, to_next):
+        for r in range(ring // TILE):
+            rows = slice(r * TILE, (r + 1) * TILE)
+            for g, parts in enumerate(Y_GROUPS):
+                packed = []
+                for c in parts:
+
+                    def tile_of(z):
+                        if r * TILE == cells_x:
+                            return halo_tile(even, even, px, c, z, layers)
+                        return own_tile(fields, permittivity, c, z, rows)
+
+                    packed.append(pack_strip(tile_of, layers, 5 if to_next else 3))
+                    if r * TILE < cells_x:
+                        strips[int(to_next), c, rows, :] = packed[-1]
                 at = slice(g * ring + r * TILE, g * ring + (r + 1) * TILE)
-                message[at, :] = jnp.where(
-                    to_next,
-                    pack_group([p[1] for p in packed], True),
-                    pack_group([p[0] for p in packed], False),
-                )
-
-
-def pack_corners(*refs, layers, n_rows, n_swaps):
-    even, odd = refs[n_swaps : 2 + n_swaps]
-    to_y = refs[-n_swaps:]
-    px = lax.axis_index("xs") % 2
-    ring = (to_y[0].shape[0] - 3 * n_rows) // len(Y_GROUPS)
-
-    def fill(message, to_next):
-        for g, parts in enumerate(Y_GROUPS):
-            packed = [
-                pack_strip(
-                    lambda z: halo_tile(even, odd, px, c, z, layers), layers, 5 if to_next else 3
-                )
-                for c in parts
-            ]
-            message[(g + 1) * ring - TILE : (g + 1) * ring, :] = pack_group(packed, to_next)
+                message[at, :] = pack_group(packed, to_next)
 
     for swap, message in enumerate(to_y):
         is_next = lax.axis_index("ys") % 2 == swap
         for to_next in (False, True):
             pl.when(is_next == to_next)(functools.partial(fill, message, to_next))
     if n_rows:
-        blocks = refs[2 + n_swaps]
         end = len(Y_GROUPS) * ring
-        x_end = x_message_rows(layers)
         to_y[0][end : end + n_rows, :] = blocks[...]
-        to_y[0][end + n_rows : end + 2 * n_rows, :] = even[x_end:, :]
-        to_y[0][end + 2 * n_rows : end + 3 * n_rows, :] = odd[x_end:, :]
+        to_y[0][end + n_rows : end + 2 * n_rows, :] = even[x_message_rows(layers) :, :]
+
+
+def own_tile(fields, permittivity, c, z, rows):
+    return fields[c, z, rows, :] if c < 6 else time_step / permittivity[z, rows, :]
 
 
 def row_index(shape):
@@ -310,7 +331,7 @@
     return jnp.where(outside, 0.0, time_step)
 
 
-def evolve_strips(strips, halo_strips, y_halos, source, strip, edge_e, edge_h):
+def evolve_strips(strips, halo_strips, y_halos, diag_halos, source, strip, edge_e, edge_h):
     me = lax.axis_index("ys")
     ring, width = strips.shape[2] + TILE, strips.shape[3]
     fold = ring // TILE
@@ -319,8 +340,14 @@
         for r in range(fold):
             before, after = zeros((TILE, width)), zeros((TILE, width))
             at = g * ring + r * TILE
-            for k, y_ref in enumerate(y_halos):
+            for k, (y_ref, d_ref) in enumerate(zip(y_halos, diag_halos)):
                 block = y_ref[at : at + TILE, :]
+                if r + 1 == fold:
+                    odd_half = (rows_of(block.shape) >= REACH) == (lax.axis_index("xs") % 2 == 0)
+                    corner = jnp.where(at_end("xs"), 0.0, d_ref[g * TILE : (g + 1) * TILE, :])
+                    block = jnp.where(odd_half, corner, block)
+                if k:
+                    block = jnp.where(at_end("ys"), 0.0, block)
                 is_next = me % 2 == k
                 after = jnp.where(is_next, block, after)
                 before = jnp.where(is_next, before, block)
@@ -366,14 +393,28 @@
     return range(max(ZS - STEPS, 0), min(ZS + STEPS + 1, layers))
 
 
-def prepare_surface(*refs, n_adj, n_rows):
-    fields, permittivity, even, odd = refs[:4]
-    state, coeffs, halo_strips = refs[4 + bool(n_adj) : 7 + bool(n_adj)]
-    rows = refs[-1]
+def prepare_surface(*refs, n_adj, n_rows, n_swaps):
+    fields, permittivity, even, odd, angle_wave = refs[1:6]
+    strips, state, coeffs, halo_strips, angles = refs[6 + bool(n_adj) : 11 + bool(n_adj)]
+    rows, angles_s, sem = refs[-3:]
+    fetch = pltpu.make_async_copy(angle_wave, angles_s, sem)
+    fetch.start()
     px = lax.axis_index("xs") % 2
     layers, cells_x, width = fields.shape[1:]
     ring = cells_x + TILE
     fold = ring // TILE
+
+    def fill(side):
+        for c in range(PARTS):
+            for r in range(cells_x // TILE):
+                at = slice(r * TILE, (r + 1) * TILE)
+                strips[side, c, at, :] = pack_strip(
+                    lambda z: own_tile(fields, permittivity, c, z, at), layers, 5 if side else 3
+                )
+
+    if n_swaps == 1:
+        for side in (0, 1):
+            pl.when(lax.axis_index("ys") % 2 == side)(functools.partial(fill, side))
     for c in range(PARTS):
         halos = [halo_tile(even, odd, px, c, z, layers) for z in range(layers)]
         for side, tile in enumerate(pack_strips(lambda z: halos[z], layers)):
@@ -387,17 +428,24 @@
             else:
                 coeffs[z] = folded
     if n_adj:
-        blocks, totals = refs[4], refs[8]
+        blocks, totals = refs[6], refs[12]
         totals[...] = zeros(totals.shape)
         end = x_message_rows(layers)
-        sets = [(blocks, 0, None), (even, end, px == 0), (odd, end, px == 1)]
+        rows[0, 0, 0:n_rows, :] = jnp.where(at_end("xs"), 0.0, odd[end:, :])
+        sets = [(blocks, 0, None), (even, end, px == 0), (rows.at[0, 0], 0, px == 1)]
         gather_sources(sets, px, lax.axis_index("ys"), totals, n_adj, cells_x)
+    fetch.wait()
+    per_block = angle_wave.shape[0] // lax.axis_size("xs")
+    for k in range(angles.shape[0]):
+        owner = lax.axis_index("xs") ^ (k // per_block * NEAR)
+        one = angles_s[owner * per_block + k % per_block]
+        angles[k : k + 1, :] = jnp.full((1, angles.shape[1]), one, jnp.int32)
 
 
 def surface_steps(*refs, n_adj, n_rows, n_swaps):
     before, coeffs, halo_strips, strips = refs[:4]
-    y_halos, given = refs[4 : 4 + n_swaps], refs[4 + n_swaps]
-    out, source, edge_e, edge_h, rows, state, strip, totals = refs[5 + n_swaps :]
+    y_halos, diag_halos = refs[4 : 4 + n_swaps], refs[4 + n_swaps : 4 + 2 * n_swaps]
+    given, out, source, edge_e, edge_h, rows, state, strip, totals = refs[4 + 2 * n_swaps :]
     px = lax.axis_index("xs") % 2
     me = lax.axis_index("ys")
     layers = before.shape[1]
@@ -411,14 +459,16 @@
         sets = [
             (y_halos[0], end, None),
             (y_halos[0], end + n_rows, px == 0),
-            (y_halos[0], end + 2 * n_rows, px == 1),
+            (rows.at[0], 0, px == 1),
         ]
+        corner_rows = diag_halos[0][len(Y_GROUPS) * TILE :, :]
+        rows[0, 0:n_rows, :] = jnp.where(at_end("xs"), 0.0, corner_rows)
         totals[...] = given[...]
         gather_sources(sets, px, me, totals, n_adj, cells_x)
         place_sources(totals, me, source)
     else:
         source[...] = given[...]
-    evolve_strips(strips, halo_strips, y_halos, source, strip, edge_e, edge_h)
+    evolve_strips(strips, halo_strips, y_halos, diag_halos, source, strip, edge_e, edge_h)
 
     dt = step_size(full)
     for step in range(STEPS):
@@ -600,32 +650,19 @@
     return jax.ShapeDtypeStruct(dims, jnp.float32)
 
 
-def far_field_weights(angle_wave, xs_size, cells_x, near):
-    me = lax.axis_index("xs")
-    per_block = angle_wave.shape[0] // xs_size
-    far = xs_size // near
-    bits = far.bit_length() - 1
-    view = angle_wave.reshape(far, near, per_block)
-    pick = jnp.arange(near, dtype=jnp.int32)[None, :, None] == me % near
-    view = jnp.sum(jnp.where(pick, view, 0), axis=1).reshape((2,) * bits + (per_block,))
-    for k in range(bits):
-        bit = (me // near >> (bits - 1 - k)) & 1
-        view = jnp.where(bit == 1, jnp.flip(view, k), view)
-    angles = view.reshape(-1)
-    owners = me ^ jnp.arange(near, dtype=jnp.int32)
-    within = jnp.arange(cells_x, dtype=jnp.int32)
-    positions = X0 + (owners[:, None] * cells_x + within[None, :]).reshape(-1)
-    phase = angles[:, None] * positions[None, :] % GRID_X
+def far_field_weights(angles, xs_size, cells_x):
+    column = jnp.arange(NEAR * cells_x, dtype=jnp.int32)
+    owner = lax.axis_index("xs") ^ (column // cells_x)
+    phase = angles * (X0 + owner * cells_x + column % cells_x)[None, :] % GRID_X
     angle = phase.astype(jnp.float32) * (2.0 * math.pi / GRID_X)
     scale = 1.0 / math.sqrt(cells_x * xs_size)
     both = jnp.stack([jnp.cos(angle) * scale, -jnp.sin(angle) * scale], axis=1)
-    return both.reshape(-1, near * cells_x)
-
-
-def far_field_exchange(tile, angle_wave, xs_size, beside, finish):
+    return both.reshape(-1, NEAR * cells_x)
+
+
+def far_field_exchange(tile, angles, xs_size, beside, finish):
     cells_x, columns = tile.shape
-    near = 4
-    weights = far_field_weights(angle_wave, xs_size, cells_x, near)
+    weights = far_field_weights(angles, xs_size, cells_x)
 
     def across(block, mask):
         return lax.ppermute(block, "xs", [(i, i ^ mask) for i in range(xs_size)])
@@ -634,17 +671,17 @@
     second = across(tile, 1)
     third, beside = lax.optimization_barrier((third, beside))
     fourth = across(third, 1)
-    far = xs_size // near
+    far = xs_size // NEAR
     rows = weights.shape[0] // far
     parts = pl.pallas_call(
-        functools.partial(multiply, n_tiles=near),
+        functools.partial(multiply, n_tiles=NEAR),
         out_shape=(shape_of(rows, columns),) * far,
-        in_specs=[VMEM] * (near + 1),
+        in_specs=[VMEM] * (NEAR + 1),
         out_specs=(VMEM,) * far,
         compiler_params=PARAMS,
         name="partial_spectrum",
     )(weights, tile, second, third, fourth)
-    arrived = [across(parts[k], k * near) for k in range(far - 1, 0, -1)]
+    arrived = [across(parts[k], k * NEAR) for k in range(far - 1, 0, -1)]
     finished = finish(beside)
     far_field = pl.pallas_call(
         add_parts,
@@ -702,15 +739,19 @@
     n_rows = -(-2 * n_adj // TILE) * TILE
     ring = cells_x + TILE
     x_rows = x_message_rows(layers) + n_rows
-    y_rows = len(Y_GROUPS) * ring + 3 * n_rows
+    y_rows = len(Y_GROUPS) * ring + 2 * n_rows
+    d_rows = len(Y_GROUPS) * TILE + n_rows
+    y_swaps = swaps(ys_size)
 
     extra = (adj_values, adj_row, adj_owner.reshape(-1)) if raw else ()
     x_message = shape_of(x_rows, cells_y)
-    to_even, to_odd, *blocks = pl.pallas_call(
-        functools.partial(pack_x, n_adj=n_adj),
-        out_shape=(x_message,) * 2 + ((shape_of(n_rows, cells_y),) if raw else ()),
+    made = (x_message,) * 2 + ((shape_of(n_rows, cells_y),) if raw else ())
+    made += (shape_of(d_rows, cells_y),) * len(y_swaps)
+    to_even, to_odd, *packed = pl.pallas_call(
+        functools.partial(pack_x, n_adj=n_adj, n_swaps=len(y_swaps)),
+        out_shape=made,
         in_specs=[ANY] * (2 + len(extra)),
-        out_specs=(VMEM,) * (3 if raw else 2),
+        out_specs=(VMEM,) * len(made),
         scratch_shapes=[
             pltpu.VMEM((2, 6, layers, TILE, cells_y), jnp.float32),
             pltpu.VMEM((2, layers, TILE, cells_y), jnp.float32),
@@ -720,52 +761,66 @@
         compiler_params=PARAMS,
         name="pack_x_edges",
     )(*[pltpu.with_memory_space_constraint(x, pltpu.HBM) for x in (fields, permittivity, *extra)])
-    x_even, x_odd = swaps(xs_size)
-    from_even = lax.ppermute(to_even, "xs", x_even)
-    from_odd = lax.ppermute(to_odd, "xs", x_odd)
-
-    y_swaps = swaps(ys_size)
-    messages = (shape_of(y_rows, cells_y),) * len(y_swaps)
+    blocks, to_diag = (packed[:1], packed[1:]) if raw else ([], packed)
+    both = ("xs", "ys")
+    from_even = lax.ppermute(to_even, "xs", swaps(xs_size)[0])
+    straight = odd_route(xs_size, ys_size, [(i, i) for i in range(ys_size)])
+    from_odd = lax.ppermute(to_odd, both, straight)
+    diag_halos = [
+        lax.ppermute(message, both, odd_route(xs_size, ys_size, route))
+        for message, route in zip(to_diag, y_swaps)
+    ]
+
+    made = (shape_of(2, PARTS, cells_x, cells_y),) + (shape_of(y_rows, cells_y),) * len(y_swaps)
     strips, *to_y = pl.pallas_call(
-        pack_y,
-        out_shape=(shape_of(2, PARTS, cells_x, cells_y),) + messages,
-        in_specs=[VMEM] * 2,
-        out_specs=(VMEM,) * (1 + len(messages)),
+        functools.partial(pack_y, n_rows=n_rows),
+        out_shape=made,
+        in_specs=[VMEM] * (3 + len(blocks)),
+        out_specs=(VMEM,) * len(made),
         compiler_params=PARAMS,
         name="pack_y_edges",
-    )(fields, permittivity)
-    to_y = pl.pallas_call(
-        functools.partial(pack_corners, layers=layers, n_rows=n_rows, n_swaps=len(y_swaps)),
-        out_shape=messages,
-        in_specs=[VMEM] * (len(messages) + 2 + len(blocks)),
-        out_specs=(VMEM,) * len(messages),
-        input_output_aliases={k: k for k in range(len(messages))},
-        compiler_params=PARAMS,
-        name="pack_corners",
-    )(*to_y, from_even, from_odd, *blocks)
+    )(fields, permittivity, from_even, *blocks)
     y_halos = [lax.ppermute(message, "ys", route) for message, route in zip(to_y, y_swaps)]
 
     fold = ring // TILE
     folded = (fold, TILE, cells_y)
+    n_angles = angle_wave.shape[0] // NEAR
     made = (
+        strips,
         shape_of(6, layers, *folded),
         shape_of(layers, *folded),
         shape_of(2, PARTS, TILE, cells_y),
+        jax.ShapeDtypeStruct((n_angles, NEAR * cells_x), jnp.int32),
     ) + ((shape_of(2, *folded),) if raw else ())
     prepared = pl.pallas_call(
-        functools.partial(prepare_surface, n_adj=n_adj, n_rows=n_rows),
-        out_shape=made,
-        in_specs=[VMEM] * (4 + len(blocks)),
+        functools.partial(prepare_surface, n_adj=n_adj, n_rows=n_rows, n_swaps=len(y_swaps)),
+        out_shape=[jax.ShapeDtypeStruct(x.shape, x.dtype) for x in made],
+        in_specs=[VMEM] * 5 + [ANY] + [VMEM] * len(blocks),
+        input_output_aliases={0: 0},
         out_specs=(VMEM,) * len(made),
-        scratch_shapes=[pltpu.VMEM((PARTS, layers, ring, cells_y), jnp.float32)],
+        scratch_shapes=[
+            pltpu.VMEM((PARTS, layers, ring, cells_y), jnp.float32),
+            pltpu.SMEM(angle_wave.shape, jnp.int32),
+            pltpu.SemaphoreType.DMA(()),
+        ],
         compiler_params=PARAMS,
         name="prepare_surface",
-    )(fields, permittivity, from_even, from_odd, *blocks)
+    )(
+        strips,
+        fields,
+        permittivity,
+        from_even,
+        from_odd,
+        pltpu.with_memory_space_constraint(angle_wave, pltpu.HBM),
+        *blocks,
+    )
+    strips, *prepared = prepared
+    angles = prepared[3]
     if raw:
-        sources = prepared[3:]
+        sources = prepared[4:]
     else:
         sources = (gathered_sources(adj_values, adj_owner, adj_row, cells_x, cells_y),)
-    operands = (*prepared[:3], strips, *y_halos, *sources)
+    operands = (*prepared[:3], strips, *y_halos, *diag_halos, *sources)
     tile, *carried = pl.pallas_call(
         functools.partial(surface_steps, n_adj=n_adj, n_rows=n_rows, n_swaps=len(y_swaps)),
         out_shape=(
@@ -816,7 +871,7 @@
             name="later_steps",
         )(*stepped, *carried)
 
-    far, new_fields = far_field_exchange(tile, angle_wave, xs_size, stepped, finish)
+    far, new_fields = far_field_exchange(tile, angles, xs_size, stepped, finish)
     per_block = angle_wave.shape[0] // xs_size
     return (new_fields, far.reshape(per_block, 2, 4, cells_y))
 

time: 33.1 us -> 30 us (0.906)
  starting transfers between devices: 15.9 us -> 13.4 us
  local copies, waits for them, and re-layouts: 0.98 us -> 0.04 us
  waiting for transfers between devices: 4.55 us -> 4.99 us
    ppermute x6, starting transfers between devices: 12.2 us -> 8.28 us  [across(): return lax.ppermute(block, 'xs', [(i, i ^ mask) for i in range(xs_size)])]
    ppermute x2 -> x3, starting transfers between devices: 1.18 us -> 3.14 us  [the longest x1 2.53 us: on_device(): from_odd = lax.ppermute(to_odd, both, straight)]
    reshape x1 -> x0, local copies, waits for them, and re-layouts: 0.75 us -> none  [far_field_weights(): view = angle_wave.reshape(far, near, per_block)]
    pallas_call x1, Pallas kernels: 0.42 us -> 1.01 us  [on_device(): pl.pallas_call(functools.partial(prepare_surface, n_adj=n_adj, n_rows=n_r...]
    ppermute x1, starting transfers between devices: 2.52 us -> 1.96 us  [on_device(): lax.ppermute(message, 'ys', route)]
    ppermute x6, waiting for transfers between devices: 2.88 us -> 3.23 us  [across(): return lax.ppermute(block, 'xs', [(i, i ^ mask) for i in range(xs_size)])]
    pallas_call x4 -> x3, Pallas kernels: 3.74 us -> 3.5 us  [the longest x1 1.7 us: on_device(): pl.pallas_call(functools.partial(pack_x, n_adj=n_adj, n_swaps=len(y_swaps...]
  transfers between devices with their start and end apart: 9 -> 10, of which waited for: 3 -> 4; matrix products, arithmetic and copies ran while one was open for 4% -> 0% of each run, Pallas kernels for 19% -> 22%
where the time goes in v6:
time: 30 us; the launch traced here: 29.9 us
  starting transfers between devices  13.4 us (45%)
  Pallas kernels  10.6 us (35%)
  waiting for transfers between devices  4.99 us (17%)
  between operations  0.74 us (2%)
    ppermute x6, starting transfers between devices, across(): return lax.ppermute(block, 'xs', [(i, i ^ mask) for i in range(xs_size)])  8.28 us
    ppermute x6, waiting for transfers between devices, across(): return lax.ppermute(block, 'xs', [(i, i ^ mask) for i in range(xs_size)])  3.23 us
    ppermute x1, starting transfers between devices, on_device(): from_odd = lax.ppermute(to_odd, both, straight)  2.53 us
    pallas_call x1, Pallas kernels, on_device(): pl.pallas_call(early_steps, out_shape=(shape_of(*state_shape), shape_of(l...  2.11 us
    ppermute x1, starting transfers between devices, on_device(): lax.ppermute(message, 'ys', route)  1.96 us
    pallas_call x1, Pallas kernels, finish(): pl.pallas_call(later_steps, out_shape=shape_of(*fields.shape), in_specs=[...  1.87 us
    ppermute x1, waiting for transfers between devices, on_device(): lax.ppermute(message, 'ys', route)  1.76 us
    pallas_call x1, Pallas kernels, on_device(): pl.pallas_call(functools.partial(pack_x, n_adj=n_adj, n_swaps=len(y_swaps...  1.7 us
  transfers between devices with their start and end apart: 10, of which 4 were waited for; matrix products, arithmetic and copies ran while one was open for 0% of the time, Pallas kernels for 22%

profile of v6, /device:TPU:0, one launch (start us, length us, event | category | flops | bytes accessed | tf_op | source)
XLA Modules:
  0.0 29.9 jit_solution(4204137330228900519)
XLA Ops:
  0.6 0.0 copy-start
  0.6 0.0 copy-start.1
  0.7 1.7 %pack_x_edges.1 = (f32[328,128]{1,0:T(8,128)S(1)}, f32[328,128]{1,0:T(8,128)S(1)}, f32[8,128]{1,0:T(8,128)S(1)}, f32[32,128]{1,0:T(8,128)S(1)}) custom-call(f32[6,16,32,128]{3,2,1,0:T(8,128)} %refs_0_.3, f32[16,32,128]{2,1,0:T(8,128)} %refs_1_.5, f32[4,128]{1,0:T(4,128)} %refs_2_.2, s32[4]{0:T(128)} %refs_3_.1, s32[4]{0:T(128)} %bitcast.9), custom_call_target="tpu_custom_call" | custom-call | tf_op jit(solution)/shard_map/pack_x_edges/pallas_call | solution.py:750
  2.4 0.5 %collective-permute-start = (f32[328,128]{1,0:T(8,128)S(1)}, f32[328,128]{1,0:T(8,128)S(1)}, u32[]{:S(2)}, u32[]{:S(2)}) collective-permute-start(f32[328,128]{1,0:T(8,128)S(1)} %get-tuple-element.27), channel_id=1, source_target_pairs={{0,2},{4,6},{8,10},{12,14},{16,18},{20,22},{24,26},{28,30},{2,0},{... | collective-permute-start | bytes 503816 | tf_op jit(solution)/shard_map/ppermute | solution.py:766
  2.9 2.5 %collective-permute-start.1 = (f32[328,128]{1,0:T(8,128)S(1)}, f32[328,128]{1,0:T(8,128)S(1)}, u32[]{:S(2)}, u32[]{:S(2)}) collective-permute-start(f32[328,128]{1,0:T(8,128)S(1)} %get-tuple-element.30), channel_id=1, source_target_pairs={{2,4},{3,5},{6,8},{7,9},{10,12},{11,13},{14,16},{15,17},{18,20},{1... | collective-permute-start | bytes 503816 | tf_op jit(solution)/shard_map/ppermute | solution.py:768
  5.4 0.1 collective-permute-start.3
  5.5 0.0 collective-permute-done.even.refs_3_.refs_2_
  5.5 0.0 copy-done
  5.5 0.0 copy-done.1
  5.5 1.5 %pack_y_edges.1 = (f32[2,7,32,128]{3,2,1,0:T(8,128)S(1)}, f32[136,128]{1,0:T(8,128)S(1)}) custom-call(f32[6,16,32,128]{3,2,1,0:T(8,128)S(1)} %copy-done, f32[16,32,128]{2,1,0:T(8,128)S(1)} %copy-done.1, f32[328,128]{1,0:T(8,128)S(1)} %collective-permute-done.even.refs_3_.refs_2_, f32[8,128]{1,0:T(8,128)S(1)} %get-tuple-element.28.refs_0_.refs_6_), custom_call_target="tpu_custom_call" | custom-call | tf_op jit(solution)/shard_map/pack_y_edges/pallas_call | solution.py:775
  7.0 2.0 %collective-permute-start.2 = (f32[136,128]{1,0:T(8,128)S(1)}, f32[136,128]{1,0:T(8,128)S(1)}, u32[]{:S(2)}, u32[]{:S(2)}) collective-permute-start(f32[136,128]{1,0:T(8,128)S(1)} %get-tuple-element.35), channel_id=1, source_target_pairs={{0,1},{1,0},{2,3},{3,2},{4,5},{5,4},{6,7},{7,6},{8,9},{9,8},{10,11... | collective-permute-start | bytes 208904 | tf_op jit(solution)/shard_map/ppermute | solution.py:783
  9.0 0.0 collective-permute-done.1.refs_4_.refs_3_
  9.0 1.0 %prepare_surface.1 = (f32[2,7,32,128]{3,2,1,0:T(8,128)S(1)}, f32[6,16,5,8,128]{4,3,2,1,0:T(8,128)S(1)}, f32[16,5,8,128]{3,2,1,0:T(8,128)S(1)}, f32[2,7,8,128]{3,...) custom-call(f32[2,7,32,128]{3,2,1,0:T(8,128)S(1)} %get-tuple-element.29.r, ...), custom_call_target="tpu_custom_call", output_to_operand_aliasing={{0}: (0, {})} | custom-call | tf_op jit(solution)/shard_map/prepare_surface/pallas_call | solution.py:795
  10.0 0.0 collective-permute-done.3.refs_5_
  10.0 1.8 %collective-permute-done.2.refs_4_ = f32[136,128]{1,0:T(8,128)S(1)} collective-permute-done((f32[136,128]{1,0:T(8,128)S(1)}, f32[136,128]{1,0:T(8,128)S(1)}, u32[]{:S(2)}, u32[]{:S(2)}) %collective-permute-start.2) | collective-permute-done | bytes 69664 | tf_op jit(solution)/shard_map/ppermute | solution.py:783
  11.8 1.5 %surface_steps.1 = (f32[32,512]{1,0:T(8,128)S(1)}, f32[3,5,8,128]{3,2,1,0:T(8,128)S(1)}, f32[3,5,8,128]{3,2,1,0:T(8,128)S(1)}, f32[3,5,8,128]{3,2,1,0:T(8,128)S(1)}) custom-call(f32[6,16,5,8,128]{4,3,2,1,0:T(8,128)S(1)} %get-tuple-element.31.refs_0_, f32[16,5,8,128]{3,2,1,0:T(8,128)S(1)} %get-tuple-element.32.refs_1_, ...), custom_call_target="tpu_custom_call" | custom-call | tf_op jit(solution)/shard_map/surface_steps/pallas_call | solution.py:824
  13.3 2.8 %collective-permute-start.4 = (f32[32,512]{1,0:T(8,128)S(1)}, f32[32,512]{1,0:T(8,128)S(1)}, u32[]{:S(2)}, u32[]{:S(2)}) collective-permute-start(f32[32,512]{1,0:T(8,128)S(1)} %get-tuple-element.38.refs_0_), channel_id=1, source_target_pairs={{0,4},{2,6},{4,0},{6,2},{8,12},{10,14},{12,8},{14,10},{16,20},{18,... | collective-permute-start | bytes 196616 | tf_op jit(solution)/shard_map/ppermute | solution.py:668
  16.0 0.1 multiply_bitcast_fusion.1
  16.1 0.1 collective-permute-start.5
  16.2 2.1 %early_steps.1 = (f32[6,18,5,8,128]{4,3,2,1,0:T(8,128)S(1)}, f32[16,5,8,128]{3,2,1,0:T(8,128)S(1)}) custom-call(f32[6,16,32,128]{3,2,1,0:T(8,128)S(1)} %copy-done, f32[16,32,128]{2,1,0:T(8,128)S(1)} %copy-done.1, f32[328,128]{1,0:T(8,128)S(1)} %collective-permute-done.even.refs_3_.refs_2_, f32[328,128]{1,0:T(8,128)S(1)} %collective-permute-done.1.refs_4_.refs_3_, ...), custom_call_target="tpu_custom_call" | custom-call | tf_op jit(solution)/shard_map/early_steps/pallas_call | solution.py:846
  18.3 0.1 collective-permute-done.4.refs_2_
  18.4 0.5 %collective-permute-start.6 = (f32[32,512]{1,0:T(8,128)S(1)}, f32[32,512]{1,0:T(8,128)S(1)}, u32[]{:S(2)}, u32[]{:S(2)}) collective-permute-start(f32[32,512]{1,0:T(8,128)S(1)} %collective-permute-done.4.refs_2_), channel_id=1, source_target_pairs={{0,2},{2,0},{4,6},{6,4},{8,10},{10,8},{12,14},{14,12},{16,18},{18,... | collective-permute-start | bytes 196616 | tf_op jit(solution)/shard_map/ppermute | solution.py:668
  18.9 0.0 collective-permute-done.5.refs_1_
  18.9 0.9 %collective-permute-done.6.refs_3_ = f32[32,512]{1,0:T(8,128)S(1)} collective-permute-done((f32[32,512]{1,0:T(8,128)S(1)}, f32[32,512]{1,0:T(8,128)S(1)}, u32[]{:S(2)}, u32[]{:S(2)}) %collective-permute-start.6) | collective-permute-done | bytes 65568 | tf_op jit(solution)/shard_map/ppermute | solution.py:668
  19.8 0.3 partial_spectrum.1
  20.1 4.3 %collective-permute-start.7 = (f32[16,512]{1,0:T(8,128)S(1)}, f32[16,512]{1,0:T(8,128)S(1)}, u32[]{:S(2)}, u32[]{:S(2)}) collective-permute-start(f32[16,512]{1,0:T(8,128)S(1)} %get-tuple-element.49), channel_id=1, source_target_pairs={{0,24},{2,26},{4,28},{6,30},{8,16},{10,18},{12,20},{14,22},{16,8},... | collective-permute-start | bytes 98312 | tf_op jit(solution)/shard_map/ppermute | solution.py:668
  24.4 0.0 collective-permute-start.8
  24.4 0.6 %collective-permute-start.9 = (f32[16,512]{1,0:T(8,128)S(1)}, f32[16,512]{1,0:T(8,128)S(1)}, u32[]{:S(2)}, u32[]{:S(2)}) collective-permute-start(f32[16,512]{1,0:T(8,128)S(1)} %get-tuple-element.51), channel_id=1, source_target_pairs={{0,8},{2,10},{4,12},{6,14},{8,0},{10,2},{12,4},{14,6},{16,24},{18,... | collective-permute-start | bytes 98312 | tf_op jit(solution)/shard_map/ppermute | solution.py:668
  25.0 1.9 %later_steps.1 = f32[6,16,32,128]{3,2,1,0:T(8,128)} custom-call(f32[6,18,5,8,128]{4,3,2,1,0:T(8,128)S(1)} %get-tuple-element.44.refs_0_, f32[16,5,8,128]{3,2,1,0:T(8,128)S(1)} %get-tuple-element.45.refs_1_, f32[3,5,8,128]{3,2,1,0:T(8,128)S(1)} %get-tuple-element.39.refs_4_.refs_2_, f32[3,5,8,128]{3,2,1,0:T(8,128)S(1)} %get-tuple-element.40.refs_5_.refs_3_, ...), custom_call_target="tpu_custom_call" | custom-call | tf_op jit(solution)/shard_map/later_steps/pallas_call | solution.py:860
  26.9 0.0 collective-permute-done.7.refs_1_
  26.9 2.3 %collective-permute-done.8.refs_2_ = f32[16,512]{1,0:T(8,128)S(1)} collective-permute-done((f32[16,512]{1,0:T(8,128)S(1)}, f32[16,512]{1,0:T(8,128)S(1)}, u32[]{:S(2)}, u32[]{:S(2)}) %collective-permute-start.8) | collective-permute-done | bytes 32800 | tf_op jit(solution)/shard_map/ppermute | solution.py:668
  29.2 0.0 collective-permute-done.9.refs_3_
  29.2 0.6 %add_arrived.1 = f32[16,4,128]{2,1,0:T(4,128)} custom-call(f32[16,512]{1,0:T(8,128)S(1)} %get-tuple-element.48.refs_0_, f32[16,512]{1,0:T(8,128)S(1)} %collective-permute-done.7.refs_1_, f32[16,512]{1,0:T(8,128)S(1)} %collective-permute-done.8.refs_2_, f32[16,512]{1,0:T(8,128)S(1)} %collective-permute-done.9.refs_3_), custom_call_target="tpu_custom_call" | custom-call | tf_op jit(solution)/shard_map/add_arrived/pallas_call | solution.py:686
  (3 shorter events, 0.0 us)
Async XLA Ops:
  0.6 4.9 %copy-start = (f32[6,16,32,128]{3,2,1,0:T(8,128)S(1)}, f32[6,16,32,128]{3,2,1,0:T(8,128)}, u32[]{:S(2)}) copy-start(f32[6,16,32,128]{3,2,1,0:T(8,128)} %refs_0_.3) | copy-start | bytes 4718596
  0.6 4.9 %copy-start.1 = (f32[16,32,128]{2,1,0:T(8,128)S(1)}, f32[16,32,128]{2,1,0:T(8,128)}, u32[]{:S(2)}) copy-start(f32[16,32,128]{2,1,0:T(8,128)} %refs_1_.5) | copy-start | bytes 786436
  2.4 3.1 %collective-permute-start = (f32[328,128]{1,0:T(8,128)S(1)}, f32[328,128]{1,0:T(8,128)S(1)}, u32[]{:S(2)}, u32[]{:S(2)}) collective-permute-start(f32[328,128]{1,0:T(8,128)S(1)} %get-tuple-element.27), channel_id=1, source_target_pairs={{0,2},{4,6},{8,10},{12,14},{16,18},{20,22},{24,26},{28,30},{2,0},{... | collective-permute-start | bytes 503816 | tf_op jit(solution)/shard_map/ppermute | solution.py:766
  2.9 6.1 %collective-permute-start.1 = (f32[328,128]{1,0:T(8,128)S(1)}, f32[328,128]{1,0:T(8,128)S(1)}, u32[]{:S(2)}, u32[]{:S(2)}) collective-permute-start(f32[328,128]{1,0:T(8,128)S(1)} %get-tuple-element.30), channel_id=1, source_target_pairs={{2,4},{3,5},{6,8},{7,9},{10,12},{11,13},{14,16},{15,17},{18,20},{1... | collective-permute-start | bytes 503816 | tf_op jit(solution)/shard_map/ppermute | solution.py:768
  5.4 4.6 %collective-permute-start.3 = (f32[32,128]{1,0:T(8,128)S(1)}, f32[32,128]{1,0:T(8,128)S(1)}, u32[]{:S(2)}, u32[]{:S(2)}) collective-permute-start(f32[32,128]{1,0:T(8,128)S(1)} %get-tuple-element.36), channel_id=1, source_target_pairs={{2,5},{3,4},{6,9},{7,8},{10,13},{11,12},{14,17},{15,16},{18,21},{1... | collective-permute-start | bytes 49160 | tf_op jit(solution)/shard_map/ppermute | solution.py:770
  7.0 4.8 %collective-permute-start.2 = (f32[136,128]{1,0:T(8,128)S(1)}, f32[136,128]{1,0:T(8,128)S(1)}, u32[]{:S(2)}, u32[]{:S(2)}) collective-permute-start(f32[136,128]{1,0:T(8,128)S(1)} %get-tuple-element.35), channel_id=1, source_target_pairs={{0,1},{1,0},{2,3},{3,2},{4,5},{5,4},{6,7},{7,6},{8,9},{9,8},{10,11... | collective-permute-start | bytes 208904 | tf_op jit(solution)/shard_map/ppermute | solution.py:783
  13.3 5.1 %collective-permute-start.4 = (f32[32,512]{1,0:T(8,128)S(1)}, f32[32,512]{1,0:T(8,128)S(1)}, u32[]{:S(2)}, u32[]{:S(2)}) collective-permute-start(f32[32,512]{1,0:T(8,128)S(1)} %get-tuple-element.38.refs_0_), channel_id=1, source_target_pairs={{0,4},{2,6},{4,0},{6,2},{8,12},{10,14},{12,8},{14,10},{16,20},{18,... | collective-permute-start | bytes 196616 | tf_op jit(solution)/shard_map/ppermute | solution.py:668
  16.1 2.8 %collective-permute-start.5 = (f32[32,512]{1,0:T(8,128)S(1)}, f32[32,512]{1,0:T(8,128)S(1)}, u32[]{:S(2)}, u32[]{:S(2)}) collective-permute-start(f32[32,512]{1,0:T(8,128)S(1)} %get-tuple-element.38.refs_0_), channel_id=1, source_target_pairs={{0,2},{2,0},{4,6},{6,4},{8,10},{10,8},{12,14},{14,12},{16,18},{18,... | collective-permute-start | bytes 196616 | tf_op jit(solution)/shard_map/ppermute | solution.py:668
  18.4 1.4 %collective-permute-start.6 = (f32[32,512]{1,0:T(8,128)S(1)}, f32[32,512]{1,0:T(8,128)S(1)}, u32[]{:S(2)}, u32[]{:S(2)}) collective-permute-start(f32[32,512]{1,0:T(8,128)S(1)} %collective-permute-done.4.refs_2_), channel_id=1, source_target_pairs={{0,2},{2,0},{4,6},{6,4},{8,10},{10,8},{12,14},{14,12},{16,18},{18,... | collective-permute-start | bytes 196616 | tf_op jit(solution)/shard_map/ppermute | solution.py:668
  20.1 6.9 %collective-permute-start.7 = (f32[16,512]{1,0:T(8,128)S(1)}, f32[16,512]{1,0:T(8,128)S(1)}, u32[]{:S(2)}, u32[]{:S(2)}) collective-permute-start(f32[16,512]{1,0:T(8,128)S(1)} %get-tuple-element.49), channel_id=1, source_target_pairs={{0,24},{2,26},{4,28},{6,30},{8,16},{10,18},{12,20},{14,22},{16,8},... | collective-permute-start | bytes 98312 | tf_op jit(solution)/shard_map/ppermute | solution.py:668
  24.4 4.8 %collective-permute-start.8 = (f32[16,512]{1,0:T(8,128)S(1)}, f32[16,512]{1,0:T(8,128)S(1)}, u32[]{:S(2)}, u32[]{:S(2)}) collective-permute-start(f32[16,512]{1,0:T(8,128)S(1)} %get-tuple-element.50), channel_id=1, source_target_pairs={{0,16},{2,18},{4,20},{6,22},{8,24},{10,26},{12,28},{14,30},{16,0},... | collective-permute-start | bytes 98312 | tf_op jit(solution)/shard_map/ppermute | solution.py:668
  24.4 4.8 %collective-permute-start.9 = (f32[16,512]{1,0:T(8,128)S(1)}, f32[16,512]{1,0:T(8,128)S(1)}, u32[]{:S(2)}, u32[]{:S(2)}) collective-permute-start(f32[16,512]{1,0:T(8,128)S(1)} %get-tuple-element.51), channel_id=1, source_target_pairs={{0,8},{2,10},{4,12},{6,14},{8,0},{10,2},{12,4},{14,6},{16,24},{18,... | collective-permute-start | bytes 98312 | tf_op jit(solution)/shard_map/ppermute | solution.py:668

commit v7 on v6

--- a/solution.py
+++ b/solution.py
@@ -669,8 +669,8 @@
 
     third = across(tile, 2)
     second = across(tile, 1)
-    third, beside = lax.optimization_barrier((third, beside))
-    fourth = across(third, 1)
+    fourth = across(tile, 3)
+    third, fourth, beside = lax.optimization_barrier((third, fourth, beside))
     far = xs_size // NEAR
     rows = weights.shape[0] // far
     parts = pl.pallas_call(

time: 30 us -> 29.5 us (0.983)
  starting transfers between devices: 13.4 us -> 12.5 us
  waiting for transfers between devices: 4.99 us -> 5.4 us
    ppermute x6, starting transfers between devices: 8.28 us -> 7.4 us  [across(): return lax.ppermute(block, 'xs', [(i, i ^ mask) for i in range(xs_size)])]
    ppermute x6, waiting for transfers between devices: 3.23 us -> 3.7 us  [across(): return lax.ppermute(block, 'xs', [(i, i ^ mask) for i in range(xs_size)])]
  transfers between devices with their start and end apart: 10 -> 10, of which waited for: 4 -> 3; matrix products, arithmetic and copies ran while one was open for 0% -> 0% of each run, Pallas kernels for 22% -> 22%
where the time goes in v7:
time: 29.5 us; the launch traced here: 29.4 us
  starting transfers between devices  12.5 us (42%)
  Pallas kernels  10.6 us (36%)
  waiting for transfers between devices  5.4 us (18%)
  between operations  0.74 us (3%)
    ppermute x6, starting transfers between devices, across(): return lax.ppermute(block, 'xs', [(i, i ^ mask) for i in range(xs_size)])  7.4 us
    ppermute x6, waiting for transfers between devices, across(): return lax.ppermute(block, 'xs', [(i, i ^ mask) for i in range(xs_size)])  3.7 us
    ppermute x1, starting transfers between devices, on_device(): from_odd = lax.ppermute(to_odd, both, straight)  2.53 us
    pallas_call x1, Pallas kernels, on_device(): pl.pallas_call(early_steps, out_shape=(shape_of(*state_shape), shape_of(l...  2.11 us
    ppermute x1, starting transfers between devices, on_device(): lax.ppermute(message, 'ys', route)  1.96 us
    pallas_call x1, Pallas kernels, finish(): pl.pallas_call(later_steps, out_shape=shape_of(*fields.shape), in_specs=[...  1.87 us
    pallas_call x1, Pallas kernels, on_device(): pl.pallas_call(functools.partial(pack_x, n_adj=n_adj, n_swaps=len(y_swaps...  1.7 us
    ppermute x1, waiting for transfers between devices, on_device(): lax.ppermute(message, 'ys', route)  1.69 us
  transfers between devices with their start and end apart: 10, of which 3 were waited for; matrix products, arithmetic and copies ran while one was open for 0% of the time, Pallas kernels for 22%

profile of v7, /device:TPU:0, one launch (start us, length us, event | category | flops | bytes accessed | tf_op | source)
XLA Modules:
  0.0 29.4 jit_solution(333078954711009751)
XLA Ops:
  0.6 0.0 copy-start
  0.6 0.0 copy-start.1
  0.7 1.7 %pack_x_edges.1 = (f32[328,128]{1,0:T(8,128)S(1)}, f32[328,128]{1,0:T(8,128)S(1)}, f32[8,128]{1,0:T(8,128)S(1)}, f32[32,128]{1,0:T(8,128)S(1)}) custom-call(f32[6,16,32,128]{3,2,1,0:T(8,128)} %refs_0_.3, f32[16,32,128]{2,1,0:T(8,128)} %refs_1_.5, f32[4,128]{1,0:T(4,128)} %refs_2_.2, s32[4]{0:T(128)} %refs_3_.1, s32[4]{0:T(128)} %bitcast.9), custom_call_target="tpu_custom_call" | custom-call | tf_op jit(solution)/shard_map/pack_x_edges/pallas_call | solution.py:750
  2.4 0.5 %collective-permute-start = (f32[328,128]{1,0:T(8,128)S(1)}, f32[328,128]{1,0:T(8,128)S(1)}, u32[]{:S(2)}, u32[]{:S(2)}) collective-permute-start(f32[328,128]{1,0:T(8,128)S(1)} %get-tuple-element.28), channel_id=1, source_target_pairs={{0,2},{4,6},{8,10},{12,14},{16,18},{20,22},{24,26},{28,30},{2,0},{... | collective-permute-start | bytes 503816 | tf_op jit(solution)/shard_map/ppermute | solution.py:766
  2.9 2.5 %collective-permute-start.1 = (f32[328,128]{1,0:T(8,128)S(1)}, f32[328,128]{1,0:T(8,128)S(1)}, u32[]{:S(2)}, u32[]{:S(2)}) collective-permute-start(f32[328,128]{1,0:T(8,128)S(1)} %get-tuple-element.31), channel_id=1, source_target_pairs={{2,4},{3,5},{6,8},{7,9},{10,12},{11,13},{14,16},{15,17},{18,20},{1... | collective-permute-start | bytes 503816 | tf_op jit(solution)/shard_map/ppermute | solution.py:768
  5.4 0.1 collective-permute-start.3
  5.5 0.0 collective-permute-done.even.refs_3_.refs_2_
  5.5 0.0 copy-done
  5.5 0.0 copy-done.1
  5.5 1.5 %pack_y_edges.1 = (f32[2,7,32,128]{3,2,1,0:T(8,128)S(1)}, f32[136,128]{1,0:T(8,128)S(1)}) custom-call(f32[6,16,32,128]{3,2,1,0:T(8,128)S(1)} %copy-done, f32[16,32,128]{2,1,0:T(8,128)S(1)} %copy-done.1, f32[328,128]{1,0:T(8,128)S(1)} %collective-permute-done.even.refs_3_.refs_2_, f32[8,128]{1,0:T(8,128)S(1)} %get-tuple-element.29.refs_0_.refs_6_), custom_call_target="tpu_custom_call" | custom-call | tf_op jit(solution)/shard_map/pack_y_edges/pallas_call | solution.py:775
  7.1 2.0 %collective-permute-start.2 = (f32[136,128]{1,0:T(8,128)S(1)}, f32[136,128]{1,0:T(8,128)S(1)}, u32[]{:S(2)}, u32[]{:S(2)}) collective-permute-start(f32[136,128]{1,0:T(8,128)S(1)} %get-tuple-element.36), channel_id=1, source_target_pairs={{0,1},{1,0},{2,3},{3,2},{4,5},{5,4},{6,7},{7,6},{8,9},{9,8},{10,11... | collective-permute-start | bytes 208904 | tf_op jit(solution)/shard_map/ppermute | solution.py:783
  9.0 0.0 collective-permute-done.1.refs_4_.refs_3_
  9.0 1.0 %prepare_surface.1 = (f32[2,7,32,128]{3,2,1,0:T(8,128)S(1)}, f32[6,16,5,8,128]{4,3,2,1,0:T(8,128)S(1)}, f32[16,5,8,128]{3,2,1,0:T(8,128)S(1)}, f32[2,7,8,128]{3,...) custom-call(f32[2,7,32,128]{3,2,1,0:T(8,128)S(1)} %get-tuple-element.30.r, ...), custom_call_target="tpu_custom_call", output_to_operand_aliasing={{0}: (0, {})} | custom-call | tf_op jit(solution)/shard_map/prepare_surface/pallas_call | solution.py:795
  10.0 0.1 multiply_bitcast_fusion.1
  10.1 0.0 collective-permute-done.3.refs_5_
  10.1 1.7 %collective-permute-done.2.refs_4_ = f32[136,128]{1,0:T(8,128)S(1)} collective-permute-done((f32[136,128]{1,0:T(8,128)S(1)}, f32[136,128]{1,0:T(8,128)S(1)}, u32[]{:S(2)}, u32[]{:S(2)}) %collective-permute-start.2) | collective-permute-done | bytes 69664 | tf_op jit(solution)/shard_map/ppermute | solution.py:783
  11.8 1.5 %surface_steps.1 = (f32[32,512]{1,0:T(8,128)S(1)}, f32[3,5,8,128]{3,2,1,0:T(8,128)S(1)}, f32[3,5,8,128]{3,2,1,0:T(8,128)S(1)}, f32[3,5,8,128]{3,2,1,0:T(8,128)S(1)}) custom-call(f32[6,16,5,8,128]{4,3,2,1,0:T(8,128)S(1)} %get-tuple-element.32.refs_0_, f32[16,5,8,128]{3,2,1,0:T(8,128)S(1)} %get-tuple-element.33.refs_1_, ...), custom_call_target="tpu_custom_call" | custom-call | tf_op jit(solution)/shard_map/surface_steps/pallas_call | solution.py:824
  13.3 2.8 %collective-permute-start.4 = (f32[32,512]{1,0:T(8,128)S(1)}, f32[32,512]{1,0:T(8,128)S(1)}, u32[]{:S(2)}, u32[]{:S(2)}) collective-permute-start(f32[32,512]{1,0:T(8,128)S(1)} %get-tuple-element.39.refs_0_), channel_id=1, source_target_pairs={{0,4},{2,6},{4,0},{6,2},{8,12},{10,14},{12,8},{14,10},{16,20},{18,... | collective-permute-start | bytes 196616 | tf_op jit(solution)/shard_map/ppermute | solution.py:668
  16.1 0.0 collective-permute-start.5
  16.1 0.2 collective-permute-start.6
  16.3 2.1 %early_steps.1 = (f32[6,18,5,8,128]{4,3,2,1,0:T(8,128)S(1)}, f32[16,5,8,128]{3,2,1,0:T(8,128)S(1)}) custom-call(f32[6,16,32,128]{3,2,1,0:T(8,128)S(1)} %copy-done, f32[16,32,128]{2,1,0:T(8,128)S(1)} %copy-done.1, f32[328,128]{1,0:T(8,128)S(1)} %collective-permute-done.even.refs_3_.refs_2_, f32[328,128]{1,0:T(8,128)S(1)} %collective-permute-done.1.refs_4_.refs_3_, ...), custom_call_target="tpu_custom_call" | custom-call | tf_op jit(solution)/shard_map/early_steps/pallas_call | solution.py:846
  18.4 0.0 collective-permute-done.4.refs_2_
  18.4 2.0 %collective-permute-done.5.refs_3_ = f32[32,512]{1,0:T(8,128)S(1)} collective-permute-done((f32[32,512]{1,0:T(8,128)S(1)}, f32[32,512]{1,0:T(8,128)S(1)}, u32[]{:S(2)}, u32[]{:S(2)}) %collective-permute-start.5) | collective-permute-done | bytes 65568 | tf_op jit(solution)/shard_map/ppermute | solution.py:668
  20.4 0.0 collective-permute-done.6.refs_1_
  20.4 0.3 partial_spectrum.1
  20.7 3.2 %collective-permute-start.7 = (f32[16,512]{1,0:T(8,128)S(1)}, f32[16,512]{1,0:T(8,128)S(1)}, u32[]{:S(2)}, u32[]{:S(2)}) collective-permute-start(f32[16,512]{1,0:T(8,128)S(1)} %get-tuple-element.51), channel_id=1, source_target_pairs={{0,24},{2,26},{4,28},{6,30},{8,16},{10,18},{12,20},{14,22},{16,8},... | collective-permute-start | bytes 98312 | tf_op jit(solution)/shard_map/ppermute | solution.py:668
  23.9 0.0 collective-permute-start.8
  23.9 1.2 %collective-permute-start.9 = (f32[16,512]{1,0:T(8,128)S(1)}, f32[16,512]{1,0:T(8,128)S(1)}, u32[]{:S(2)}, u32[]{:S(2)}) collective-permute-start(f32[16,512]{1,0:T(8,128)S(1)} %get-tuple-element.53), channel_id=1, source_target_pairs={{0,8},{2,10},{4,12},{6,14},{8,0},{10,2},{12,4},{14,6},{16,24},{18,... | collective-permute-start | bytes 98312 | tf_op jit(solution)/shard_map/ppermute | solution.py:668
  25.2 1.9 %later_steps.1 = f32[6,16,32,128]{3,2,1,0:T(8,128)} custom-call(f32[6,18,5,8,128]{4,3,2,1,0:T(8,128)S(1)} %get-tuple-element.45.refs_0_, f32[16,5,8,128]{3,2,1,0:T(8,128)S(1)} %get-tuple-element.46.refs_1_, f32[3,5,8,128]{3,2,1,0:T(8,128)S(1)} %get-tuple-element.40.refs_4_.refs_2_, f32[3,5,8,128]{3,2,1,0:T(8,128)S(1)} %get-tuple-element.41.refs_5_.refs_3_, ...), custom_call_target="tpu_custom_call" | custom-call | tf_op jit(solution)/shard_map/later_steps/pallas_call | solution.py:860
  27.1 0.0 collective-permute-done.7.refs_1_
  27.1 1.7 %collective-permute-done.8.refs_2_ = f32[16,512]{1,0:T(8,128)S(1)} collective-permute-done((f32[16,512]{1,0:T(8,128)S(1)}, f32[16,512]{1,0:T(8,128)S(1)}, u32[]{:S(2)}, u32[]{:S(2)}) %collective-permute-start.8) | collective-permute-done | bytes 32800 | tf_op jit(solution)/shard_map/ppermute | solution.py:668
  28.7 0.0 collective-permute-done.9.refs_3_
  28.7 0.6 %add_arrived.1 = f32[16,4,128]{2,1,0:T(4,128)} custom-call(f32[16,512]{1,0:T(8,128)S(1)} %get-tuple-element.50.refs_0_, f32[16,512]{1,0:T(8,128)S(1)} %collective-permute-done.7.refs_1_, f32[16,512]{1,0:T(8,128)S(1)} %collective-permute-done.8.refs_2_, f32[16,512]{1,0:T(8,128)S(1)} %collective-permute-done.9.refs_3_), custom_call_target="tpu_custom_call" | custom-call | tf_op jit(solution)/shard_map/add_arrived/pallas_call | solution.py:686
  (3 shorter events, 0.0 us)
Async XLA Ops:
  0.6 4.9 %copy-start = (f32[6,16,32,128]{3,2,1,0:T(8,128)S(1)}, f32[6,16,32,128]{3,2,1,0:T(8,128)}, u32[]{:S(2)}) copy-start(f32[6,16,32,128]{3,2,1,0:T(8,128)} %refs_0_.3) | copy-start | bytes 4718596
  0.6 4.9 %copy-start.1 = (f32[16,32,128]{2,1,0:T(8,128)S(1)}, f32[16,32,128]{2,1,0:T(8,128)}, u32[]{:S(2)}) copy-start(f32[16,32,128]{2,1,0:T(8,128)} %refs_1_.5) | copy-start | bytes 786436
  2.4 3.1 %collective-permute-start = (f32[328,128]{1,0:T(8,128)S(1)}, f32[328,128]{1,0:T(8,128)S(1)}, u32[]{:S(2)}, u32[]{:S(2)}) collective-permute-start(f32[328,128]{1,0:T(8,128)S(1)} %get-tuple-element.28), channel_id=1, source_target_pairs={{0,2},{4,6},{8,10},{12,14},{16,18},{20,22},{24,26},{28,30},{2,0},{... | collective-permute-start | bytes 503816 | tf_op jit(solution)/shard_map/ppermute | solution.py:766
  2.9 6.1 %collective-permute-start.1 = (f32[328,128]{1,0:T(8,128)S(1)}, f32[328,128]{1,0:T(8,128)S(1)}, u32[]{:S(2)}, u32[]{:S(2)}) collective-permute-start(f32[328,128]{1,0:T(8,128)S(1)} %get-tuple-element.31), channel_id=1, source_target_pairs={{2,4},{3,5},{6,8},{7,9},{10,12},{11,13},{14,16},{15,17},{18,20},{1... | collective-permute-start | bytes 503816 | tf_op jit(solution)/shard_map/ppermute | solution.py:768
  5.4 4.7 %collective-permute-start.3 = (f32[32,128]{1,0:T(8,128)S(1)}, f32[32,128]{1,0:T(8,128)S(1)}, u32[]{:S(2)}, u32[]{:S(2)}) collective-permute-start(f32[32,128]{1,0:T(8,128)S(1)} %get-tuple-element.37), channel_id=1, source_target_pairs={{2,5},{3,4},{6,9},{7,8},{10,13},{11,12},{14,17},{15,16},{18,21},{1... | collective-permute-start | bytes 49160 | tf_op jit(solution)/shard_map/ppermute | solution.py:770
  7.1 4.8 %collective-permute-start.2 = (f32[136,128]{1,0:T(8,128)S(1)}, f32[136,128]{1,0:T(8,128)S(1)}, u32[]{:S(2)}, u32[]{:S(2)}) collective-permute-start(f32[136,128]{1,0:T(8,128)S(1)} %get-tuple-element.36), channel_id=1, source_target_pairs={{0,1},{1,0},{2,3},{3,2},{4,5},{5,4},{6,7},{7,6},{8,9},{9,8},{10,11... | collective-permute-start | bytes 208904 | tf_op jit(solution)/shard_map/ppermute | solution.py:783
  13.3 5.1 %collective-permute-start.4 = (f32[32,512]{1,0:T(8,128)S(1)}, f32[32,512]{1,0:T(8,128)S(1)}, u32[]{:S(2)}, u32[]{:S(2)}) collective-permute-start(f32[32,512]{1,0:T(8,128)S(1)} %get-tuple-element.39.refs_0_), channel_id=1, source_target_pairs={{0,4},{2,6},{4,0},{6,2},{8,12},{10,14},{12,8},{14,10},{16,20},{18,... | collective-permute-start | bytes 196616 | tf_op jit(solution)/shard_map/ppermute | solution.py:668
  16.1 4.4 %collective-permute-start.5 = (f32[32,512]{1,0:T(8,128)S(1)}, f32[32,512]{1,0:T(8,128)S(1)}, u32[]{:S(2)}, u32[]{:S(2)}) collective-permute-start(f32[32,512]{1,0:T(8,128)S(1)} %get-tuple-element.39.refs_0_), channel_id=1, source_target_pairs={{0,6},{2,4},{4,2},{6,0},{8,14},{10,12},{12,10},{14,8},{16,22},{18,... | collective-permute-start | bytes 196616 | tf_op jit(solution)/shard_map/ppermute | solution.py:668
  16.1 4.4 %collective-permute-start.6 = (f32[32,512]{1,0:T(8,128)S(1)}, f32[32,512]{1,0:T(8,128)S(1)}, u32[]{:S(2)}, u32[]{:S(2)}) collective-permute-start(f32[32,512]{1,0:T(8,128)S(1)} %get-tuple-element.39.refs_0_), channel_id=1, source_target_pairs={{0,2},{2,0},{4,6},{6,4},{8,10},{10,8},{12,14},{14,12},{16,18},{18,... | collective-permute-start | bytes 196616 | tf_op jit(solution)/shard_map/ppermute | solution.py:668
  20.7 6.3 %collective-permute-start.7 = (f32[16,512]{1,0:T(8,128)S(1)}, f32[16,512]{1,0:T(8,128)S(1)}, u32[]{:S(2)}, u32[]{:S(2)}) collective-permute-start(f32[16,512]{1,0:T(8,128)S(1)} %get-tuple-element.51), channel_id=1, source_target_pairs={{0,24},{2,26},{4,28},{6,30},{8,16},{10,18},{12,20},{14,22},{16,8},... | collective-permute-start | bytes 98312 | tf_op jit(solution)/shard_map/ppermute | solution.py:668
  23.9 4.8 %collective-permute-start.8 = (f32[16,512]{1,0:T(8,128)S(1)}, f32[16,512]{1,0:T(8,128)S(1)}, u32[]{:S(2)}, u32[]{:S(2)}) collective-permute-start(f32[16,512]{1,0:T(8,128)S(1)} %get-tuple-element.52), channel_id=1, source_target_pairs={{0,16},{2,18},{4,20},{6,22},{8,24},{10,26},{12,28},{14,30},{16,0},... | collective-permute-start | bytes 98312 | tf_op jit(solution)/shard_map/ppermute | solution.py:668
  23.9 4.8 %collective-permute-start.9 = (f32[16,512]{1,0:T(8,128)S(1)}, f32[16,512]{1,0:T(8,128)S(1)}, u32[]{:S(2)}, u32[]{:S(2)}) collective-permute-start(f32[16,512]{1,0:T(8,128)S(1)} %get-tuple-element.53), channel_id=1, source_target_pairs={{0,8},{2,10},{4,12},{6,14},{8,0},{10,2},{12,4},{14,6},{16,24},{18,... | collective-permute-start | bytes 98312 | tf_op jit(solution)/shard_map/ppermute | solution.py:668

commit v8 on v7

--- a/solution.py
+++ b/solution.py
@@ -681,7 +681,8 @@
         compiler_params=PARAMS,
         name="partial_spectrum",
     )(weights, tile, second, third, fourth)
-    arrived = [across(parts[k], k * NEAR) for k in range(far - 1, 0, -1)]
+    order = [far // 2] + [k for k in range(far - 1, 0, -1) if k != far // 2]
+    arrived = [across(parts[k], k * NEAR) for k in order]
     finished = finish(beside)
     far_field = pl.pallas_call(
         add_parts,

time: 29.5 us -> 29.8 us (1.010)
  waiting for transfers between devices: 5.4 us -> 6.2 us
  starting transfers between devices: 12.5 us -> 12 us
    ppermute x6, waiting for transfers between devices: 3.7 us -> 4.5 us  [across(): return lax.ppermute(block, 'xs', [(i, i ^ mask) for i in range(xs_size)])]
    ppermute x6, starting transfers between devices: 7.4 us -> 6.9 us  [across(): return lax.ppermute(block, 'xs', [(i, i ^ mask) for i in range(xs_size)])]
where the time goes in v8:
time: 29.8 us; the launch traced here: 29.7 us
  starting transfers between devices  12 us (40%)
  Pallas kernels  10.6 us (36%)
  waiting for transfers between devices  6.2 us (21%)
  between operations  0.74 us (2%)
    ppermute x6, starting transfers between devices, across(): return lax.ppermute(block, 'xs', [(i, i ^ mask) for i in range(xs_size)])  6.9 us
    ppermute x6, waiting for transfers between devices, across(): return lax.ppermute(block, 'xs', [(i, i ^ mask) for i in range(xs_size)])  4.5 us
    ppermute x1, starting transfers between devices, on_device(): from_odd = lax.ppermute(to_odd, both, straight)  2.53 us
    pallas_call x1, Pallas kernels, on_device(): pl.pallas_call(early_steps, out_shape=(shape_of(*state_shape), shape_of(l...  2.11 us
    ppermute x1, starting transfers between devices, on_device(): lax.ppermute(message, 'ys', route)  1.96 us
    pallas_call x1, Pallas kernels, finish(): pl.pallas_call(later_steps, out_shape=shape_of(*fields.shape), in_specs=[...  1.87 us
    pallas_call x1, Pallas kernels, on_device(): pl.pallas_call(functools.partial(pack_x, n_adj=n_adj, n_swaps=len(y_swaps...  1.7 us
    ppermute x1, waiting for transfers between devices, on_device(): lax.ppermute(message, 'ys', route)  1.69 us
  transfers between devices with their start and end apart: 10, of which 3 were waited for; matrix products, arithmetic and copies ran while one was open for 0% of the time, Pallas kernels for 22%

profile of v8, /device:TPU:0, one launch (start us, length us, event | category | flops | bytes accessed | tf_op | source)
XLA Modules:
  0.0 29.7 jit_solution(6714926608727341477)
XLA Ops:
  0.6 0.0 copy-start
  0.6 0.0 copy-start.1
  0.7 1.7 %pack_x_edges.1 = (f32[328,128]{1,0:T(8,128)S(1)}, f32[328,128]{1,0:T(8,128)S(1)}, f32[8,128]{1,0:T(8,128)S(1)}, f32[32,128]{1,0:T(8,128)S(1)}) custom-call(f32[6,16,32,128]{3,2,1,0:T(8,128)} %refs_0_.3, f32[16,32,128]{2,1,0:T(8,128)} %refs_1_.5, f32[4,128]{1,0:T(4,128)} %refs_2_.2, s32[4]{0:T(128)} %refs_3_.1, s32[4]{0:T(128)} %bitcast.9), custom_call_target="tpu_custom_call" | custom-call | tf_op jit(solution)/shard_map/pack_x_edges/pallas_call | solution.py:751
  2.4 0.5 %collective-permute-start = (f32[328,128]{1,0:T(8,128)S(1)}, f32[328,128]{1,0:T(8,128)S(1)}, u32[]{:S(2)}, u32[]{:S(2)}) collective-permute-start(f32[328,128]{1,0:T(8,128)S(1)} %get-tuple-element.28), channel_id=1, source_target_pairs={{0,2},{4,6},{8,10},{12,14},{16,18},{20,22},{24,26},{28,30},{2,0},{... | collective-permute-start | bytes 503816 | tf_op jit(solution)/shard_map/ppermute | solution.py:767
  2.9 2.5 %collective-permute-start.1 = (f32[328,128]{1,0:T(8,128)S(1)}, f32[328,128]{1,0:T(8,128)S(1)}, u32[]{:S(2)}, u32[]{:S(2)}) collective-permute-start(f32[328,128]{1,0:T(8,128)S(1)} %get-tuple-element.31), channel_id=1, source_target_pairs={{2,4},{3,5},{6,8},{7,9},{10,12},{11,13},{14,16},{15,17},{18,20},{1... | collective-permute-start | bytes 503816 | tf_op jit(solution)/shard_map/ppermute | solution.py:769
  5.4 0.1 collective-permute-start.3
  5.5 0.0 collective-permute-done.even.refs_3_.refs_2_
  5.5 0.0 copy-done
  5.5 0.0 copy-done.1
  5.5 1.5 %pack_y_edges.1 = (f32[2,7,32,128]{3,2,1,0:T(8,128)S(1)}, f32[136,128]{1,0:T(8,128)S(1)}) custom-call(f32[6,16,32,128]{3,2,1,0:T(8,128)S(1)} %copy-done, f32[16,32,128]{2,1,0:T(8,128)S(1)} %copy-done.1, f32[328,128]{1,0:T(8,128)S(1)} %collective-permute-done.even.refs_3_.refs_2_, f32[8,128]{1,0:T(8,128)S(1)} %get-tuple-element.29.refs_0_.refs_6_), custom_call_target="tpu_custom_call" | custom-call | tf_op jit(solution)/shard_map/pack_y_edges/pallas_call | solution.py:776
  7.1 2.0 %collective-permute-start.2 = (f32[136,128]{1,0:T(8,128)S(1)}, f32[136,128]{1,0:T(8,128)S(1)}, u32[]{:S(2)}, u32[]{:S(2)}) collective-permute-start(f32[136,128]{1,0:T(8,128)S(1)} %get-tuple-element.36), channel_id=1, source_target_pairs={{0,1},{1,0},{2,3},{3,2},{4,5},{5,4},{6,7},{7,6},{8,9},{9,8},{10,11... | collective-permute-start | bytes 208904 | tf_op jit(solution)/shard_map/ppermute | solution.py:784
  9.0 0.0 collective-permute-done.1.refs_4_.refs_3_
  9.0 1.0 %prepare_surface.1 = (f32[2,7,32,128]{3,2,1,0:T(8,128)S(1)}, f32[6,16,5,8,128]{4,3,2,1,0:T(8,128)S(1)}, f32[16,5,8,128]{3,2,1,0:T(8,128)S(1)}, f32[2,7,8,128]{3,...) custom-call(f32[2,7,32,128]{3,2,1,0:T(8,128)S(1)} %get-tuple-element.30.r, ...), custom_call_target="tpu_custom_call", output_to_operand_aliasing={{0}: (0, {})} | custom-call | tf_op jit(solution)/shard_map/prepare_surface/pallas_call | solution.py:796
  10.0 0.1 multiply_bitcast_fusion.1
  10.1 0.0 collective-permute-done.3.refs_5_
  10.1 1.7 %collective-permute-done.2.refs_4_ = f32[136,128]{1,0:T(8,128)S(1)} collective-permute-done((f32[136,128]{1,0:T(8,128)S(1)}, f32[136,128]{1,0:T(8,128)S(1)}, u32[]{:S(2)}, u32[]{:S(2)}) %collective-permute-start.2) | collective-permute-done | bytes 69664 | tf_op jit(solution)/shard_map/ppermute | solution.py:784
  11.8 1.5 %surface_steps.1 = (f32[32,512]{1,0:T(8,128)S(1)}, f32[3,5,8,128]{3,2,1,0:T(8,128)S(1)}, f32[3,5,8,128]{3,2,1,0:T(8,128)S(1)}, f32[3,5,8,128]{3,2,1,0:T(8,128)S(1)}) custom-call(f32[6,16,5,8,128]{4,3,2,1,0:T(8,128)S(1)} %get-tuple-element.32.refs_0_, f32[16,5,8,128]{3,2,1,0:T(8,128)S(1)} %get-tuple-element.33.refs_1_, ...), custom_call_target="tpu_custom_call" | custom-call | tf_op jit(solution)/shard_map/surface_steps/pallas_call | solution.py:825
  13.3 2.8 %collective-permute-start.4 = (f32[32,512]{1,0:T(8,128)S(1)}, f32[32,512]{1,0:T(8,128)S(1)}, u32[]{:S(2)}, u32[]{:S(2)}) collective-permute-start(f32[32,512]{1,0:T(8,128)S(1)} %get-tuple-element.39.refs_0_), channel_id=1, source_target_pairs={{0,4},{2,6},{4,0},{6,2},{8,12},{10,14},{12,8},{14,10},{16,20},{18,... | collective-permute-start | bytes 196616 | tf_op jit(solution)/shard_map/ppermute | solution.py:668
  16.1 0.0 collective-permute-start.5
  16.1 0.2 collective-permute-start.6
  16.3 2.1 %early_steps.1 = (f32[6,18,5,8,128]{4,3,2,1,0:T(8,128)S(1)}, f32[16,5,8,128]{3,2,1,0:T(8,128)S(1)}) custom-call(f32[6,16,32,128]{3,2,1,0:T(8,128)S(1)} %copy-done, f32[16,32,128]{2,1,0:T(8,128)S(1)} %copy-done.1, f32[328,128]{1,0:T(8,128)S(1)} %collective-permute-done.even.refs_3_.refs_2_, f32[328,128]{1,0:T(8,128)S(1)} %collective-permute-done.1.refs_4_.refs_3_, ...), custom_call_target="tpu_custom_call" | custom-call | tf_op jit(solution)/shard_map/early_steps/pallas_call | solution.py:847
  18.4 0.0 collective-permute-done.4.refs_2_
  18.4 2.0 %collective-permute-done.5.refs_3_ = f32[32,512]{1,0:T(8,128)S(1)} collective-permute-done((f32[32,512]{1,0:T(8,128)S(1)}, f32[32,512]{1,0:T(8,128)S(1)}, u32[]{:S(2)}, u32[]{:S(2)}) %collective-permute-start.5) | collective-permute-done | bytes 65568 | tf_op jit(solution)/shard_map/ppermute | solution.py:668
  20.4 0.0 collective-permute-done.6.refs_1_
  20.4 0.3 partial_spectrum.1
  20.7 2.6 %collective-permute-start.7 = (f32[16,512]{1,0:T(8,128)S(1)}, f32[16,512]{1,0:T(8,128)S(1)}, u32[]{:S(2)}, u32[]{:S(2)}) collective-permute-start(f32[16,512]{1,0:T(8,128)S(1)} %get-tuple-element.51), channel_id=1, source_target_pairs={{0,16},{2,18},{4,20},{6,22},{8,24},{10,26},{12,28},{14,30},{16,0},... | collective-permute-start | bytes 98312 | tf_op jit(solution)/shard_map/ppermute | solution.py:668
  23.3 1.3 %collective-permute-start.8 = (f32[16,512]{1,0:T(8,128)S(1)}, f32[16,512]{1,0:T(8,128)S(1)}, u32[]{:S(2)}, u32[]{:S(2)}) collective-permute-start(f32[16,512]{1,0:T(8,128)S(1)} %get-tuple-element.52), channel_id=1, source_target_pairs={{0,24},{2,26},{4,28},{6,30},{8,16},{10,18},{12,20},{14,22},{16,8},... | collective-permute-start | bytes 98312 | tf_op jit(solution)/shard_map/ppermute | solution.py:668
  24.7 0.0 collective-permute-start.9
  24.7 1.9 %later_steps.1 = f32[6,16,32,128]{3,2,1,0:T(8,128)} custom-call(f32[6,18,5,8,128]{4,3,2,1,0:T(8,128)S(1)} %get-tuple-element.45.refs_0_, f32[16,5,8,128]{3,2,1,0:T(8,128)S(1)} %get-tuple-element.46.refs_1_, f32[3,5,8,128]{3,2,1,0:T(8,128)S(1)} %get-tuple-element.40.refs_4_.refs_2_, f32[3,5,8,128]{3,2,1,0:T(8,128)S(1)} %get-tuple-element.41.refs_5_.refs_3_, ...), custom_call_target="tpu_custom_call" | custom-call | tf_op jit(solution)/shard_map/later_steps/pallas_call | solution.py:861
  26.5 0.0 collective-permute-done.7.refs_1_
  26.6 2.5 %collective-permute-done.8.refs_2_ = f32[16,512]{1,0:T(8,128)S(1)} collective-permute-done((f32[16,512]{1,0:T(8,128)S(1)}, f32[16,512]{1,0:T(8,128)S(1)}, u32[]{:S(2)}, u32[]{:S(2)}) %collective-permute-start.8) | collective-permute-done | bytes 32800 | tf_op jit(solution)/shard_map/ppermute | solution.py:668
  29.0 0.0 collective-permute-done.9.refs_3_
  29.0 0.6 %add_arrived.1 = f32[16,4,128]{2,1,0:T(4,128)} custom-call(f32[16,512]{1,0:T(8,128)S(1)} %get-tuple-element.50.refs_0_, f32[16,512]{1,0:T(8,128)S(1)} %collective-permute-done.7.refs_1_, f32[16,512]{1,0:T(8,128)S(1)} %collective-permute-done.8.refs_2_, f32[16,512]{1,0:T(8,128)S(1)} %collective-permute-done.9.refs_3_), custom_call_target="tpu_custom_call" | custom-call | tf_op jit(solution)/shard_map/add_arrived/pallas_call | solution.py:687
  (3 shorter events, 0.0 us)
Async XLA Ops:
  0.6 4.9 %copy-start = (f32[6,16,32,128]{3,2,1,0:T(8,128)S(1)}, f32[6,16,32,128]{3,2,1,0:T(8,128)}, u32[]{:S(2)}) copy-start(f32[6,16,32,128]{3,2,1,0:T(8,128)} %refs_0_.3) | copy-start | bytes 4718596
  0.6 4.9 %copy-start.1 = (f32[16,32,128]{2,1,0:T(8,128)S(1)}, f32[16,32,128]{2,1,0:T(8,128)}, u32[]{:S(2)}) copy-start(f32[16,32,128]{2,1,0:T(8,128)} %refs_1_.5) | copy-start | bytes 786436
  2.4 3.1 %collective-permute-start = (f32[328,128]{1,0:T(8,128)S(1)}, f32[328,128]{1,0:T(8,128)S(1)}, u32[]{:S(2)}, u32[]{:S(2)}) collective-permute-start(f32[328,128]{1,0:T(8,128)S(1)} %get-tuple-element.28), channel_id=1, source_target_pairs={{0,2},{4,6},{8,10},{12,14},{16,18},{20,22},{24,26},{28,30},{2,0},{... | collective-permute-start | bytes 503816 | tf_op jit(solution)/shard_map/ppermute | solution.py:767
  2.9 6.1 %collective-permute-start.1 = (f32[328,128]{1,0:T(8,128)S(1)}, f32[328,128]{1,0:T(8,128)S(1)}, u32[]{:S(2)}, u32[]{:S(2)}) collective-permute-start(f32[328,128]{1,0:T(8,128)S(1)} %get-tuple-element.31), channel_id=1, source_target_pairs={{2,4},{3,5},{6,8},{7,9},{10,12},{11,13},{14,16},{15,17},{18,20},{1... | collective-permute-start | bytes 503816 | tf_op jit(solution)/shard_map/ppermute | solution.py:769
  5.4 4.7 %collective-permute-start.3 = (f32[32,128]{1,0:T(8,128)S(1)}, f32[32,128]{1,0:T(8,128)S(1)}, u32[]{:S(2)}, u32[]{:S(2)}) collective-permute-start(f32[32,128]{1,0:T(8,128)S(1)} %get-tuple-element.37), channel_id=1, source_target_pairs={{2,5},{3,4},{6,9},{7,8},{10,13},{11,12},{14,17},{15,16},{18,21},{1... | collective-permute-start | bytes 49160 | tf_op jit(solution)/shard_map/ppermute | solution.py:771
  7.1 4.8 %collective-permute-start.2 = (f32[136,128]{1,0:T(8,128)S(1)}, f32[136,128]{1,0:T(8,128)S(1)}, u32[]{:S(2)}, u32[]{:S(2)}) collective-permute-start(f32[136,128]{1,0:T(8,128)S(1)} %get-tuple-element.36), channel_id=1, source_target_pairs={{0,1},{1,0},{2,3},{3,2},{4,5},{5,4},{6,7},{7,6},{8,9},{9,8},{10,11... | collective-permute-start | bytes 208904 | tf_op jit(solution)/shard_map/ppermute | solution.py:784
  13.3 5.1 %collective-permute-start.4 = (f32[32,512]{1,0:T(8,128)S(1)}, f32[32,512]{1,0:T(8,128)S(1)}, u32[]{:S(2)}, u32[]{:S(2)}) collective-permute-start(f32[32,512]{1,0:T(8,128)S(1)} %get-tuple-element.39.refs_0_), channel_id=1, source_target_pairs={{0,4},{2,6},{4,0},{6,2},{8,12},{10,14},{12,8},{14,10},{16,20},{18,... | collective-permute-start | bytes 196616 | tf_op jit(solution)/shard_map/ppermute | solution.py:668
  16.1 4.4 %collective-permute-start.5 = (f32[32,512]{1,0:T(8,128)S(1)}, f32[32,512]{1,0:T(8,128)S(1)}, u32[]{:S(2)}, u32[]{:S(2)}) collective-permute-start(f32[32,512]{1,0:T(8,128)S(1)} %get-tuple-element.39.refs_0_), channel_id=1, source_target_pairs={{0,6},{2,4},{4,2},{6,0},{8,14},{10,12},{12,10},{14,8},{16,22},{18,... | collective-permute-start | bytes 196616 | tf_op jit(solution)/shard_map/ppermute | solution.py:668
  16.1 4.4 %collective-permute-start.6 = (f32[32,512]{1,0:T(8,128)S(1)}, f32[32,512]{1,0:T(8,128)S(1)}, u32[]{:S(2)}, u32[]{:S(2)}) collective-permute-start(f32[32,512]{1,0:T(8,128)S(1)} %get-tuple-element.39.refs_0_), channel_id=1, source_target_pairs={{0,2},{2,0},{4,6},{6,4},{8,10},{10,8},{12,14},{14,12},{16,18},{18,... | collective-permute-start | bytes 196616 | tf_op jit(solution)/shard_map/ppermute | solution.py:668
  20.7 5.8 %collective-permute-start.7 = (f32[16,512]{1,0:T(8,128)S(1)}, f32[16,512]{1,0:T(8,128)S(1)}, u32[]{:S(2)}, u32[]{:S(2)}) collective-permute-start(f32[16,512]{1,0:T(8,128)S(1)} %get-tuple-element.51), channel_id=1, source_target_pairs={{0,16},{2,18},{4,20},{6,22},{8,24},{10,26},{12,28},{14,30},{16,0},... | collective-permute-start | bytes 98312 | tf_op jit(solution)/shard_map/ppermute | solution.py:668
  23.3 5.7 %collective-permute-start.8 = (f32[16,512]{1,0:T(8,128)S(1)}, f32[16,512]{1,0:T(8,128)S(1)}, u32[]{:S(2)}, u32[]{:S(2)}) collective-permute-start(f32[16,512]{1,0:T(8,128)S(1)} %get-tuple-element.52), channel_id=1, source_target_pairs={{0,24},{2,26},{4,28},{6,30},{8,16},{10,18},{12,20},{14,22},{16,8},... | collective-permute-start | bytes 98312 | tf_op jit(solution)/shard_map/ppermute | solution.py:668
  24.7 4.4 %collective-permute-start.9 = (f32[16,512]{1,0:T(8,128)S(1)}, f32[16,512]{1,0:T(8,128)S(1)}, u32[]{:S(2)}, u32[]{:S(2)}) collective-permute-start(f32[16,512]{1,0:T(8,128)S(1)} %get-tuple-element.53), channel_id=1, source_target_pairs={{0,8},{2,10},{4,12},{6,14},{8,0},{10,2},{12,4},{14,6},{16,24},{18,... | collective-permute-start | bytes 98312 | tf_op jit(solution)/shard_map/ppermute | solution.py:668
